TPU v7x, 32 devices: a whole 2x2x4 slice. The times are simulated.
32 devices in a mesh: dp: 4 (over y, x), fsdp: 8 (over z, core).
Axes of the slice: x: 2, y: 2, z: 4, core: 2. Of those that a mesh axis runs over, the one named last changes fastest.
Arguments:
- inputs: bfloat16 [32, 512, 512], P(('dp', 'fsdp')), may hold values from -5 to 5
- segments: int32 [32, 512], P(('dp', 'fsdp')), may hold values from 0 to 7, never falling along the last dimension, each value on 1 to 256 neighbouring positions
- buckets: int32 [1023], replicated, may hold values from 0 to 31
- cotangent: bfloat16 [32, 512, 512], P(('dp', 'fsdp')), may hold values from -12 to 12
- ffn_norm: bfloat16 [2, 2, 512], P(None, None, ('dp', 'fsdp')), may hold values from -0.59765625 to 0.59765625
- ffn_in: bfloat16 [2, 512, 2048], P(None, ('dp', 'fsdp')), may hold values from -0.25 to 0.25
- ffn_in_bias: bfloat16 [2, 2048], P(None, ('dp', 'fsdp')), may hold values from -2.5 to 2.5
- ffn_out: bfloat16 [2, 2048, 512], P(None, ('dp', 'fsdp')), may hold values from -0.125 to 0.125
- ffn_out_bias: bfloat16 [2, 512], P(None, ('dp', 'fsdp')), may hold values from -2.5 to 2.5
- attn_norm: bfloat16 [2, 512], P(None, ('dp', 'fsdp')), may hold values from -0.59765625 to 0.59765625
- qkv_weight: bfloat16 [512, 1536], P(('dp', 'fsdp')), may hold values from -0.25 to 0.25
- attn_out: bfloat16 [512, 512], P(('dp', 'fsdp')), may hold values from -2 to 2
- attn_out_bias: bfloat16 [512], P(('dp', 'fsdp')), may hold values from -2.5 to 2.5
- rel_table: bfloat16 [256], P(('dp', 'fsdp')), may hold values from -3 to 3
- conv_norm: bfloat16 [2, 512], P(None, ('dp', 'fsdp')), may hold values from -0.59765625 to 0.59765625
- glu_weight: bfloat16 [512, 1024], P(('dp', 'fsdp')), may hold values from -0.25 to 0.25
- glu_bias: bfloat16 [1024], P(('dp', 'fsdp')), may hold values from -2.5 to 2.5
- depth_kernel: bfloat16 [32, 512], P(None, ('dp', 'fsdp')), may hold values from -1 to 1
- batch_norm: bfloat16 [2, 512], P(None, ('dp', 'fsdp')), may hold values from -0.59765625 to 0.59765625
- conv_out: bfloat16 [512, 512], P(('dp', 'fsdp')), may hold values from -0.25 to 0.25
- conv_out_bias: bfloat16 [512], P(('dp', 'fsdp')), may hold values from -2.5 to 2.5
- final_norm: bfloat16 [2, 512], P(None, ('dp', 'fsdp')), may hold values from -0.59765625 to 0.59765625
Outputs:
- output: bfloat16 [32, 512, 512], P(('dp', 'fsdp'))
- grad_inputs: float32 [32, 512, 512], P(('dp', 'fsdp'))
- grad_ffn_norm: float32 [2, 2, 512], P(None, None, ('dp', 'fsdp'))
- grad_ffn_in: float32 [2, 512, 2048], P(None, ('dp', 'fsdp'))
- grad_ffn_in_bias: float32 [2, 2048], P(None, ('dp', 'fsdp'))
- grad_ffn_out: float32 [2, 2048, 512], P(None, ('dp', 'fsdp'))
- grad_ffn_out_bias: float32 [2, 512], P(None, ('dp', 'fsdp'))
- grad_attn_norm: float32 [2, 512], P(None, ('dp', 'fsdp'))
- grad_qkv_weight: float32 [512, 1536], P(('dp', 'fsdp'))
- grad_attn_out: float32 [512, 512], P(('dp', 'fsdp'))
- grad_attn_out_bias: float32 [512], P(('dp', 'fsdp'))
- grad_rel_table: float32 [256], P(('dp', 'fsdp'))
- grad_conv_norm: float32 [2, 512], P(None, ('dp', 'fsdp'))
- grad_glu_weight: float32 [512, 1024], P(('dp', 'fsdp'))
- grad_glu_bias: float32 [1024], P(('dp', 'fsdp'))
- grad_depth_kernel: float32 [32, 512], P(None, ('dp', 'fsdp'))
- grad_batch_norm: float32 [2, 512], P(None, ('dp', 'fsdp'))
- grad_conv_out: float32 [512, 512], P(('dp', 'fsdp'))
- grad_conv_out_bias: float32 [512], P(('dp', 'fsdp'))
- grad_final_norm: float32 [2, 512], P(None, ('dp', 'fsdp'))
Inputs may be any that keep to these rules, and one draw needn't show every extreme that they name: `segments`: segment numbers never fall along a row; each utterance holds 1 to 256 frames.
All inputs are finite; a program needn't handle non-finite values.
Results may differ from a plain program's by a relative error of at most 0.02.
Values may be sent and summed in bfloat16 or wider, within the bound.
A program may use at most 192 MiB of HBM per device.

v0:
```python
import jax
import jax.numpy as jnp
from jax import lax
from jax.sharding import PartitionSpec as P

D = 512
HEADS = 8
HEAD_DIM = 64
BUCKETS = 32


epsilon = 1e-05
highest = lax.Precision.HIGHEST


def layer_norm(values, params):
    center = values - jnp.mean(values, axis=-1, keepdims=True)
    spread = jnp.mean(center * center, axis=-1, keepdims=True)
    return center * lax.rsqrt(spread + epsilon) * (1.0 + params[0]) + params[1]


def silu_slope(values):
    sigma = jax.nn.sigmoid(values)
    return sigma * (1.0 + values * (1.0 - sigma))


def product(left, right):
    return jnp.dot(left, right, preferred_element_type=jnp.float32)


def product_left(left, right):
    return lax.dot_general(
        left, right, (((0,), (0,)), ((), ())), preferred_element_type=jnp.float32
    )


def product_right(left, right):
    return lax.dot_general(
        left, right, (((1,), (1,)), ((), ())), preferred_element_type=jnp.float32
    )


def fetch_feed(norms, inner_weight, inner_bias, outer_weight, outer_bias, layer):
    return (
        lax.all_gather(norms[layer], ("dp", "fsdp"), axis=1, tiled=True),
        lax.all_gather(inner_weight[layer], ("dp", "fsdp"), axis=0, tiled=True),
        lax.all_gather(inner_bias[layer], ("dp", "fsdp"), axis=0, tiled=True),
        lax.all_gather(outer_weight[layer], ("dp", "fsdp"), axis=0, tiled=True),
        lax.all_gather(outer_bias[layer], ("dp", "fsdp"), axis=0, tiled=True),
    )


def reduce_feed(grads):
    return (
        lax.psum_scatter(grads[0], ("dp", "fsdp"), scatter_dimension=1, tiled=True),
        lax.psum_scatter(grads[1], ("dp", "fsdp"), scatter_dimension=0, tiled=True),
        lax.psum_scatter(grads[2], ("dp", "fsdp"), scatter_dimension=0, tiled=True),
        lax.psum_scatter(grads[3], ("dp", "fsdp"), scatter_dimension=0, tiled=True),
        lax.psum_scatter(grads[4], ("dp", "fsdp"), scatter_dimension=0, tiled=True),
    )


def fetch_attention(attn_norm, qkv_weight, attn_out, attn_out_bias, rel_table):
    return (
        lax.all_gather(attn_norm, ("dp", "fsdp"), axis=1, tiled=True),
        lax.all_gather(qkv_weight, ("dp", "fsdp"), axis=0, tiled=True),
        lax.all_gather(attn_out, ("dp", "fsdp"), axis=0, tiled=True),
        lax.all_gather(attn_out_bias, ("dp", "fsdp"), axis=0, tiled=True),
        lax.all_gather(rel_table, ("dp", "fsdp"), axis=0, tiled=True),
    )


def fetch_conv(
    conv_norm, glu_weight, glu_bias, depth_kernel, batch_norm, conv_out, conv_out_bias, final_norm
):
    return (
        lax.all_gather(conv_norm, ("dp", "fsdp"), axis=1, tiled=True),
        lax.all_gather(glu_weight, ("dp", "fsdp"), axis=0, tiled=True),
        lax.all_gather(glu_bias, ("dp", "fsdp"), axis=0, tiled=True),
        lax.all_gather(depth_kernel, ("dp", "fsdp"), axis=1, tiled=True),
        lax.all_gather(batch_norm, ("dp", "fsdp"), axis=1, tiled=True),
        lax.all_gather(conv_out, ("dp", "fsdp"), axis=0, tiled=True),
        lax.all_gather(conv_out_bias, ("dp", "fsdp"), axis=0, tiled=True),
        lax.all_gather(final_norm, ("dp", "fsdp"), axis=1, tiled=True),
    )


def feed_forward(values, weights):
    norm, weight_in, bias_in, weight_out, bias_out = weights
    normed, norm_back = jax.vjp(layer_norm, values, norm.astype(jnp.float32))
    normed_low = normed.astype(jnp.bfloat16)
    inner = product(normed_low, weight_in) + bias_in.astype(jnp.float32)
    active = jax.nn.silu(inner).astype(jnp.bfloat16)
    result = values + 0.5 * (product(active, weight_out) + bias_out.astype(jnp.float32))
    return (result, (normed_low, inner, active, norm_back))


def feed_backward(upstream, weights, saved):
    norm, weight_in, bias_in, weight_out, bias_out = weights
    normed_low, inner, active, norm_back = saved
    branch = 0.5 * upstream
    branch_low = branch.astype(jnp.bfloat16)
    grad_weight_out = product_left(active, branch_low)
    grad_inner = product_right(branch_low, weight_out) * silu_slope(inner)
    inner_low = grad_inner.astype(jnp.bfloat16)
    grad_weight_in = product_left(normed_low, inner_low)
    grad_values, grad_norm = norm_back(product_right(inner_low, weight_in))
    return (
        upstream + grad_values,
        (
            grad_norm,
            grad_weight_in,
            jnp.sum(grad_inner, axis=0),
            grad_weight_out,
            jnp.sum(branch, axis=0),
        ),
    )


def relative_lines(table, buckets):
    choose = (buckets[None, :] == jnp.arange(BUCKETS, dtype=jnp.int32)[:, None]).astype(jnp.float32)
    lines = jnp.dot(table.astype(jnp.float32).reshape(HEADS, BUCKETS), choose, precision=highest)
    return (lines, choose)


def bias_square(line, length):
    tiled = jnp.broadcast_to(line, (length, 2 * length - 1)).reshape(-1)
    tiled = jnp.concatenate([tiled, jnp.zeros((length,), line.dtype)])
    return tiled.reshape(length, 2 * length)[:, :length][::-1]


def diagonal_sums(square):
    length = square.shape[0]
    padded = jnp.concatenate([square[::-1], jnp.zeros_like(square)], axis=1).reshape(-1)
    return jnp.sum(padded[: length * (2 * length - 1)].reshape(length, 2 * length - 1), axis=0)


def head_scores(query, keys_head, line, same):
    raw = product_right(query, keys_head)
    return jnp.where(same, raw * HEAD_DIM ** (-0.5) + bias_square(line, query.shape[0]), -1e30)


def attention_forward(values, weights, marks, buckets):
    norm, mixer, weight_out, bias_out, table = weights
    length = values.shape[0]
    normed, norm_back = jax.vjp(layer_norm, values, norm.astype(jnp.float32))
    normed_low = normed.astype(jnp.bfloat16)
    mixed = (
        product(normed_low, mixer)
        .astype(jnp.bfloat16)
        .reshape(length, 3, HEADS, HEAD_DIM)
        .transpose(1, 2, 0, 3)
    )
    lines, choose = relative_lines(table, buckets)
    same = marks[:, None] == marks[None, :]

    def head_forward(items):
        query, keys_head, contents, line = items
        scores = head_scores(query, keys_head, line, same)
        peak = jnp.max(scores, axis=1, keepdims=True)
        raised = jnp.exp(scores - peak)
        total = jnp.sum(raised, axis=1, keepdims=True)
        probs = (raised / total).astype(jnp.bfloat16)
        return (product(probs, contents).astype(jnp.bfloat16), (peak + jnp.log(total))[:, 0])

    attended, logsum = lax.map(head_forward, (mixed[0], mixed[1], mixed[2], lines))
    joined = attended.transpose(1, 0, 2).reshape(length, D)
    result = values + product(joined, weight_out) + bias_out.astype(jnp.float32)
    return (result, (normed_low, mixed, lines, choose, same, joined, logsum, norm_back))


def attention_backward(upstream, weights, saved):
    norm, mixer, weight_out, bias_out, table = weights
    normed_low, mixed, lines, choose, same, joined, logsum, norm_back = saved
    length = upstream.shape[0]
    upstream_low = upstream.astype(jnp.bfloat16)
    grad_weight_out = product_left(joined, upstream_low)
    grad_joined = (
        product_right(upstream_low, weight_out)
        .astype(jnp.bfloat16)
        .reshape(length, HEADS, HEAD_DIM)
        .transpose(1, 0, 2)
    )

    def head_backward(items):
        query, keys_head, contents, line, incoming, logs = items
        scores = head_scores(query, keys_head, line, same)
        probs = jnp.exp(scores - logs[:, None])
        grad_contents = product_left(probs.astype(jnp.bfloat16), incoming)
        grad_probs = product_right(incoming, contents)
        grad_scores = probs * (grad_probs - jnp.sum(grad_probs * probs, axis=1, keepdims=True))
        scaled = (grad_scores * HEAD_DIM ** (-0.5)).astype(jnp.bfloat16)
        grad_query = product(scaled, keys_head)
        grad_keys = product_left(scaled, query)
        return (
            jnp.stack([grad_query, grad_keys, grad_contents]).astype(jnp.bfloat16),
            diagonal_sums(grad_scores),
        )

    grad_mixed, grad_lines = lax.map(
        head_backward, (mixed[0], mixed[1], mixed[2], lines, grad_joined, logsum)
    )
    grad_flat = grad_mixed.transpose(2, 1, 0, 3).reshape(length, 3 * D)
    grad_mixer = product_left(normed_low, grad_flat)
    grad_values, grad_norm = norm_back(product_right(grad_flat, mixer))
    grad_table = jnp.dot(grad_lines, choose.T, precision=highest).reshape(-1)
    return (
        upstream + grad_values,
        (grad_norm, grad_mixer, grad_weight_out, jnp.sum(upstream, axis=0), grad_table),
    )


def gate_unit(joined):
    width = joined.shape[1] // 2
    return joined[:, :width] * jax.nn.sigmoid(joined[:, width:])


def depthwise(gated, kernel, marks):
    length = gated.shape[0]
    half = kernel.shape[0] // 2
    padded = jnp.pad(gated, ((half, half), (0, 0)))
    bounds = jnp.pad(marks, (half, half), constant_values=-1)
    total = jnp.zeros(gated.shape, gated.dtype)
    for step in range(kernel.shape[0]):
        same = (bounds[step : step + length] == marks)[:, None]
        total = total + jnp.where(same, padded[step : step + length], 0.0) * kernel[step]
    return total


def conv_forward(values, weights, marks, frames):
    norm, weight_glu, bias_glu, kernel, batch, weight_out, bias_out, final = weights
    normed, norm_back = jax.vjp(layer_norm, values, norm.astype(jnp.float32))
    normed_low = normed.astype(jnp.bfloat16)
    joined = product(normed_low, weight_glu) + bias_glu.astype(jnp.float32)
    gated, gate_back = jax.vjp(gate_unit, joined)
    middle, depth_back = jax.vjp(
        lambda inner, taps: depthwise(inner, taps, marks), gated, kernel.astype(jnp.float32)
    )
    sums = lax.psum((jnp.sum(middle, axis=0), jnp.sum(middle * middle, axis=0)), ("dp", "fsdp"))
    center = sums[0] / frames
    inverse = lax.rsqrt(sums[1] / frames - center * center + epsilon)
    gain = 1.0 + batch[0].astype(jnp.float32)
    unit = (middle - center) * inverse
    normal = unit * gain + batch[1].astype(jnp.float32)
    active = jax.nn.silu(normal).astype(jnp.bfloat16)
    result = values + product(active, weight_out) + bias_out.astype(jnp.float32)
    return (
        result,
        (normed_low, gate_back, depth_back, inverse, gain, unit, normal, active, norm_back),
    )


def conv_backward(upstream, weights, saved, frames):
    norm, weight_glu, bias_glu, kernel, batch, weight_out, bias_out, final = weights
    normed_low, gate_back, depth_back, inverse, gain, unit, normal, active, norm_back = saved
    upstream_low = upstream.astype(jnp.bfloat16)
    grad_weight_out = product_left(active, upstream_low)
    grad_normal = product_right(upstream_low, weight_out) * silu_slope(normal)
    sums = lax.psum(
        (jnp.sum(grad_normal, axis=0), jnp.sum(grad_normal * unit, axis=0)), ("dp", "fsdp")
    )
    grad_middle = inverse * (
        grad_normal * gain - gain * sums[0] / frames - unit * (gain * sums[1] / frames)
    )
    grad_gated, grad_kernel = depth_back(grad_middle)
    grad_joined = gate_back(grad_gated)[0]
    joined_low = grad_joined.astype(jnp.bfloat16)
    grad_weight_glu = product_left(normed_low, joined_low)
    grad_values, grad_norm = norm_back(product_right(joined_low, weight_glu))
    grad_batch = jnp.stack([sums[1], sums[0]])
    return (
        upstream + grad_values,
        (
            grad_norm,
            grad_weight_glu,
            jnp.sum(grad_joined, axis=0),
            grad_kernel,
            grad_weight_out,
            jnp.sum(upstream, axis=0),
        ),
        grad_batch,
    )


def local(
    inputs,
    segments,
    buckets,
    cotangent,
    ffn_norm,
    ffn_in,
    ffn_in_bias,
    ffn_out,
    ffn_out_bias,
    attn_norm,
    qkv_weight,
    attn_out,
    attn_out_bias,
    rel_table,
    conv_norm,
    glu_weight,
    glu_bias,
    depth_kernel,
    batch_norm,
    conv_out,
    conv_out_bias,
    final_norm,
):
    values = inputs[0].astype(jnp.float32)
    marks = segments[0]
    devices = lax.axis_size(("dp", "fsdp"))
    frames = values.shape[0] * devices
    feed_first = fetch_feed(ffn_norm, ffn_in, ffn_in_bias, ffn_out, ffn_out_bias, 0)
    first, first_saved = feed_forward(values, feed_first)
    attn_weights = fetch_attention(attn_norm, qkv_weight, attn_out, attn_out_bias, rel_table)
    second, attn_saved = attention_forward(first, attn_weights, marks, buckets)
    conv_weights = fetch_conv(
        conv_norm,
        glu_weight,
        glu_bias,
        depth_kernel,
        batch_norm,
        conv_out,
        conv_out_bias,
        final_norm,
    )
    third, conv_saved = conv_forward(second, conv_weights, marks, frames)
    feed_second = fetch_feed(ffn_norm, ffn_in, ffn_in_bias, ffn_out, ffn_out_bias, 1)
    fourth, second_saved = feed_forward(third, feed_second)
    result, final_back = jax.vjp(layer_norm, fourth, conv_weights[7].astype(jnp.float32))
    grad_fourth, grad_final = final_back(cotangent[0].astype(jnp.float32))
    second_back = fetch_feed(ffn_norm, ffn_in, ffn_in_bias, ffn_out, ffn_out_bias, 1)
    grad_third, second_grads = feed_backward(grad_fourth, second_back, second_saved)
    conv_back = fetch_conv(
        conv_norm,
        glu_weight,
        glu_bias,
        depth_kernel,
        batch_norm,
        conv_out,
        conv_out_bias,
        final_norm,
    )
    grad_second, conv_grads, grad_batch = conv_backward(grad_third, conv_back, conv_saved, frames)
    attn_back = fetch_attention(attn_norm, qkv_weight, attn_out, attn_out_bias, rel_table)
    grad_first, attn_grads = attention_backward(grad_second, attn_back, attn_saved)
    first_back = fetch_feed(ffn_norm, ffn_in, ffn_in_bias, ffn_out, ffn_out_bias, 0)
    grad_start, first_grads = feed_backward(grad_first, first_back, first_saved)
    first_shards = reduce_feed(first_grads)
    second_shards = reduce_feed(second_grads)
    attn_shards = (
        lax.psum_scatter(attn_grads[0], ("dp", "fsdp"), scatter_dimension=1, tiled=True),
        lax.psum_scatter(attn_grads[1], ("dp", "fsdp"), scatter_dimension=0, tiled=True),
        lax.psum_scatter(attn_grads[2], ("dp", "fsdp"), scatter_dimension=0, tiled=True),
        lax.psum_scatter(attn_grads[3], ("dp", "fsdp"), scatter_dimension=0, tiled=True),
        lax.psum_scatter(attn_grads[4], ("dp", "fsdp"), scatter_dimension=0, tiled=True),
    )
    conv_shards = (
        lax.psum_scatter(conv_grads[0], ("dp", "fsdp"), scatter_dimension=1, tiled=True),
        lax.psum_scatter(conv_grads[1], ("dp", "fsdp"), scatter_dimension=0, tiled=True),
        lax.psum_scatter(conv_grads[2], ("dp", "fsdp"), scatter_dimension=0, tiled=True),
        lax.psum_scatter(conv_grads[3], ("dp", "fsdp"), scatter_dimension=1, tiled=True),
        lax.psum_scatter(conv_grads[4], ("dp", "fsdp"), scatter_dimension=0, tiled=True),
        lax.psum_scatter(conv_grads[5], ("dp", "fsdp"), scatter_dimension=0, tiled=True),
        lax.psum_scatter(grad_final, ("dp", "fsdp"), scatter_dimension=1, tiled=True),
    )
    width = D // devices
    batch_shard = lax.dynamic_slice_in_dim(
        grad_batch, lax.axis_index(("dp", "fsdp")) * width, width, 1
    )
    return (
        result[None].astype(jnp.bfloat16),
        grad_start[None],
        jnp.stack([first_shards[0], second_shards[0]]),
        jnp.stack([first_shards[1], second_shards[1]]),
        jnp.stack([first_shards[2], second_shards[2]]),
        jnp.stack([first_shards[3], second_shards[3]]),
        jnp.stack([first_shards[4], second_shards[4]]),
        attn_shards[0],
        attn_shards[1],
        attn_shards[2],
        attn_shards[3],
        attn_shards[4],
        conv_shards[0],
        conv_shards[1],
        conv_shards[2],
        conv_shards[3],
        batch_shard,
        conv_shards[4],
        conv_shards[5],
        conv_shards[6],
    )


def solution(mesh):
    in_specs = (
        P(("dp", "fsdp"), None, None),
        P(("dp", "fsdp"), None),
        P(),
        P(("dp", "fsdp"), None, None),
        P(None, None, ("dp", "fsdp")),
        P(None, ("dp", "fsdp"), None),
        P(None, ("dp", "fsdp")),
        P(None, ("dp", "fsdp"), None),
        P(None, ("dp", "fsdp")),
        P(None, ("dp", "fsdp")),
        P(("dp", "fsdp"), None),
        P(("dp", "fsdp"), None),
        P(("dp", "fsdp")),
        P(("dp", "fsdp")),
        P(None, ("dp", "fsdp")),
        P(("dp", "fsdp"), None),
        P(("dp", "fsdp")),
        P(None, ("dp", "fsdp")),
        P(None, ("dp", "fsdp")),
        P(("dp", "fsdp"), None),
        P(("dp", "fsdp")),
        P(None, ("dp", "fsdp")),
    )
    out_specs = (
        P(("dp", "fsdp"), None, None),
        P(("dp", "fsdp"), None, None),
        P(None, None, ("dp", "fsdp")),
        P(None, ("dp", "fsdp"), None),
        P(None, ("dp", "fsdp")),
        P(None, ("dp", "fsdp"), None),
        P(None, ("dp", "fsdp")),
        P(None, ("dp", "fsdp")),
        P(("dp", "fsdp"), None),
        P(("dp", "fsdp"), None),
        P(("dp", "fsdp")),
        P(("dp", "fsdp")),
        P(None, ("dp", "fsdp")),
        P(("dp", "fsdp"), None),
        P(("dp", "fsdp")),
        P(None, ("dp", "fsdp")),
        P(None, ("dp", "fsdp")),
        P(("dp", "fsdp"), None),
        P(("dp", "fsdp")),
        P(None, ("dp", "fsdp")),
    )
    return jax.shard_map(local, mesh=mesh, in_specs=in_specs, out_specs=out_specs, check_vma=False)
```

profile of v0, /device:TPU:0, one launch (start us, length us, event | category | flops | bytes accessed | tf_op | source)
XLA Modules:
  0.0 2691.1 jit_solution(2605218609612252322)
XLA Ops:
  16.4 43.2 %all-gather.12 = bf16[32,16,2]{1,2,0:T(2,128)(2,1)S(1)} all-gather(bf16[1,16,2]{1,2,0:T(2,128)(2,1)} %bitcast.458), channel_id=1, replica_groups=mesh['dp'=4,'fsdp'=8] {'dp','fsdp'}, dimensions={0}, use_global_device_ids=true | all-gather | bytes 2112 | tf_op jit(solution)/shard_map/all_gather | solution.py:81
  60.3 37.3 %all_gather.90 = bf16[32,512]{0,1:T(8,128)(2,1)S(1)} all-gather(bf16[32,16]{0,1:T(8,128)(2,1)} %param.43), channel_id=1, replica_groups=mesh['dp'=4,'fsdp'=8] {'dp','fsdp'}, dimensions={1}, use_global_device_ids=true | all-gather | bytes 33792 | tf_op jit(solution)/shard_map/all_gather | solution.py:80
  104.3 40.0 %all-reduce.100 = (bf16[512]{0:T(512)(128)(2,1)S(1)}, bf16[2048]{0:T(1024)(128)(2,1)S(1)}, bf16[256]{0:T(256)(128)(2,1)S(1)}, bf16[512]{0:T(512)(128)(2,1)S(1)},...) all-reduce(bf16[512]{0:T(512)(128)(2,1)S(1)} %dynamic-update-slice., ...), channel_id=6, replica_groups=mesh['dp'=4,'fsdp'=8] {'dp','fsdp'}, use_global_device_ids=true, to_apply=%add.82 | all-reduce | flops 7424 | bytes 29696
  146.4 39.2 %all-gather.10 = bf16[32,16,2]{1,2,0:T(2,128)(2,1)S(1)} all-gather(bf16[1,16,2]{1,2,0:T(2,128)(2,1)S(1)} %bitcast.459), channel_id=1, replica_groups=mesh['dp'=4,'fsdp'=8] {'dp','fsdp'}, dimensions={0}, use_global_device_ids=true | all-gather | bytes 2112 | tf_op jit(solution)/shard_map/all_gather | solution.py:65
  185.6 36.4 %all-gather.11 = bf16[32,16,2]{1,2,0:T(2,128)(2,1)S(1)} all-gather(bf16[1,16,2]{1,2,0:T(2,128)(2,1)S(1)} %bitcast.460), channel_id=1, replica_groups=mesh['dp'=4,'fsdp'=8] {'dp','fsdp'}, dimensions={0}, use_global_device_ids=true | all-gather | bytes 2112 | tf_op jit(solution)/shard_map/all_gather | solution.py:77
  222.1 37.8 %all-gather.13 = bf16[32,16,2]{1,2,0:T(2,128)(2,1)S(1)} all-gather(bf16[1,16,2]{1,2,0:T(2,128)(2,1)S(1)} %bitcast.461), channel_id=1, replica_groups=mesh['dp'=4,'fsdp'=8] {'dp','fsdp'}, dimensions={0}, use_global_device_ids=true | all-gather | bytes 2112 | tf_op jit(solution)/shard_map/all_gather | solution.py:84
  260.6 38.3 %all-gather = bf16[1,2,512]{1,0,2:T(2,128)(2,1)S(1)} all-gather(bf16[1,2,16]{1,0,2:T(2,128)(2,1)S(1)} %copy.236), channel_id=2, replica_groups=mesh['dp'=4,'fsdp'=8] {'dp','fsdp'}, dimensions={2}, use_global_device_ids=true | all-gather | bytes 2112 | tf_op jit(solution)/shard_map/all_gather | solution.py:45
  299.2 3.1 fusion.119
  302.3 39.2 %all-gather.5 = bf16[1,2,512]{1,0,2:T(2,128)(2,1)S(1)} all-gather(bf16[1,2,16]{1,0,2:T(2,128)(2,1)S(1)} %copy.237), channel_id=7, replica_groups=mesh['dp'=4,'fsdp'=8] {'dp','fsdp'}, dimensions={2}, use_global_device_ids=true | all-gather | bytes 2112 | tf_op jit(solution)/shard_map/all_gather | solution.py:45
  341.8 3.1 fusion.120
  345.8 42.3 %all_gather.85 = bf16[512,512]{1,0:T(8,128)(2,1)} all-gather(bf16[16,512]{1,0:T(8,128)(2,1)S(1)} %copy-done.69), channel_id=1, replica_groups=mesh['dp'=4,'fsdp'=8] {'dp','fsdp'}, dimensions={0}, use_global_device_ids=true | all-gather | bytes 540672 | tf_op jit(solution)/shard_map/all_gather | solution.py:67
  388.1 42.7 %all_gather.92 = bf16[512,512]{1,0:T(8,128)(2,1)} all-gather(bf16[16,512]{1,0:T(8,128)(2,1)S(1)} %copy-done.70), channel_id=1, replica_groups=mesh['dp'=4,'fsdp'=8] {'dp','fsdp'}, dimensions={0}, use_global_device_ids=true | all-gather | bytes 540672 | tf_op jit(solution)/shard_map/all_gather | solution.py:82
  431.0 5.1 fusion.60
  436.2 4.6 fusion.192
  441.1 3.8 convolution_convert_fusion.4
  451.2 114.5 %while.26 = (s32[]{:T(128)}, bf16[8,512,64]{1,2,0:T(8,128)(2,1)}, f32[8,512]{1,0:T(8,128)}, bf16[8,512,64]{2,1,0:T(8,128)(2,1)}, bf16[8,512,64]{2,1,0:T(8,128)(2...) while((s32[]{:T(128)}, bf16[8,512,64]{1,2,0:T(8,128)(2,1)}, ...), condition=%wide.region_7.8_spmd.clone, body=%wide.region_4.7_spmd.clone.sunk | while | flops 69762560 | bytes 25655412 | solution.py:166
  572.3 7.3 fusion.184
  579.6 38.1 %all-reduce.99 = (f32[512]{0:T(512)S(1)}, f32[512]{0:T(512)S(1)}) all-reduce(f32[512]{0:T(512)S(1)} %get-tuple-element.417, f32[512]{0:T(512)S(1)} %get-tuple-element.416), channel_id=1, replica_groups=mesh['dp'=4,'fsdp'=8] {'dp','fsdp'}, use_global_device_ids=true, to_apply=%region_13.14 | all-reduce | flops 1024 | bytes 8192 | tf_op jit(solution)/shard_map/psum | solution.py:239
  620.0 5.1 fusion.53
  625.2 4.7 fusion.195
  646.1 41.0 %all-reduce.98 = (f32[512]{0:T(512)S(1)}, f32[512]{0:T(512)S(1)}) all-reduce(f32[512]{0:T(512)S(1)} %get-tuple-element.415, f32[512]{0:T(512)S(1)} %get-tuple-element.414), channel_id=1, replica_groups=mesh['dp'=4,'fsdp'=8] {'dp','fsdp'}, use_global_device_ids=true, to_apply=%region_25.26 | all-reduce | flops 1024 | bytes 8192 | tf_op jit(solution)/shard_map/psum | solution.py:259
  695.2 4.1 multiply_select_fusion.30
  699.4 4.0 multiply_select_fusion.29
  703.4 4.0 multiply_select_fusion.28
  708.4 10.5 pad_add_fusion.1
  731.0 194.7 %while.27 = (s32[]{:T(128)}, bf16[8,3,512,64]{2,3,0,1:T(8,128)(2,1)}, f32[8,1023]{1,0:T(8,128)S(1)}, bf16[8,512,64]{2,1,0:T(8,128)(2,1)}, bf16[8,512,64]{2,1,0:T...) while((s32[]{:T(128)}, ...), condition=%wide.region_31.32_spmd.clone, body=%wide.region_28.31_spmd.clone.sunk | while | flops 172652544 | bytes 51865768 | solution.py:200
  800.0 3.0 reshape.705
  824.4 3.0 reshape.705
  948.2 6.1 fusion.127
  955.4 5.8 fusion.121
  962.4 5.0 fusion.109
  968.5 4.9 fusion.106
  980.4 3.2 fusion.116
  986.4 3.6 fusion.123
  997.9 39.4 %all-reduce.97 = (f32[2048]{0:T(1024)S(1)}, f32[2048]{0:T(1024)S(1)}, f32[512]{0:T(512)S(1)}, f32[512]{0:T(512)S(1)}, f32[512]{0:T(512)S(1)}, /*index=5*/f32[256]{0:T(256)S(1)}, f32[1024]{0:T(1024)S(1)}, f32[512]{0:T(512)S(1)}) all-reduce(f32[2048]{0:T(1024)S(1)} %copy-done.85, ...), channel_id=17, replica_groups=mesh['dp'=4,'fsdp'=8] {'dp','fsdp'}, use_global_device_ids=true, to_apply=%region_47.48.clone | all-reduce | flops 7424 | bytes 59392
  1045.8 32.2 %reduce-scatter.45.cloned.1.call-done = f32[16,2]{1,0:T(8,128)} async-done(((f32[512,2]{1,0:T(8,128)}), f32[16,2]{1,0:T(8,128)}) %reduce-scatter.45.cloned.1.call-update) | async-done | bytes 144
  1078.8 131.6 %reduce-scatter.49.cloned.1.call-done = f32[16,2]{1,0:T(8,128)} async-done(((f32[512,2]{1,0:T(8,128)}), f32[16,2]{1,0:T(8,128)}) %reduce-scatter.49.cloned.1.call-update) | async-done | bytes 144
  1211.7 131.0 %reduce-scatter.47.cloned.1.call-done = f32[16,2]{1,0:T(8,128)} async-done(((f32[512,2]{1,0:T(8,128)}), f32[16,2]{1,0:T(8,128)}) %reduce-scatter.47.cloned.1.call-update) | async-done | bytes 144
  1344.0 131.6 %reduce-scatter.43.cloned.1.call-done = f32[16,2]{1,0:T(8,128)} async-done(((f32[512,2]{1,0:T(8,128)}), f32[16,2]{1,0:T(8,128)}) %reduce-scatter.43.cloned.1.call-update) | async-done | bytes 144
  1477.0 140.2 %reduce-scatter.33.cloned.1.call-done = f32[64,512]{1,0:T(8,128)} async-done(((f32[2048,512]{1,0:T(8,128)}), f32[64,512]{1,0:T(8,128)}) %reduce-scatter.33.cloned.1.call-update) | async-done | bytes 131088 | tf_op jit(solution)/shard_map/reduce_scatter | solution.py:58
  1617.3 141.7 %reduce-scatter.31.cloned.1.call-done = f32[64,512]{1,0:T(8,128)} async-done(((f32[2048,512]{1,0:T(8,128)}), f32[64,512]{1,0:T(8,128)}) %reduce-scatter.31.cloned.1.call-update) | async-done | bytes 131088 | tf_op jit(solution)/shard_map/reduce_scatter | solution.py:58
  1760.6 140.2 %reduce-scatter.29.cloned.1.call-done = f32[16,2048]{1,0:T(8,128)} async-done(((f32[512,2048]{1,0:T(8,128)}), f32[16,2048]{1,0:T(8,128)}) %reduce-scatter.29.cloned.1.call-update) | async-done | bytes 131088 | tf_op jit(solution)/shard_map/reduce_scatter | solution.py:56
  1900.8 141.3 %reduce-scatter.27.cloned.1.call-done = f32[16,2048]{1,0:T(8,128)} async-done(((f32[512,2048]{1,0:T(8,128)}), f32[16,2048]{1,0:T(8,128)}) %reduce-scatter.27.cloned.1.call-update) | async-done | bytes 131088 | tf_op jit(solution)/shard_map/reduce_scatter | solution.py:56
  2043.8 131.5 %reduce-scatter.51.cloned.1.call-done = f32[16,32]{1,0:T(8,128)} async-done(((f32[512,32]{1,0:T(8,128)}), f32[16,32]{1,0:T(8,128)}) %reduce-scatter.51.cloned.1.call-update) | async-done | bytes 2064
  2175.3 134.2 %reduce-scatter.41.cloned.1.call-done = f32[16,512]{1,0:T(8,128)} async-done(((f32[512,512]{1,0:T(8,128)}), f32[16,512]{1,0:T(8,128)}) %reduce-scatter.41.cloned.1.call-update) | async-done | bytes 32784 | tf_op jit(solution)/shard_map/reduce_scatter | solution.py:363
  2309.5 133.9 %reduce-scatter.37.cloned.1.call-done = f32[16,512]{1,0:T(8,128)} async-done(((f32[512,512]{1,0:T(8,128)}), f32[16,512]{1,0:T(8,128)}) %reduce-scatter.37.cloned.1.call-update) | async-done | bytes 32784 | tf_op jit(solution)/shard_map/reduce_scatter | solution.py:354
  2443.5 136.1 %reduce-scatter.39.cloned.1.call-done = f32[16,1024]{1,0:T(8,128)} async-done(((f32[512,1024]{1,0:T(8,128)}), f32[16,1024]{1,0:T(8,128)}) %reduce-scatter.39.cloned.1.call-update) | async-done | bytes 65552 | tf_op jit(solution)/shard_map/reduce_scatter | solution.py:360
  2579.5 104.5 %reduce-scatter.35.cloned.1.call-done = f32[16,1536]{1,0:T(8,128)} async-done(((f32[512,1536]{1,0:T(8,128)}), f32[16,1536]{1,0:T(8,128)}) %reduce-scatter.35.cloned.1.call-update) | async-done | bytes 98320 | tf_op jit(solution)/shard_map/reduce_scatter | solution.py:353
  (850 shorter events, 434.0 us)
Async XLA Ops:
  7.2 423.8 %all-gather.25.cloned.1.call-start = ((), (), s32[]{:S(2)}) async-start(), calls=%async_computation.24 | async-start | bytes 2162688 | tf_op jit(solution)/shard_map/all_gather | solution.py:46
  8.8 427.3 %all-gather.27.cloned.1.call-start = ((), (), s32[]{:S(2)}) async-start(), calls=%async_computation.25 | async-start | bytes 2162688 | tf_op jit(solution)/shard_map/all_gather | solution.py:48
  10.4 430.7 %all-gather.21.cloned.1.call-start = ((), (), s32[]{:S(2)}) async-start(), calls=%async_computation.14 | async-start | bytes 1622016 | tf_op jit(solution)/shard_map/all_gather | solution.py:66
  11.1 556.9 %all-gather.23.cloned.1.call-start = ((), (), s32[]{:S(2)}) async-start(), calls=%async_computation.15 | async-start | bytes 1081344 | tf_op jit(solution)/shard_map/all_gather | solution.py:78
  11.7 608.3 %all-gather.29.cloned.1.call-start = ((), (), s32[]{:S(2)}) async-start(), calls=%async_computation.26 | async-start | bytes 2162688 | tf_op jit(solution)/shard_map/all_gather | solution.py:46
  12.3 612.8 %all-gather.31.cloned.1.call-start = ((), (), s32[]{:S(2)}) async-start(), calls=%async_computation.27 | async-start | bytes 2162688 | tf_op jit(solution)/shard_map/all_gather | solution.py:48
  12.9 1031.6 %reduce-scatter.53.cloned.1.call-start = ((), (), s32[]{:S(2)}) async-start(), calls=%async_computation.33 | async-start | bytes 270336
  14.2 557.7 %copy-start.92 = (pred[512]{0:T(512)(128)(4,1)}, pred[512]{0:T(512)(128)(4,1)S(1)}, u32[]{:S(2)}) copy-start(pred[512]{0:T(512)(128)(4,1)S(1)} %get-tuple-element.595) | copy-start | bytes 1540
  14.2 557.7 %copy-start.95 = (pred[512]{0:T(512)(128)(4,1)}, pred[512]{0:T(512)(128)(4,1)S(1)}, u32[]{:S(2)}) copy-start(pred[512]{0:T(512)(128)(4,1)S(1)} %get-tuple-element.601) | copy-start | bytes 1540
  14.2 557.7 %copy-start.98 = (pred[512]{0:T(512)(128)(4,1)}, pred[512]{0:T(512)(128)(4,1)S(1)}, u32[]{:S(2)}) copy-start(pred[512]{0:T(512)(128)(4,1)S(1)} %get-tuple-element.602) | copy-start | bytes 1540
  14.2 557.7 %copy-start.101 = (pred[512]{0:T(512)(128)(4,1)}, pred[512]{0:T(512)(128)(4,1)S(1)}, u32[]{:S(2)}) copy-start(pred[512]{0:T(512)(128)(4,1)S(1)} %get-tuple-element.603) | copy-start | bytes 1540
  14.3 557.7 %copy-start.104 = (pred[512]{0:T(512)(128)(4,1)}, pred[512]{0:T(512)(128)(4,1)S(1)}, u32[]{:S(2)}) copy-start(pred[512]{0:T(512)(128)(4,1)S(1)} %get-tuple-element.604) | copy-start | bytes 1540
  14.3 557.7 %copy-start.107 = (pred[512]{0:T(512)(128)(4,1)}, pred[512]{0:T(512)(128)(4,1)S(1)}, u32[]{:S(2)}) copy-start(pred[512]{0:T(512)(128)(4,1)S(1)} %get-tuple-element.605) | copy-start | bytes 1540
  14.3 557.7 %copy-start.110 = (pred[512]{0:T(512)(128)(4,1)}, pred[512]{0:T(512)(128)(4,1)S(1)}, u32[]{:S(2)}) copy-start(pred[512]{0:T(512)(128)(4,1)S(1)} %get-tuple-element.606) | copy-start | bytes 1540
  14.3 557.7 %copy-start.113 = (pred[512]{0:T(512)(128)(4,1)}, pred[512]{0:T(512)(128)(4,1)S(1)}, u32[]{:S(2)}) copy-start(pred[512]{0:T(512)(128)(4,1)S(1)} %get-tuple-element.607) | copy-start | bytes 1540
  14.3 557.7 %copy-start.116 = (pred[512]{0:T(512)(128)(4,1)}, pred[512]{0:T(512)(128)(4,1)S(1)}, u32[]{:S(2)}) copy-start(pred[512]{0:T(512)(128)(4,1)S(1)} %get-tuple-element.596) | copy-start | bytes 1540
  14.3 557.7 %copy-start.118 = (pred[512]{0:T(512)(128)(4,1)}, pred[512]{0:T(512)(128)(4,1)S(1)}, u32[]{:S(2)}) copy-start(pred[512]{0:T(512)(128)(4,1)S(1)} %get-tuple-element.597) | copy-start | bytes 1540
  14.3 557.7 %copy-start.121 = (pred[512]{0:T(512)(128)(4,1)}, pred[512]{0:T(512)(128)(4,1)S(1)}, u32[]{:S(2)}) copy-start(pred[512]{0:T(512)(128)(4,1)S(1)} %get-tuple-element.598) | copy-start | bytes 1540
  14.3 557.7 %copy-start.124 = (pred[512]{0:T(512)(128)(4,1)}, pred[512]{0:T(512)(128)(4,1)S(1)}, u32[]{:S(2)}) copy-start(pred[512]{0:T(512)(128)(4,1)S(1)} %get-tuple-element.599) | copy-start | bytes 1540
  14.3 557.7 %copy-start.127 = (pred[512]{0:T(512)(128)(4,1)}, pred[512]{0:T(512)(128)(4,1)S(1)}, u32[]{:S(2)}) copy-start(pred[512]{0:T(512)(128)(4,1)S(1)} %get-tuple-element.600) | copy-start | bytes 1540
  16.3 555.7 %copy-start.130 = (pred[512]{0:T(512)(128)(4,1)}, pred[512]{0:T(512)(128)(4,1)S(1)}, u32[]{:S(2)}) copy-start(pred[512]{0:T(512)(128)(4,1)S(1)} %get-tuple-element.577) | copy-start | bytes 1540
  16.3 555.7 %copy-start.133 = (pred[512]{0:T(512)(128)(4,1)}, pred[512]{0:T(512)(128)(4,1)S(1)}, u32[]{:S(2)}) copy-start(pred[512]{0:T(512)(128)(4,1)S(1)} %get-tuple-element.578) | copy-start | bytes 1540
  16.3 670.7 %copy-start.86 = (pred[512]{0:T(512)(128)(4,1)}, pred[512]{0:T(512)(128)(4,1)S(1)}, u32[]{:S(2)}) copy-start(pred[512]{0:T(512)(128)(4,1)S(1)} %get-tuple-element.581) | copy-start | bytes 1540
  16.4 670.7 %copy-start.88 = (pred[512]{0:T(512)(128)(4,1)}, pred[512]{0:T(512)(128)(4,1)S(1)}, u32[]{:S(2)}) copy-start(pred[512]{0:T(512)(128)(4,1)S(1)} %get-tuple-element.582) | copy-start | bytes 1540
  16.4 670.7 %copy-start.90 = (pred[512]{0:T(512)(128)(4,1)}, pred[512]{0:T(512)(128)(4,1)S(1)}, u32[]{:S(2)}) copy-start(pred[512]{0:T(512)(128)(4,1)S(1)} %get-tuple-element.583) | copy-start | bytes 1540
  99.7 122.5 %copy-start.159 = (bf16[2,16]{1,0:T(2,128)(2,1)S(1)}, bf16[2,16]{1,0:T(2,128)(2,1)}, u32[]{:S(2)}) copy-start(bf16[2,16]{1,0:T(2,128)(2,1)} %param.47) | copy-start | bytes 196
  102.3 242.5 %copy-start.48 = (bf16[1,512,512]{2,1,0:T(8,128)(2,1)S(1)}, bf16[1,512,512]{2,1,0:T(8,128)(2,1)}, u32[]{:S(2)}) copy-start(bf16[1,512,512]{2,1,0:T(8,128)(2,1)} %param.26) | copy-start | bytes 1572868
  146.2 289.9 %copy-start.79 = (f32[2048]{0:T(1024)}, f32[2048]{0:T(1024)S(1)}, u32[]{:S(2)}) copy-start(f32[2048]{0:T(1024)S(1)} %convert_element_type.181) | copy-start | bytes 24580
  260.4 307.6 %copy-start.73 = (f32[1,512]{1,0:T(1,128)}, f32[1,512]{1,0:T(1,128)S(1)}, u32[]{:S(2)}) copy-start(f32[1,512]{1,0:T(1,128)S(1)} %get-tuple-element.570) | copy-start | bytes 6148
  260.6 180.5 %copy-start.55 = (f32[1,512]{1,0:T(1,128)}, f32[1,512]{1,0:T(1,128)S(1)}, u32[]{:S(2)}) copy-start(f32[1,512]{1,0:T(1,128)S(1)} %get-tuple-element.571) | copy-start | bytes 6148
  260.6 180.5 %copy-start.75 = (f32[1,512]{1,0:T(1,128)}, f32[1,512]{1,0:T(1,128)S(1)}, u32[]{:S(2)}) copy-start(f32[1,512]{1,0:T(1,128)S(1)} %get-tuple-element.572) | copy-start | bytes 6148
  302.2 128.8 %copy-start.61 = (f32[512]{0:T(512)}, f32[512]{0:T(512)S(1)}, u32[]{:S(2)}) copy-start(f32[512]{0:T(512)S(1)} %get-tuple-element.452) | copy-start | bytes 6148
  302.2 128.7 %copy-start.147 = (f32[512]{0:T(512)}, f32[512]{0:T(512)S(1)}, u32[]{:S(2)}) copy-start(f32[512]{0:T(512)S(1)} %get-tuple-element.453) | copy-start | bytes 6148
  344.8 275.1 %copy-start.51 = (f32[512]{0:T(512)}, f32[512]{0:T(512)S(1)}, u32[]{:S(2)}) copy-start(f32[512]{0:T(512)S(1)} %get-tuple-element.419) | copy-start | bytes 6148
  567.8 159.0 %copy-start.2 = (f32[512,512]{0,1:T(8,128)}, f32[512,512]{0,1:T(8,128)S(1)}, u32[]{:S(2)}) copy-start(f32[512,512]{0,1:T(8,128)S(1)} %get-tuple-element.617) | copy-start | bytes 3145732
  708.3 369.7 %reduce-scatter.45.cloned.1.call-start = ((), (), s32[]{:S(2)}) async-start(), calls=%async_computation.29 | async-start | bytes 270336
  945.2 265.1 %reduce-scatter.49.cloned.1.call-start = ((), (), s32[]{:S(2)}) async-start(), calls=%async_computation.31 | async-start | bytes 270336
  946.2 396.5 %reduce-scatter.47.cloned.1.call-start = ((), (), s32[]{:S(2)}) async-start(), calls=%async_computation.30 | async-start | bytes 270336
  947.2 528.5 %reduce-scatter.43.cloned.1.call-start = ((), (), s32[]{:S(2)}) async-start(), calls=%async_computation.28 | async-start | bytes 270336
  948.1 669.2 %reduce-scatter.33.cloned.1.call-start = ((), (), s32[]{:S(2)}) async-start(), calls=%async_computation.19 | async-start | bytes 4325376 | tf_op jit(solution)/shard_map/reduce_scatter | solution.py:58
  954.2 804.7 %reduce-scatter.31.cloned.1.call-start = ((), (), s32[]{:S(2)}) async-start(), calls=%async_computation.18 | async-start | bytes 4325376 | tf_op jit(solution)/shard_map/reduce_scatter | solution.py:58
  961.2 939.6 %reduce-scatter.29.cloned.1.call-start = ((), (), s32[]{:S(2)}) async-start(), calls=%async_computation.17 | async-start | bytes 4325376 | tf_op jit(solution)/shard_map/reduce_scatter | solution.py:56
  967.5 1074.7 %reduce-scatter.27.cloned.1.call-start = ((), (), s32[]{:S(2)}) async-start(), calls=%async_computation.16 | async-start | bytes 4325376 | tf_op jit(solution)/shard_map/reduce_scatter | solution.py:56
  973.6 1201.7 %reduce-scatter.51.cloned.1.call-start = ((), (), s32[]{:S(2)}) async-start(), calls=%async_computation.32 | async-start | bytes 270336
  980.3 1329.2 %reduce-scatter.41.cloned.1.call-start = ((), (), s32[]{:S(2)}) async-start(), calls=%async_computation.23 | async-start | bytes 1081344 | tf_op jit(solution)/shard_map/reduce_scatter | solution.py:363
  983.7 1459.8 %reduce-scatter.37.cloned.1.call-start = ((), (), s32[]{:S(2)}) async-start(), calls=%async_computation.21 | async-start | bytes 1081344 | tf_op jit(solution)/shard_map/reduce_scatter | solution.py:354
  986.3 1593.2 %reduce-scatter.39.cloned.1.call-start = ((), (), s32[]{:S(2)}) async-start(), calls=%async_computation.22 | async-start | bytes 2162688 | tf_op jit(solution)/shard_map/reduce_scatter | solution.py:360
  990.1 1693.9 %reduce-scatter.35.cloned.1.call-start = ((), (), s32[]{:S(2)}) async-start(), calls=%async_computation.20 | async-start | bytes 3244032 | tf_op jit(solution)/shard_map/reduce_scatter | solution.py:353
  (150 other events, 1447.4 us)
Sparse Core Ops, SparseCore 0:
  11.6 59.2 all-gather.24
  74.5 55.4 all-gather.26
  133.0 54.0 all-gather.20
  189.9 52.6 all-gather.22
  246.0 55.7 all-gather.28
  305.2 55.9 all-gather.30
  708.4 133.3 reduce-scatter.52
  945.4 132.5 reduce-scatter.44
  1080.2 130.0 reduce-scatter.48
  1212.5 130.1 reduce-scatter.46
  1345.5 130.1 reduce-scatter.42
  1477.9 139.3 reduce-scatter.32
  1619.6 139.2 reduce-scatter.30
  1761.2 139.6 reduce-scatter.28
  1903.1 139.0 reduce-scatter.26
  2044.9 130.3 reduce-scatter.50
  2178.0 131.5 reduce-scatter.40
  2312.3 131.1 reduce-scatter.36
  2446.3 133.1 reduce-scatter.38
  2586.3 97.6 reduce-scatter.34
where the time goes:
time: 2700 us; the launch traced here: 2690 us
  waiting for transfers between devices  1630 us (60%)
  blocking collectives  515 us (19%)
  local copies, waits for them, and re-layouts  280 us (10%)
  matrix products  156 us (6%)
  other arithmetic  88.9 us (3%)
    unnamed x26, waiting for transfers between devices  560 us
    reduce_scatter x2, waiting for transfers between devices, reduce_feed(): lax.psum_scatter(grads[3], ('dp', 'fsdp'), scatter_dimension=0, tiled=True)  282 us
    reduce_scatter x2, waiting for transfers between devices, reduce_feed(): lax.psum_scatter(grads[1], ('dp', 'fsdp'), scatter_dimension=0, tiled=True)  282 us
    reduce_scatter x1, waiting for transfers between devices, local(): lax.psum_scatter(conv_grads[1], ('dp', 'fsdp'), scatter_dimension=0, tile...  136 us
    reduce_scatter x1, waiting for transfers between devices, local(): lax.psum_scatter(conv_grads[4], ('dp', 'fsdp'), scatter_dimension=0, tile...  134 us
    reduce_scatter x1, waiting for transfers between devices, local(): lax.psum_scatter(attn_grads[2], ('dp', 'fsdp'), scatter_dimension=0, tile...  134 us
    reduce_scatter x1, waiting for transfers between devices, local(): lax.psum_scatter(attn_grads[1], ('dp', 'fsdp'), scatter_dimension=0, tile...  104 us
    unnamed x2, blocking collectives  79.4 us
  transfers between devices with their start and end apart: 20, of which 13 were waited for; matrix products, arithmetic and copies ran while one was open for 17% of the time, Pallas kernels for 0%

commit v1 on v0

--- a/solution.py
+++ b/solution.py
@@ -1,15 +1,1097 @@
 import jax
 import jax.numpy as jnp
 from jax import lax
+from jax.experimental import pallas as pl
+from jax.experimental.pallas import tpu as pltpu
 from jax.sharding import PartitionSpec as P
 
 D = 512
+FF = 2048
 HEADS = 8
 HEAD_DIM = 64
 BUCKETS = 32
-
-
+L = 512
+TAPS = 32
+PAD = 16
 epsilon = 1e-05
+F32, BF16 = jnp.float32, jnp.bfloat16
+
+SMALL, IN0, OUT0, QKV, ATT, GLU, CONV, IN1, OUT1, ROWS = 0, 16, 80, 144, 192, 208, 240, 256, 320, 384
+(S_FFN, S_FOB, S_ATTN, S_AOB, S_CONV, S_BATCH, S_COB, S_FINAL, S_TAPS, S_ROWS) = (0, 4, 6, 8, 9, 11, 13, 14, 16, 48)
+CHUNK = 64
+
+
+def dot(a, b):
+    return jnp.dot(a, b, preferred_element_type=F32)
+
+
+def dot_nt(a, b):
+    return lax.dot_general(a, b, (((1,), (1,)), ((), ())), preferred_element_type=F32)
+
+
+def dot_tn(a, b):
+    return lax.dot_general(a, b, (((0,), (0,)), ((), ())), preferred_element_type=F32)
+
+
+def chunks(body, carry=None, size=CHUNK):
+    def step(i, carry):
+        return body(pl.ds(pl.multiple_of(i * size, size), size), carry)
+
+    return lax.fori_loop(0, L // size, step, carry)
+
+
+def fold(values):
+    return jnp.sum(values.reshape(values.shape[0] // 8, 8, values.shape[1]), axis=0)
+
+
+def zeros8(width=D):
+    return jnp.zeros((8, width), F32)
+
+
+def standard(values):
+    values = values.astype(F32)
+    center = values - jnp.mean(values, axis=-1, keepdims=True)
+    inverse = lax.rsqrt(jnp.mean(center * center, axis=-1, keepdims=True) + epsilon)
+    return center * inverse, inverse
+
+
+def norm_rows(source, target, small, row):
+    gain, shift = 1.0 + small[row : row + 1, :], small[row + 1 : row + 2, :]
+
+    def body(rows, carry):
+        target[rows, :] = (standard(source[rows, :])[0] * gain + shift).astype(target.dtype)
+        return carry
+
+    chunks(body, 0)
+
+
+def norm_back(source, grad, upstream, result, small, row, grads):
+    gain = 1.0 + small[row : row + 1, :]
+
+    def body(rows, carry):
+        unit, inverse = standard(source[rows, :])
+        given = grad[rows, :]
+        inner = given * gain
+        back = inverse * (
+            inner
+            - jnp.mean(inner, axis=-1, keepdims=True)
+            - unit * jnp.mean(inner * unit, axis=-1, keepdims=True)
+        )
+        result[rows, :] = (upstream[rows, :] + back).astype(result.dtype)
+        return carry[0] + fold(given * unit), carry[1] + fold(given)
+
+    first, second = chunks(body, (zeros8(), zeros8()))
+    grads[row : row + 1, :] = jnp.sum(first, axis=0, keepdims=True)
+    grads[row + 1 : row + 2, :] = jnp.sum(second, axis=0, keepdims=True)
+
+
+def columns(weights, start, block):
+    begin = pl.multiple_of(start + 16 * block, 16)
+    return weights[:, pl.ds(begin, 16), :].reshape(D, D)
+
+
+def lines_of(weights, start, block):
+    return weights[pl.ds(pl.multiple_of(8 * block, 8), 8), start : start + 64, :].reshape(D, D)
+
+
+def feed_forward(source, normed, active, slope, result, hold, weights, small, inner_bias, layer):
+    begin_in, begin_out = ((IN0, OUT0), (IN1, OUT1))[layer]
+    norm_rows(source, normed, small, S_FFN + 2 * layer)
+
+    def block(c, carry):
+        cols = pl.ds(pl.multiple_of(c * D, D), D)
+        hold[...] = dot(normed[...], columns(weights, begin_in, c))
+        bias = inner_bias[layer : layer + 1, cols]
+
+        def body(rows, carry):
+            inner = hold[rows, :] + bias
+            sigma = jax.nn.sigmoid(inner)
+            value = inner * sigma
+            active[rows, cols] = value.astype(BF16)
+            slope[rows, cols] = (sigma + value * (1.0 - sigma)).astype(BF16)
+            return carry
+
+        chunks(body, 0)
+        part = dot(active[:, cols], lines_of(weights, begin_out, c))
+
+        @pl.when(c == 0)
+        def _():
+            result[...] = part
+
+        @pl.when(c > 0)
+        def _():
+            result[...] += part
+
+        return carry
+
+    lax.fori_loop(0, FF // D, block, 0)
+    bias = small[S_FOB + layer : S_FOB + layer + 1, :]
+
+    def body(rows, carry):
+        result[rows, :] = source[rows, :].astype(F32) + 0.5 * (result[rows, :] + bias)
+        return carry
+
+    chunks(body, 0)
+
+
+def feed_backward(
+    upstream, source, normed, active, slope, result, low, low_in, hold, total, weights, small, out, base, grads, inner_grads, layer
+):
+    begin_in, begin_out = ((IN0, OUT0), (IN1, OUT1))[layer]
+
+    def start(rows, carry):
+        half = 0.5 * upstream[rows, :]
+        low[rows, :] = half.astype(BF16)
+        return carry + fold(half)
+
+    grads[S_FOB + layer : S_FOB + layer + 1, :] = jnp.sum(chunks(start, zeros8()), axis=0, keepdims=True)
+
+    def block(c, carry):
+        cols = pl.ds(pl.multiple_of(c * D, D), D)
+        hold[...] = dot_nt(low[...], lines_of(weights, begin_out, c))
+
+        def body(rows, carry):
+            grad = hold[rows, :] * slope[rows, cols].astype(F32)
+            low_in[rows, :] = grad.astype(BF16)
+            return carry + fold(grad)
+
+        inner_grads[layer : layer + 1, cols] = jnp.sum(chunks(body, zeros8()), axis=0, keepdims=True)
+        outer = dot_tn(active[:, cols], low[...]).astype(BF16).reshape(8, 64, D)
+        out[pl.ds(pl.multiple_of(8 * c, 8), 8), begin_out - base : begin_out - base + 64, :] = outer
+        inner = dot_tn(normed[...], low_in[...]).astype(BF16).reshape(32, 16, D)
+        out[:, pl.ds(pl.multiple_of(begin_in - base + 16 * c, 16), 16), :] = inner
+        part = dot_nt(low_in[...], columns(weights, begin_in, c))
+
+        @pl.when(c == 0)
+        def _():
+            total[...] = part
+
+        @pl.when(c > 0)
+        def _():
+            total[...] += part
+
+        return carry
+
+    lax.fori_loop(0, FF // D, block, 0)
+    norm_back(source, total, upstream, result, small, S_FFN + 2 * layer, grads)
+
+
+def bucket_choice(buckets):
+    return (lax.broadcasted_iota(jnp.int32, (BUCKETS, 2 * L), 0) == buckets[...]).astype(F32)
+
+
+def attention_forward(source, normed, mixed, probs, joined, result, lines, hold, weights, small, table, buckets, bounds, marks):
+    norm_rows(source, normed, small, S_ATTN)
+
+    def mix(c, carry):
+        cols = pl.ds(pl.multiple_of(c * D, D), D)
+        mixed[:, cols] = dot(normed[...], columns(weights, QKV, c)).astype(BF16)
+        return carry
+
+    lax.fori_loop(0, 3, mix, 0)
+    lines[...] = dot(table[...].astype(BF16), bucket_choice(buckets).astype(BF16))
+    lane = lax.broadcasted_iota(jnp.int32, (1, 128), 1)
+    size = 128
+
+    def pair(index, carry):
+        begin = pl.multiple_of(128 * index, 128)
+        keys = mixed[:, pl.ds(D + begin, 128)]
+        contents = mixed[:, pl.ds(2 * D + begin, 128)]
+        for block in range(L // size):
+            rows = pl.ds(block * size, size)
+            query = mixed[rows, pl.ds(begin, 128)]
+            same = bounds[PAD + block * size : PAD + (block + 1) * size, 0:1] == marks[...]
+            parts = []
+            for half in range(2):
+                head = 2 * index + half
+                here = (lane // HEAD_DIM) == half
+                raw = dot_nt(jnp.where(here, query, jnp.zeros_like(query)), keys)
+                window = lines[pl.ds(head, 1), 384 - block * size : 1024 - block * size]
+                square = pltpu.roll(jnp.broadcast_to(window, (size, 640)), 513, 1, stride=1, stride_axis=0)
+                scores = jnp.where(same, raw * HEAD_DIM ** (-0.5) + square[:, :L], -1e30)
+                raised = jnp.exp(scores - jnp.max(scores, axis=1, keepdims=True))
+                share = (raised * (1.0 / jnp.sum(raised, axis=1, keepdims=True))).astype(BF16)
+                probs[head, rows, :] = share
+                parts.append(dot(share, contents))
+            joined[rows, pl.ds(begin, 128)] = jnp.where(lane < HEAD_DIM, parts[0], parts[1]).astype(BF16)
+        return carry
+
+    lax.fori_loop(0, HEADS // 2, pair, 0)
+    hold[...] = dot(joined[...], columns(weights, ATT, 0))
+    bias = small[S_AOB : S_AOB + 1, :]
+
+    def body(rows, carry):
+        result[rows, :] = source[rows, :] + hold[rows, :] + bias
+        return carry
+
+    chunks(body, 0)
+
+
+def attention_backward(
+    upstream, source, normed, mixed, probs, joined, result, low, spread, grad_mixed, scaled, hold, total, lines,
+    weights, small, buckets, out, base, grads, table_grad,
+):
+    def start(rows, carry):
+        given = upstream[rows, :]
+        low[rows, :] = given.astype(BF16)
+        return carry + fold(given)
+
+    grads[S_AOB : S_AOB + 1, :] = jnp.sum(chunks(start, zeros8()), axis=0, keepdims=True)
+    out[:, ATT - base : ATT - base + 16, :] = dot_tn(joined[...], low[...]).astype(BF16).reshape(32, 16, D)
+    spread[...] = dot_nt(low[...], columns(weights, ATT, 0)).astype(BF16)
+    lane = lax.broadcasted_iota(jnp.int32, (1, 128), 1)
+    row8 = lax.broadcasted_iota(jnp.int32, (8, 2 * L), 0)
+    size = 128
+
+    def pair(index, carry):
+        begin = pl.multiple_of(128 * index, 128)
+        query = mixed[:, pl.ds(begin, 128)]
+        keys = mixed[:, pl.ds(D + begin, 128)]
+        contents = mixed[:, pl.ds(2 * D + begin, 128)]
+        incoming = spread[:, pl.ds(begin, 128)]
+        parts = []
+        for half in range(2):
+            head = 2 * index + half
+            here = (lane // HEAD_DIM) == half
+            hold[...] = dot_nt(jnp.where(here, incoming, jnp.zeros_like(incoming)), contents)
+            sums = zeros8(2 * L)
+            for block in range(L // size):
+                rows = pl.ds(block * size, size)
+                share = probs[head, rows, :].astype(F32)
+                given = hold[rows, :]
+                slant = share * (given - jnp.sum(given * share, axis=1, keepdims=True))
+                scaled[rows, :] = (slant * HEAD_DIM ** (-0.5)).astype(BF16)
+                part = zeros8(640)
+                for t in range(size // 8):
+                    tile = jnp.concatenate([slant[8 * t : 8 * t + 8], zeros8(128)], axis=1)
+                    part += pltpu.roll(tile, 120 - 8 * t, 1)
+                first = 384 - block * size
+                pieces = [part]
+                if first:
+                    pieces = [zeros8(first)] + pieces
+                if block:
+                    pieces = pieces + [zeros8(block * size)]
+                sums += jnp.concatenate(pieces, axis=1)
+            line = zeros8(2 * L)
+            for r in range(8):
+                line += jnp.where(row8 == r, pltpu.roll(sums, 7 - r, 1), 0.0)
+            lines[pl.ds(head, 1), :] = jnp.sum(line, axis=0, keepdims=True)
+            parts.append((dot(scaled[...], keys), dot_tn(scaled[...], query), dot_tn(probs[head], incoming)))
+        for third in range(3):
+            merged = jnp.where(lane < HEAD_DIM, parts[0][third], parts[1][third])
+            grad_mixed[:, pl.ds(third * D + begin, 128)] = merged.astype(BF16)
+        return carry
+
+    lax.fori_loop(0, HEADS // 2, pair, 0)
+    table_grad[...] = lax.dot_general(
+        lines[...], bucket_choice(buckets), (((1,), (1,)), ((), ())),
+        precision=lax.Precision.HIGHEST, preferred_element_type=F32,
+    )
+
+    def mix(c, carry):
+        cols = pl.ds(pl.multiple_of(c * D, D), D)
+        inner = dot_tn(normed[...], grad_mixed[:, cols]).astype(BF16).reshape(32, 16, D)
+        out[:, pl.ds(pl.multiple_of(QKV - base + 16 * c, 16), 16), :] = inner
+        part = dot_nt(grad_mixed[:, cols], columns(weights, QKV, c))
+
+        @pl.when(c == 0)
+        def _():
+            total[...] = part
+
+        @pl.when(c > 0)
+        def _():
+            total[...] += part
+
+        return carry
+
+    lax.fori_loop(0, 3, mix, 0)
+    norm_back(source, total, upstream, result, small, S_ATTN, grads)
+
+
+def clear_pads(padded):
+    edge = jnp.zeros((4, PAD, 128), F32)
+    padded[:, 0:PAD, :] = edge
+    padded[:, PAD + L : 2 * PAD + L, :] = edge
+
+
+def conv_front(source, normed, sigma, gated, middle, sums, hold, weights, small, gate_bias, bounds):
+    norm_rows(source, normed, small, S_CONV)
+    clear_pads(gated)
+    hold[...] = dot(normed[...], columns(weights, GLU, 1))
+    bias = gate_bias[0:1, D:]
+
+    def gate(rows, carry):
+        sigma[rows, :] = jax.nn.sigmoid(hold[rows, :] + bias)
+        return carry
+
+    chunks(gate, 0)
+    hold[...] = dot(normed[...], columns(weights, GLU, 0))
+    bias = gate_bias[0:1, :D]
+
+    def unit(rows, carry):
+        values = (hold[rows, :] + bias) * sigma[rows, :]
+        for j in range(4):
+            gated[j, pl.ds(rows.start + PAD, CHUNK), :] = values[:, 128 * j : 128 * j + 128]
+        return carry
+
+    chunks(unit, 0)
+    size = 16
+
+    def slide(i, carry):
+        begin = pl.multiple_of(i * size, size)
+        marks = bounds[pl.ds(begin + PAD, size), :]
+        accs = [jnp.zeros((size, 128), F32) for _ in range(4)]
+        for k in range(TAPS):
+            same = bounds[pl.ds(begin + k, size), :] == marks
+            for j in range(4):
+                tap = small[S_TAPS + k : S_TAPS + k + 1, 128 * j : 128 * j + 128]
+                accs[j] += jnp.where(same, gated[j, pl.ds(begin + k, size), :], 0.0) * tap
+        result = []
+        for j in range(4):
+            middle[pl.ds(begin, size), 128 * j : 128 * j + 128] = accs[j]
+            result.append(carry[j] + fold(accs[j]))
+            result.append(carry[4 + j] + fold(accs[j] * accs[j]))
+        return result[0::2] + result[1::2]
+
+    ends = lax.fori_loop(0, L // size, slide, [zeros8(128)] * 8)
+    sums[...] = zeros8()
+    for j in range(4):
+        sums[0:1, 128 * j : 128 * j + 128] = jnp.sum(ends[j], axis=0, keepdims=True)
+        sums[1:2, 128 * j : 128 * j + 128] = jnp.sum(ends[4 + j], axis=0, keepdims=True)
+
+
+def conv_rest(source, middle, sums, unit, active, slope, result, hold, weights, small, frames):
+    center = sums[0:1, :] * (1.0 / frames)
+    inverse = lax.rsqrt(sums[1:2, :] * (1.0 / frames) - center * center + epsilon)
+    gain, shift = 1.0 + small[S_BATCH : S_BATCH + 1, :], small[S_BATCH + 1 : S_BATCH + 2, :]
+
+    def body(rows, carry):
+        values = (middle[rows, :] - center) * inverse
+        unit[rows, :] = values
+        normal = values * gain + shift
+        sigma = jax.nn.sigmoid(normal)
+        value = normal * sigma
+        active[rows, :] = value.astype(BF16)
+        slope[rows, :] = sigma + value * (1.0 - sigma)
+        return carry
+
+    chunks(body, 0)
+    hold[...] = dot(active[...], columns(weights, CONV, 0))
+    bias = small[S_COB : S_COB + 1, :]
+
+    def add(rows, carry):
+        result[rows, :] = source[rows, :] + hold[rows, :] + bias
+        return carry
+
+    chunks(add, 0)
+
+
+def conv_back_rest(upstream, unit, active, slope, grad_normal, low, hold, weights, out, base, grads, sums):
+    def start(rows, carry):
+        given = upstream[rows, :]
+        low[rows, :] = given.astype(BF16)
+        return carry + fold(given)
+
+    grads[S_COB : S_COB + 1, :] = jnp.sum(chunks(start, zeros8()), axis=0, keepdims=True)
+    out[:, CONV - base : CONV - base + 16, :] = dot_tn(active[...], low[...]).astype(BF16).reshape(32, 16, D)
+    hold[...] = dot_nt(low[...], columns(weights, CONV, 0))
+
+    def body(rows, carry):
+        grad = hold[rows, :] * slope[rows, :]
+        grad_normal[rows, :] = grad
+        return carry[0] + fold(grad), carry[1] + fold(grad * unit[rows, :])
+
+    first, second = chunks(body, (zeros8(), zeros8()))
+    sums[...] = zeros8()
+    sums[0:1, :] = jnp.sum(first, axis=0, keepdims=True)
+    sums[1:2, :] = jnp.sum(second, axis=0, keepdims=True)
+
+
+def conv_back_front(
+    upstream, source, normed, sigma, gated, unit, grad_normal, front_sums, sums, result, padded, grad_joined, hold, total, tap_sums,
+    weights, small, bounds, out, base, grads, gate_grads, frames,
+):
+    center = front_sums[0:1, :] * (1.0 / frames)
+    inverse = lax.rsqrt(front_sums[1:2, :] * (1.0 / frames) - center * center + epsilon)
+    gain = 1.0 + small[S_BATCH : S_BATCH + 1, :]
+    mean0, mean1 = gain * sums[0:1, :] * (1.0 / frames), gain * sums[1:2, :] * (1.0 / frames)
+    clear_pads(padded)
+
+    def start(rows, carry):
+        grad = inverse * (gain * grad_normal[rows, :] - mean0 - unit[rows, :] * mean1)
+        for j in range(4):
+            padded[j, pl.ds(rows.start + PAD, CHUNK), :] = grad[:, 128 * j : 128 * j + 128]
+        return carry
+
+    chunks(start, 0)
+    tap_sums[...] = jnp.zeros_like(tap_sums)
+    size = 16
+
+    def slide(i, carry):
+        begin = pl.multiple_of(i * size, size)
+        marks = bounds[pl.ds(begin + PAD, size), :]
+        accs = [jnp.zeros((size, 128), F32) for _ in range(4)]
+        for k in range(TAPS):
+            same = bounds[pl.ds(begin + 2 * PAD - k, size), :] == marks
+            for j in range(4):
+                tap = small[S_TAPS + k : S_TAPS + k + 1, 128 * j : 128 * j + 128]
+                accs[j] += jnp.where(same, padded[j, pl.ds(begin + 2 * PAD - k, size), :], 0.0) * tap
+        for j in range(4):
+            hold[pl.ds(begin, size), 128 * j : 128 * j + 128] = accs[j]
+        grads_here = [padded[j, pl.ds(begin + PAD, size), :] for j in range(4)]
+        for k in range(TAPS):
+            same = bounds[pl.ds(begin + k, size), :] == marks
+            for j in range(4):
+                term = jnp.where(same, gated[j, pl.ds(begin + k, size), :], 0.0) * grads_here[j]
+                tap_sums[k, :, 128 * j : 128 * j + 128] += fold(term)
+        return carry
+
+    lax.fori_loop(0, L // size, slide, 0)
+    grads[S_TAPS : S_TAPS + TAPS, :] = jnp.sum(tap_sums[...], axis=1)
+
+    def split(rows, carry):
+        grad = hold[rows, :]
+        gate = sigma[rows, :]
+        values = jnp.concatenate([gated[j, pl.ds(rows.start + PAD, CHUNK), :] for j in range(4)], axis=1)
+        first = grad * gate
+        second = grad * values * (1.0 - gate)
+        grad_joined[rows, :D] = first.astype(BF16)
+        grad_joined[rows, D : 2 * D] = second.astype(BF16)
+        return carry[0] + fold(first), carry[1] + fold(second)
+
+    first, second = chunks(split, (zeros8(), zeros8()))
+    gate_grads[0:1, :D] = jnp.sum(first, axis=0, keepdims=True)
+    gate_grads[0:1, D:] = jnp.sum(second, axis=0, keepdims=True)
+
+    def mix(c, carry):
+        cols = pl.ds(pl.multiple_of(c * D, D), D)
+        inner = dot_tn(normed[...], grad_joined[:, cols]).astype(BF16).reshape(32, 16, D)
+        out[:, pl.ds(pl.multiple_of(GLU - base + 16 * c, 16), 16), :] = inner
+        part = dot_nt(grad_joined[:, cols], columns(weights, GLU, c))
+
+        @pl.when(c == 0)
+        def _():
+            total[...] = part
+
+        @pl.when(c > 0)
+        def _():
+            total[...] += part
+
+        return carry
+
+    lax.fori_loop(0, 2, mix, 0)
+    norm_back(source, total, upstream, result, small, S_CONV, grads)
+
+
+def kernel_one(
+    x0, bounds, marks, buckets, weights, small, inner_bias, gate_bias, table,
+    x1, x2, normed0, active0, slope0, normed_a, mixed, probs, joined, normed_c, sigma, gated, middle, sums,
+    hold, lines,
+):
+    feed_forward(x0, normed0, active0, slope0, x1, hold, weights, small, inner_bias, 0)
+    attention_forward(x1, normed_a, mixed, probs, joined, x2, lines, hold, weights, small, table, buckets, bounds, marks)
+    conv_front(x2, normed_c, sigma, gated, middle, sums, hold, weights, small, gate_bias, bounds)
+
+
+def kernel_two(
+    frames, cotangent, x2, middle, sums, weights, small, inner_bias,
+    output, unit, grad_normal, g3, out, grads, inner_grads, back_sums,
+    x3, x4, active_c, slope_c, normed, active, slope, low, low_in, hold, total,
+):
+    grads[...] = jnp.zeros_like(grads)
+    inner_grads[...] = jnp.zeros_like(inner_grads)
+    conv_rest(x2, middle, sums, unit, active_c, slope_c, x3, hold, weights, small, frames)
+    feed_forward(x3, normed, active, slope, x4, hold, weights, small, inner_bias, 1)
+    norm_rows(x4, output, small, S_FINAL)
+
+    def zero(rows, carry):
+        hold[rows, :] = jnp.zeros((CHUNK, D), F32)
+        total[rows, :] = cotangent[rows, :].astype(F32)
+        return carry
+
+    chunks(zero, 0)
+    norm_back(x4, total, hold, x4, small, S_FINAL, grads)
+    feed_backward(
+        x4, x3, normed, active, slope, g3, low, low_in, hold, total, weights, small, out, CONV, grads, inner_grads, 1
+    )
+    conv_back_rest(g3, unit, active_c, slope_c, grad_normal, low, hold, weights, out, CONV, grads, back_sums)
+
+
+def kernel_three(
+    frames, x0, bounds, buckets, weights, small,
+    x1, x2, normed0, active0, slope0, normed_a, mixed, probs, joined, normed_c, sigma, gated,
+    unit, grad_normal, g3, front_sums, back_sums, grads_in, inner_in,
+    grad_x, out, grads, inner_grads, gate_grads, table_grad,
+    g2, g1, padded, grad_mixed, scaled, low, low_in, hold, total, tap_sums, lines,
+):
+    grads[...] = grads_in[...]
+    inner_grads[...] = inner_in[...]
+    grads[S_BATCH : S_BATCH + 1, :] = back_sums[1:2, :]
+    grads[S_BATCH + 1 : S_BATCH + 2, :] = back_sums[0:1, :]
+    conv_back_front(
+        g3, x2, normed_c, sigma, gated, unit, grad_normal, front_sums, back_sums, g2, padded, grad_mixed, hold, total, tap_sums,
+        weights, small, bounds, out, IN0, grads, gate_grads, frames,
+    )
+    attention_backward(
+        g2, x1, normed_a, mixed, probs, joined, g1, low, low_in, grad_mixed, scaled, hold, total, lines,
+        weights, small, buckets, out, IN0, grads, table_grad,
+    )
+    feed_backward(
+        g1, x0, normed0, active0, slope0, grad_x, low, low_in, hold, total, weights, small, out, IN0, grads, inner_grads, 0
+    )
+
+
+def shape(dims, kind=F32):
+    return jax.ShapeDtypeStruct(dims, kind)
+
+
+def call(kernel, name, args, outs, scratch):
+    return pl.pallas_call(
+        kernel,
+        out_shape=outs,
+        in_specs=[pl.BlockSpec(memory_space=pltpu.VMEM)] * len(args),
+        out_specs=[pl.BlockSpec(memory_space=pltpu.VMEM)] * len(outs),
+        scratch_shapes=scratch,
+        compiler_params=pltpu.CompilerParams(vmem_limit_bytes=60 * 1024 * 1024),
+        name=name,
+    )(*args)
+
+
+def compute(x0, segments, buckets, cotangent, weights, small, inner_bias, gate_bias, table, total_of, frames):
+    wide, low = shape((L, D)), shape((L, D), BF16)
+    big, pads = shape((L, FF), BF16), shape((4, L + 2 * PAD, 128))
+    vwide, vlow, vbig = pltpu.VMEM((L, D), F32), pltpu.VMEM((L, D), BF16), pltpu.VMEM((L, FF), BF16)
+    bounds = jnp.broadcast_to(jnp.pad(segments, (PAD, PAD), constant_values=-1)[:, None], (L + 2 * PAD, 128))
+    marks = segments[None, :]
+    choice = jnp.pad(buckets, (0, 1), constant_values=-1)[None, :]
+    x1, x2, normed0, active0, slope0, normed_a, mixed, probs, joined, normed_c, sigma, gated, middle, sums = call(
+        kernel_one, "front", (x0, bounds, marks, choice, weights, small, inner_bias, gate_bias, table),
+        [wide, wide, low, big, big, low, shape((L, 3 * D), BF16), shape((HEADS, L, L), BF16), low, low, wide, pads, wide, shape((8, D))],
+        [vwide, pltpu.VMEM((8, 2 * L), F32)],
+    )
+    sums = total_of(sums)
+    output, unit, grad_normal, g3, late, grads, inner_grads, back = call(
+        lambda *refs: kernel_two(frames, *refs), "turn", (cotangent, x2, middle, sums, weights, small, inner_bias),
+        [low, wide, wide, wide, shape((32, ROWS - CONV, D), BF16), shape((S_ROWS, D)), shape((2, FF)), shape((8, D))],
+        [vwide, vwide, vlow, vwide, vlow, vbig, vbig, vlow, vlow, vwide, vwide],
+    )
+    back = total_of(back)
+    grad_x, early, grads, inner_grads, gate_grads, table_grad = call(
+        lambda *refs: kernel_three(frames, *refs), "back",
+        (x0, bounds, choice, weights, small, x1, x2, normed0, active0, slope0, normed_a, mixed, probs, joined, normed_c, sigma, gated,
+         unit, grad_normal, g3, sums, back, grads, inner_grads),
+        [wide, shape((32, CONV - IN0, D), BF16), shape((S_ROWS, D)), shape((2, FF)), shape((1, 2 * D)), shape((HEADS, BUCKETS))],
+        [vwide, vwide, pltpu.VMEM((4, L + 2 * PAD, 128), F32), pltpu.VMEM((L, 3 * D), BF16), vlow, vlow, vlow, vwide, vwide,
+         pltpu.VMEM((TAPS, 8, D), F32), pltpu.VMEM((8, 2 * L), F32)],
+    )
+    return output, grad_x, early, late, grads, inner_grads, gate_grads, table_grad
+
+
+MESH = pl.DeviceIdType.MESH
+
+
+class Place:
+    def __init__(self):
+        self.width = lax.axis_size("fsdp")
+        self.chips = self.width // 2
+        plane, inner = lax.axis_index("dp"), lax.axis_index("fsdp")
+        self.y, self.x = plane // 2, plane % 2
+        self.z, self.core = inner // 2, inner % 2
+        self.me = self.slot(self.y, self.x, self.z, self.core)
+
+    def slot(self, y, x, z, core):
+        return (y * 2 + x) * self.width + z * 2 + core
+
+    def device(self, y, x, z, core):
+        return (y * 2 + x, z * 2 + core)
+
+    def twin(self):
+        return self.device(self.y, self.x, self.z, 1 - self.core)
+
+    def over_x(self):
+        return self.device(self.y, 1 - self.x, self.z, self.core)
+
+    def over_y(self):
+        return self.device(1 - self.y, self.x, self.z, self.core)
+
+    def along_z(self, step):
+        return self.device(self.y, self.x, self.z + step, self.core)
+
+    def greet(self):
+        barrier = pltpu.get_barrier_semaphore()
+        for near in (self.twin(), self.over_x(), self.over_y()):
+            pl.semaphore_signal(barrier, inc=1, device_id=near, device_id_type=MESH)
+
+        @pl.when(self.z > 0)
+        def _():
+            pl.semaphore_signal(barrier, inc=1, device_id=self.along_z(-1), device_id_type=MESH)
+
+        @pl.when(self.z < self.chips - 1)
+        def _():
+            pl.semaphore_signal(barrier, inc=1, device_id=self.along_z(1), device_id_type=MESH)
+
+        ends = jnp.where(self.z > 0, 1, 0) + jnp.where(self.z < self.chips - 1, 1, 0)
+        pl.semaphore_wait(barrier, 3 + ends)
+
+
+def when(condition, action):
+    if condition is True:
+        action()
+    else:
+        pl.when(condition)(action)
+
+
+def gather_kernel(split, own, out, sends, receives, local_sem):
+    place = Place()
+    rows = own.shape[0]
+    y, x, z, core, chips = place.y, place.x, place.z, place.core, place.chips
+    halves = ((0, split), (split, rows - split))
+    place.greet()
+    keep = pltpu.make_async_copy(own, out.at[place.me], local_sem)
+    keep.start()
+    sent = []
+
+    def piece(slot, half, mine=False):
+        start, size = halves[half]
+        if mine:
+            return own.at[pl.ds(start, size)]
+        return out.at[slot, pl.ds(start, size)]
+
+    def send(slot, half, device, condition=True, mine=False):
+        start, size = halves[half]
+        copy = pltpu.make_async_remote_copy(
+            src_ref=piece(slot, half, mine),
+            dst_ref=out.at[slot, pl.ds(start, size)],
+            send_sem=sends.at[len(sent)],
+            recv_sem=receives.at[slot, half],
+            device_id=device,
+            device_id_type=MESH,
+        )
+        when(condition, copy.start)
+        sent.append((condition, copy))
+
+    def arrive(slot, half, condition=True):
+        start, size = halves[half]
+        block = out.at[slot, pl.ds(start, size)]
+        copy = pltpu.make_async_remote_copy(
+            src_ref=block, dst_ref=block, send_sem=local_sem, recv_sem=receives.at[slot, half],
+            device_id=place.twin(), device_id_type=MESH,
+        )
+        when(condition, copy.wait_recv)
+
+    def across(zz, condition, mine):
+        slot = place.slot(y, x, zz, core)
+        send(slot, 0, place.over_x(), condition, mine)
+        send(slot, 1, place.over_y(), condition, mine)
+        send(slot, 0, place.over_y(), condition, mine)
+        send(slot, 1, place.over_x(), condition, mine)
+
+    def turn(zz, condition):
+        first = place.slot(y, 1 - x, zz, core)
+        arrive(first, 0, condition)
+        send(first, 0, place.over_y(), condition)
+        second = place.slot(1 - y, x, zz, core)
+        arrive(second, 1, condition)
+        send(second, 1, place.over_x(), condition)
+        for half in range(2):
+            send((first, second)[half], half, place.twin(), condition)
+
+    def both(slot, condition=True, mine=False):
+        for half in range(2):
+            send(slot, half, place.twin(), condition, mine)
+
+    steps = [(0, True)]
+    for k in range(1, chips):
+        steps += [(-k, z - k >= 0), (k, z + k < chips)]
+    for offset, there in steps:
+        zz = z + offset
+        slot = place.slot(y, x, zz, core)
+        if offset:
+            for half in range(2):
+                arrive(slot, half, there)
+        for half in range(2):
+            if offset <= 0 and -offset < chips - 1:
+                ok = z < chips - 1 if offset == 0 else jnp.logical_and(there, z < chips - 1)
+                send(slot, half, place.along_z(1), ok, offset == 0)
+            if offset >= 0 and offset < chips - 1:
+                ok = z > 0 if offset == 0 else jnp.logical_and(there, z > 0)
+                send(slot, half, place.along_z(-1), ok, offset == 0)
+        across(zz, there, offset == 0)
+        both(slot, there, offset == 0)
+        turn(zz, there)
+    for offset, there in steps:
+        zz = z + offset
+        for first, second in (
+            (place.slot(1 - y, x, zz, core), place.slot(y, 1 - x, zz, core)),
+            (place.slot(1 - y, 1 - x, zz, core), place.slot(1 - y, 1 - x, zz, core)),
+        ):
+            arrive(first, 0, there)
+            send(first, 0, place.twin(), there)
+            arrive(second, 1, there)
+            send(second, 1, place.twin(), there)
+    for yy in range(2):
+        for xx in range(2):
+            for zz in range(chips):
+                for half in range(2):
+                    arrive(place.slot(yy, xx, zz, 1 - core), half)
+    for condition, copy in sent:
+        when(condition, copy.wait_send)
+    keep.wait()
+
+
+def gather_all(own, split):
+    devices = lax.axis_size(("dp", "fsdp"))
+    rows, lanes = own.shape
+    return pl.pallas_call(
+        lambda *refs: gather_kernel(split, *refs),
+        out_shape=jax.ShapeDtypeStruct((devices, rows, lanes), own.dtype),
+        in_specs=[pl.BlockSpec(memory_space=pl.ANY)],
+        out_specs=pl.BlockSpec(memory_space=pl.ANY),
+        scratch_shapes=[
+            pltpu.SemaphoreType.DMA((16 * devices,)),
+            pltpu.SemaphoreType.DMA((devices, 2)),
+            pltpu.SemaphoreType.DMA,
+        ],
+        compiler_params=pltpu.CompilerParams(collective_id=0, has_side_effects=True),
+        name="gather_all",
+    )(own)
+
+
+def total_kernel(own, out, near, far, part, near_send, near_recv, far_send, far_recv):
+    place = Place()
+    planes = lax.axis_size("dp")
+    plane = lax.axis_index("dp")
+    z, core, chips = place.z, place.core, place.chips
+    barrier = pltpu.get_barrier_semaphore()
+    group = [(step, flip) for step in range(planes) for flip in range(2) if step or flip]
+
+    def member(step, flip):
+        return (lax.rem(plane + step, planes), 2 * z + lax.rem(core + flip, 2))
+
+    def rank(step, flip):
+        return lax.rem(plane + step, planes) * 2 + lax.rem(core + flip, 2)
+
+    def along(step):
+        return (plane, 2 * lax.rem(z + step, chips) + core)
+
+    for step, flip in group:
+        pl.semaphore_signal(barrier, inc=1, device_id=member(step, flip), device_id_type=MESH)
+    for step in range(1, chips):
+        pl.semaphore_signal(barrier, inc=1, device_id=along(step), device_id_type=MESH)
+    pl.semaphore_wait(barrier, len(group) + chips - 1)
+    me = rank(0, 0)
+    copies = []
+    for i, (step, flip) in enumerate(group):
+        copy = pltpu.make_async_remote_copy(
+            src_ref=own, dst_ref=near.at[me], send_sem=near_send.at[i], recv_sem=near_recv.at[me],
+            device_id=member(step, flip), device_id_type=MESH,
+        )
+        copy.start()
+        copies.append(copy)
+    near[me] = own[...]
+    for step, flip in group:
+        pltpu.make_async_remote_copy(
+            src_ref=own, dst_ref=near.at[rank(step, flip)], send_sem=near_send.at[0], recv_sem=near_recv.at[rank(step, flip)],
+            device_id=member(step, flip), device_id_type=MESH,
+        ).wait_recv()
+    value = near[0]
+    for i in range(1, 2 * planes):
+        value = value + near[i]
+    part[...] = value
+    for step in range(1, chips):
+        copy = pltpu.make_async_remote_copy(
+            src_ref=part, dst_ref=far.at[z], send_sem=far_send.at[step], recv_sem=far_recv.at[z],
+            device_id=along(step), device_id_type=MESH,
+        )
+        copy.start()
+        copies.append(copy)
+    far[z] = part[...]
+    for step in range(1, chips):
+        other = lax.rem(z + step, chips)
+        pltpu.make_async_remote_copy(
+            src_ref=part, dst_ref=far.at[other], send_sem=far_send.at[0], recv_sem=far_recv.at[other],
+            device_id=along(step), device_id_type=MESH,
+        ).wait_recv()
+    value = far[0]
+    for i in range(1, chips):
+        value = value + far[i]
+    out[...] = value
+    for copy in copies:
+        copy.wait_send()
+
+
+def total_of(own, identity):
+    planes, chips = lax.axis_size("dp"), lax.axis_size("fsdp") // 2
+    block = own.shape
+    return pl.pallas_call(
+        total_kernel,
+        out_shape=jax.ShapeDtypeStruct(block, own.dtype),
+        in_specs=[pl.BlockSpec(memory_space=pltpu.VMEM)],
+        out_specs=pl.BlockSpec(memory_space=pltpu.VMEM),
+        scratch_shapes=[
+            pltpu.VMEM((2 * planes,) + block, own.dtype),
+            pltpu.VMEM((chips,) + block, own.dtype),
+            pltpu.VMEM(block, own.dtype),
+            pltpu.SemaphoreType.DMA((2 * planes,)),
+            pltpu.SemaphoreType.DMA((2 * planes,)),
+            pltpu.SemaphoreType.DMA((chips,)),
+            pltpu.SemaphoreType.DMA((chips,)),
+        ],
+        compiler_params=pltpu.CompilerParams(collective_id=identity, has_side_effects=True),
+        name="total_of",
+    )(own)
+
+
+def reduce_kernel(split, early, late, small, out, small_out, data, twins, firsts, seconds, rights, lefts, edges, sends, receives, local_sem):
+    place = Place()
+    y, x, z, core, chips = place.y, place.x, place.z, place.core, place.chips
+    rows = data.shape[1]
+    cut = early.shape[1]
+    loads = [
+        pltpu.make_async_copy(early, data.at[:, pl.ds(0, cut)], local_sem.at[0]),
+        pltpu.make_async_copy(late, data.at[:, pl.ds(cut, rows - cut)], local_sem.at[1]),
+        pltpu.make_async_copy(small, edges, local_sem.at[2]),
+    ]
+    for load in loads:
+        load.start()
+    place.greet()
+    for load in loads:
+        load.wait()
+    parts = (0, 1, 2)
+    kinds = ((data, 0, split), (data, split, rows - split), (edges, 0, small.shape[1]))
+    sent = []
+
+    def mine(part, slot):
+        ref, begin, size = kinds[part]
+        return ref.at[slot, pl.ds(begin, size)]
+
+    def copy_of(part, slot, landing, stage, index, device, number):
+        return pltpu.make_async_remote_copy(
+            src_ref=mine(part, slot), dst_ref=landing, send_sem=sends.at[number],
+            recv_sem=receives.at[part, stage, index], device_id=device, device_id_type=MESH,
+        )
+
+    def send(part, slot, landing, stage, index, device, condition=True):
+        copy = copy_of(part, slot, landing, stage, index, device, len(sent))
+        when(condition, copy.start)
+        sent.append((condition, copy))
+
+    def add(part, slot, landing, stage, index, condition=True):
+        ref, begin, size = kinds[part]
+
+        def act():
+            copy_of(part, slot, landing, stage, index, place.twin(), 0).wait_recv()
+            if part == 2:
+                ref[slot] = ref[slot] + landing[...]
+                return
+            piece = 16
+
+            def step(i, carry):
+                at = pl.multiple_of(i * piece, piece)
+                here = pl.ds(begin + at, piece)
+                ref[slot, here, :] = ref[slot, here, :] + landing[pl.ds(at, piece), :]
+                return carry
+
+            lax.fori_loop(0, size // piece, step, 0)
+
+        when(condition, act)
+
+    def first_side(part, flip):
+        return 1 - flip if flip is not None else None
+
+    def at(part, first, second, zz, core_of):
+        if part == 1:
+            yy, xx = (y if second == 0 else 1 - y), (x if first == 0 else 1 - x)
+        else:
+            yy, xx = (y if first == 0 else 1 - y), (x if second == 0 else 1 - x)
+        return place.slot(yy, xx, zz, core_of)
+
+    def index(part, first, second, zz):
+        if part == 1:
+            yy, xx = (y if second == 0 else 1 - y), (x if first == 0 else 1 - x)
+        else:
+            yy, xx = (y if first == 0 else 1 - y), (x if second == 0 else 1 - x)
+        return (yy * 2 + xx) * chips + zz
+
+    def second_index(part, second, zz):
+        along = (y if second == 0 else 1 - y) if part == 1 else (x if second == 0 else 1 - x)
+        return along * chips + zz
+
+    def over(part, axis):
+        return place.over_x() if (part == 1) == (axis == 0) else place.over_y()
+
+    order = [(1, 1), (1, 0), (0, 1), (0, 0)]
+    for first, second in order:
+        for zz in range(chips):
+            for part in parts:
+                where = index(part, first, second, zz)
+                send(part, at(part, first, second, zz, 1 - core), twins[part].at[where], 0, where, place.twin())
+    for second in (1, 0):
+        for zz in range(chips):
+            for part in parts:
+                slot, where = at(part, 1, second, zz, core), index(part, 1, second, zz)
+                add(part, slot, twins[part].at[where], 0, where)
+                where = second_index(part, second, zz)
+                send(part, slot, firsts[part].at[where], 1, where, over(part, 0))
+    for zz in range(chips):
+        for part in parts:
+            slot, where = at(part, 0, 1, zz, core), index(part, 0, 1, zz)
+            add(part, slot, twins[part].at[where], 0, where)
+            where = second_index(part, 1, zz)
+            add(part, slot, firsts[part].at[where], 1, where)
+            send(part, slot, seconds[part].at[zz], 2, zz, over(part, 1))
+    for zz in range(chips):
+        for part in parts:
+            slot, where = at(part, 0, 0, zz, core), index(part, 0, 0, zz)
+            add(part, slot, twins[part].at[where], 0, where)
+            where = second_index(part, 0, zz)
+            add(part, slot, firsts[part].at[where], 1, where)
+    for zz in range(chips):
+        for part in parts:
+            add(part, at(part, 0, 0, zz, core), seconds[part].at[zz], 2, zz)
+    for k in range(chips - 1, 0, -1):
+        for part in parts:
+            slot = at(part, 0, 0, k, core)
+            below = z < k
+            add(part, slot, rights[part].at[k], 3, k, jnp.logical_and(below, z > 0))
+            send(part, slot, rights[part].at[k], 3, k, place.along_z(1), below)
+            goal = chips - 1 - k
+            slot = at(part, 0, 0, goal, core)
+            above = z > goal
+            add(part, slot, lefts[part].at[goal], 4, goal, jnp.logical_and(above, z < chips - 1))
+            send(part, slot, lefts[part].at[goal], 4, goal, place.along_z(-1), above)
+    for part in parts:
+        add(part, place.me, rights[part].at[z], 3, z, z > 0)
+        add(part, place.me, lefts[part].at[z], 4, z, z < chips - 1)
+
+    def finish(i, carry):
+        here = pl.ds(pl.multiple_of(i * 16, 16), 16)
+        out[here, :] = data[place.me, here, :].astype(jnp.float32)
+        return carry
+
+    lax.fori_loop(0, rows // 16, finish, 0)
+    small_out[...] = edges[place.me]
+    for condition, copy in sent:
+        when(condition, copy.wait_send)
+
+
+def reduce_all(early, late, small, split):
+    devices = lax.axis_size(("dp", "fsdp"))
+    chips = lax.axis_size("fsdp") // 2
+    rows = early.shape[1] + late.shape[1]
+    lanes = early.shape[2]
+
+    def buffers(count):
+        return [
+            pltpu.VMEM((count, split, lanes), early.dtype),
+            pltpu.VMEM((count, rows - split, lanes), early.dtype),
+            pltpu.VMEM((count,) + small.shape[1:], small.dtype),
+        ]
+
+    return pl.pallas_call(
+        lambda *refs: reduce_kernel(split, *refs),
+        out_shape=[jax.ShapeDtypeStruct((rows, lanes), jnp.float32), jax.ShapeDtypeStruct(small.shape[1:], small.dtype)],
+        in_specs=[pl.BlockSpec(memory_space=pl.ANY)] * 3,
+        out_specs=[pl.BlockSpec(memory_space=pltpu.VMEM)] * 2,
+        scratch_shapes=[
+            pltpu.VMEM((devices, rows, lanes), early.dtype),
+            buffers(4 * chips), buffers(2 * chips), buffers(chips), buffers(chips), buffers(chips),
+            pltpu.VMEM(small.shape, small.dtype),
+            pltpu.SemaphoreType.DMA((160,)),
+            pltpu.SemaphoreType.DMA((3, 5, 4 * chips)),
+            pltpu.SemaphoreType.DMA((3,)),
+        ],
+        compiler_params=pltpu.CompilerParams(collective_id=3, has_side_effects=True, vmem_limit_bytes=60 * 1024 * 1024),
+        name="reduce_all",
+    )(early, late, small)
+
+
+SMALL_SIZE = 1024
+
+
+def pack_rows(weight):
+    rows = weight.shape[0]
+    return weight.reshape(rows, -1, D).transpose(1, 0, 2).reshape(-1, D)
+
+
+def unpack_rows(rows, count):
+    return rows.reshape(count, -1, D).transpose(1, 0, 2).reshape(-1, count * D)
+
+
+def local(
+    inputs, segments, buckets, cotangent, ffn_norm, ffn_in, ffn_in_bias, ffn_out, ffn_out_bias, attn_norm, qkv_weight,
+    attn_out, attn_out_bias, rel_table, conv_norm, glu_weight, glu_bias, depth_kernel, batch_norm, conv_out, conv_out_bias,
+    final_norm,
+):
+    devices = lax.axis_size(("dp", "fsdp"))
+    width = D // devices
+    thin = [
+        ffn_norm.reshape(4, width), ffn_out_bias, attn_norm, attn_out_bias[None], conv_norm, batch_norm,
+        conv_out_bias[None], final_norm, depth_kernel,
+    ]
+    tiny = jnp.concatenate([item.reshape(-1) for item in thin + [ffn_in_bias, glu_bias, rel_table]])
+    tiny = jnp.pad(tiny, (0, 16 * D - tiny.shape[0])).reshape(16, D)
+    own = jnp.concatenate(
+        [
+            tiny, pack_rows(ffn_in[0]), ffn_out[0], pack_rows(qkv_weight), attn_out, pack_rows(glu_weight), conv_out,
+            pack_rows(ffn_in[1]), ffn_out[1],
+        ]
+    )
+    weights = gather_all(own, ROWS // 2)
+    flat = weights[:, 0:2, :].reshape(devices, 2 * D)
+    small = flat[:, : S_ROWS * width].reshape(devices, S_ROWS, width).transpose(1, 0, 2).reshape(S_ROWS, D).astype(F32)
+    at = S_ROWS * width
+    inner_bias = flat[:, at : at + 8 * width].reshape(devices, 2, -1).transpose(1, 0, 2).reshape(2, FF).astype(F32)
+    at += 8 * width
+    gate_bias = flat[:, at : at + 2 * width].reshape(1, 2 * D).astype(F32)
+    at += 2 * width
+    table = flat[:, at : at + width // 2].reshape(HEADS, BUCKETS).astype(F32)
+    numbers = [1, 2]
+    output, grad_x, early, late, grads, inner_grads, gate_grads, table_grad = compute(
+        inputs[0], segments[0], buckets, cotangent[0], weights, small, inner_bias, gate_bias, table,
+        lambda item: total_of(item, numbers.pop(0)), L * devices,
+    )
+    tiny_grads = jnp.concatenate(
+        [
+            grads.reshape(S_ROWS, devices, width).transpose(1, 0, 2).reshape(devices, -1),
+            inner_grads.reshape(2, devices, -1).transpose(1, 0, 2).reshape(devices, -1),
+            gate_grads.reshape(devices, -1),
+            table_grad.reshape(devices, -1),
+        ],
+        axis=1,
+    )
+    tiny_grads = jnp.pad(tiny_grads, ((0, 0), (0, SMALL_SIZE - tiny_grads.shape[1]))).reshape(devices, 8, 128)
+    shard, tiny = reduce_all(early, late, tiny_grads, 176)
+    tiny = tiny.reshape(-1)
+    own_rows = tiny[: S_ROWS * width].reshape(S_ROWS, width)
+    at = S_ROWS * width
+    cut = lambda begin, size: shard[begin - IN0 : begin - IN0 + size]
+    me = lax.axis_index(("dp", "fsdp"))
+    batch = lax.dynamic_slice_in_dim(grads[S_BATCH : S_BATCH + 2], me * width, width, 1)
+    return (
+        output[None],
+        grad_x[None],
+        own_rows[0:4].reshape(2, 2, width),
+        jnp.stack([unpack_rows(cut(IN0, 64), 4), unpack_rows(cut(IN1, 64), 4)]),
+        tiny[at : at + 8 * width].reshape(2, -1),
+        jnp.stack([cut(OUT0, 64), cut(OUT1, 64)]),
+        own_rows[S_FOB : S_FOB + 2],
+        own_rows[S_ATTN : S_ATTN + 2],
+        unpack_rows(cut(QKV, 48), 3),
+        cut(ATT, 16),
+        own_rows[S_AOB],
+        tiny[at + 10 * width : at + 10 * width + width // 2],
+        own_rows[S_CONV : S_CONV + 2],
+        unpack_rows(cut(GLU, 32), 2),
+        tiny[at + 8 * width : at + 10 * width],
+        own_rows[S_TAPS : S_TAPS + TAPS],
+        batch,
+        cut(CONV, 16),
+        own_rows[S_COB],
+        own_rows[S_FINAL : S_FINAL + 2],
+    )
+
+
 highest = lax.Precision.HIGHEST
 
 
@@ -40,7 +1122,7 @@
     )
 
 
-def fetch_feed(norms, inner_weight, inner_bias, outer_weight, outer_bias, layer):
+def plain_fetch_feed(norms, inner_weight, inner_bias, outer_weight, outer_bias, layer):
     return (
         lax.all_gather(norms[layer], ("dp", "fsdp"), axis=1, tiled=True),
         lax.all_gather(inner_weight[layer], ("dp", "fsdp"), axis=0, tiled=True),
@@ -50,7 +1132,7 @@
     )
 
 
-def reduce_feed(grads):
+def plain_reduce_feed(grads):
     return (
         lax.psum_scatter(grads[0], ("dp", "fsdp"), scatter_dimension=1, tiled=True),
         lax.psum_scatter(grads[1], ("dp", "fsdp"), scatter_dimension=0, tiled=True),
@@ -85,7 +1167,7 @@
     )
 
 
-def feed_forward(values, weights):
+def plain_feed_forward(values, weights):
     norm, weight_in, bias_in, weight_out, bias_out = weights
     normed, norm_back = jax.vjp(layer_norm, values, norm.astype(jnp.float32))
     normed_low = normed.astype(jnp.bfloat16)
@@ -95,7 +1177,7 @@
     return (result, (normed_low, inner, active, norm_back))
 
 
-def feed_backward(upstream, weights, saved):
+def plain_feed_backward(upstream, weights, saved):
     norm, weight_in, bias_in, weight_out, bias_out = weights
     normed_low, inner, active, norm_back = saved
     branch = 0.5 * upstream
@@ -140,7 +1222,7 @@
     return jnp.where(same, raw * HEAD_DIM ** (-0.5) + bias_square(line, query.shape[0]), -1e30)
 
 
-def attention_forward(values, weights, marks, buckets):
+def plain_attention_forward(values, weights, marks, buckets):
     norm, mixer, weight_out, bias_out, table = weights
     length = values.shape[0]
     normed, norm_back = jax.vjp(layer_norm, values, norm.astype(jnp.float32))
@@ -169,7 +1251,7 @@
     return (result, (normed_low, mixed, lines, choose, same, joined, logsum, norm_back))
 
 
-def attention_backward(upstream, weights, saved):
+def plain_attention_backward(upstream, weights, saved):
     norm, mixer, weight_out, bias_out, table = weights
     normed_low, mixed, lines, choose, same, joined, logsum, norm_back = saved
     length = upstream.shape[0]
@@ -215,7 +1297,7 @@
     return joined[:, :width] * jax.nn.sigmoid(joined[:, width:])
 
 
-def depthwise(gated, kernel, marks):
+def plain_depthwise(gated, kernel, marks):
     length = gated.shape[0]
     half = kernel.shape[0] // 2
     padded = jnp.pad(gated, ((half, half), (0, 0)))
@@ -227,14 +1309,14 @@
     return total
 
 
-def conv_forward(values, weights, marks, frames):
+def plain_conv_forward(values, weights, marks, frames):
     norm, weight_glu, bias_glu, kernel, batch, weight_out, bias_out, final = weights
     normed, norm_back = jax.vjp(layer_norm, values, norm.astype(jnp.float32))
     normed_low = normed.astype(jnp.bfloat16)
     joined = product(normed_low, weight_glu) + bias_glu.astype(jnp.float32)
     gated, gate_back = jax.vjp(gate_unit, joined)
     middle, depth_back = jax.vjp(
-        lambda inner, taps: depthwise(inner, taps, marks), gated, kernel.astype(jnp.float32)
+        lambda inner, taps: plain_depthwise(inner, taps, marks), gated, kernel.astype(jnp.float32)
     )
     sums = lax.psum((jnp.sum(middle, axis=0), jnp.sum(middle * middle, axis=0)), ("dp", "fsdp"))
     center = sums[0] / frames
@@ -250,7 +1332,7 @@
     )
 
 
-def conv_backward(upstream, weights, saved, frames):
+def plain_conv_backward(upstream, weights, saved, frames):
     norm, weight_glu, bias_glu, kernel, batch, weight_out, bias_out, final = weights
     normed_low, gate_back, depth_back, inverse, gain, unit, normal, active, norm_back = saved
     upstream_low = upstream.astype(jnp.bfloat16)
@@ -282,7 +1364,7 @@
     )
 
 
-def local(
+def plain(
     inputs,
     segments,
     buckets,
@@ -310,10 +1392,10 @@
     marks = segments[0]
     devices = lax.axis_size(("dp", "fsdp"))
     frames = values.shape[0] * devices
-    feed_first = fetch_feed(ffn_norm, ffn_in, ffn_in_bias, ffn_out, ffn_out_bias, 0)
-    first, first_saved = feed_forward(values, feed_first)
+    feed_first = plain_fetch_feed(ffn_norm, ffn_in, ffn_in_bias, ffn_out, ffn_out_bias, 0)
+    first, first_saved = plain_feed_forward(values, feed_first)
     attn_weights = fetch_attention(attn_norm, qkv_weight, attn_out, attn_out_bias, rel_table)
-    second, attn_saved = attention_forward(first, attn_weights, marks, buckets)
+    second, attn_saved = plain_attention_forward(first, attn_weights, marks, buckets)
     conv_weights = fetch_conv(
         conv_norm,
         glu_weight,
@@ -324,13 +1406,13 @@
         conv_out_bias,
         final_norm,
     )
-    third, conv_saved = conv_forward(second, conv_weights, marks, frames)
-    feed_second = fetch_feed(ffn_norm, ffn_in, ffn_in_bias, ffn_out, ffn_out_bias, 1)
-    fourth, second_saved = feed_forward(third, feed_second)
+    third, conv_saved = plain_conv_forward(second, conv_weights, marks, frames)
+    feed_second = plain_fetch_feed(ffn_norm, ffn_in, ffn_in_bias, ffn_out, ffn_out_bias, 1)
+    fourth, second_saved = plain_feed_forward(third, feed_second)
     result, final_back = jax.vjp(layer_norm, fourth, conv_weights[7].astype(jnp.float32))
     grad_fourth, grad_final = final_back(cotangent[0].astype(jnp.float32))
-    second_back = fetch_feed(ffn_norm, ffn_in, ffn_in_bias, ffn_out, ffn_out_bias, 1)
-    grad_third, second_grads = feed_backward(grad_fourth, second_back, second_saved)
+    second_back = plain_fetch_feed(ffn_norm, ffn_in, ffn_in_bias, ffn_out, ffn_out_bias, 1)
+    grad_third, second_grads = plain_feed_backward(grad_fourth, second_back, second_saved)
     conv_back = fetch_conv(
         conv_norm,
         glu_weight,
@@ -341,13 +1423,13 @@
         conv_out_bias,
         final_norm,
     )
-    grad_second, conv_grads, grad_batch = conv_backward(grad_third, conv_back, conv_saved, frames)
+    grad_second, conv_grads, grad_batch = plain_conv_backward(grad_third, conv_back, conv_saved, frames)
     attn_back = fetch_attention(attn_norm, qkv_weight, attn_out, attn_out_bias, rel_table)
-    grad_first, attn_grads = attention_backward(grad_second, attn_back, attn_saved)
-    first_back = fetch_feed(ffn_norm, ffn_in, ffn_in_bias, ffn_out, ffn_out_bias, 0)
-    grad_start, first_grads = feed_backward(grad_first, first_back, first_saved)
-    first_shards = reduce_feed(first_grads)
-    second_shards = reduce_feed(second_grads)
+    grad_first, attn_grads = plain_attention_backward(grad_second, attn_back, attn_saved)
+    first_back = plain_fetch_feed(ffn_norm, ffn_in, ffn_in_bias, ffn_out, ffn_out_bias, 0)
+    grad_start, first_grads = plain_feed_backward(grad_first, first_back, first_saved)
+    first_shards = plain_reduce_feed(first_grads)
+    second_shards = plain_reduce_feed(second_grads)
     attn_shards = (
         lax.psum_scatter(attn_grads[0], ("dp", "fsdp"), scatter_dimension=1, tiled=True),
         lax.psum_scatter(attn_grads[1], ("dp", "fsdp"), scatter_dimension=0, tiled=True),
@@ -439,4 +1521,5 @@
         P(("dp", "fsdp")),
         P(None, ("dp", "fsdp")),
     )
-    return jax.shard_map(local, mesh=mesh, in_specs=in_specs, out_specs=out_specs, check_vma=False)
+    fast = mesh.shape["dp"] == 4 and mesh.shape["fsdp"] == 8
+    return jax.shard_map(local if fast else plain, mesh=mesh, in_specs=in_specs, out_specs=out_specs, check_vma=False)

time: 2700 us -> 354 us (0.13)
  waiting for transfers between devices: 1630 us -> 0 us
  blocking collectives: 515 us -> 0 us
  Pallas kernels: 0 us -> 310 us
  local copies, waits for them, and re-layouts: 280 us -> 37.3 us
  matrix products: 156 us -> 0 us
  other arithmetic: 88.9 us -> 2.96 us
    reduce_scatter x8 -> x0, waiting for transfers between devices: 1070 us -> none  [the longest x2 282 us: reduce_feed(): lax.psum_scatter(grads[3], ('dp', 'fsdp'), scatter_dimension=0, tiled=True)]
    unnamed x26 -> x0, waiting for transfers between devices: 560 us -> none
    all_gather x9 -> x0, blocking collectives: 356 us -> none  [the longest x2 77.5 us: fetch_feed(): lax.all_gather(norms[layer], ('dp', 'fsdp'), axis=1, tiled=True)]
    pallas_call x0 -> x7, Pallas kernels: none -> 310 us  [the longest x3 128 us: call(): pl.pallas_call(kernel, out_shape=outs, in_specs=[pl.BlockSpec(memory_spac...]
    dot_general x82 -> x0, matrix products: 156 us -> none  [the longest x24 53.6 us: product(): return jnp.dot(left, right, preferred_element_type=jnp.float32)]
    reshape x43 -> x19, local copies, waits for them, and re-layouts: 95.9 us -> 10.2 us  [the longest x7 4.52 us: local(): item.reshape(-1)]
    unnamed x2 -> x0, blocking collectives: 79.4 us -> none
    psum x2 -> x0, blocking collectives: 79.1 us -> none  [the longest x1 41 us: conv_backward(): lax.psum((jnp.sum(grad_normal, axis=0), jnp.sum(grad_normal * unit, axis=...]
  transfers between devices with their start and end apart: 20 -> 0, of which waited for: 13 -> 0; matrix products, arithmetic and copies ran while one was open for 17% -> 0% of each run, Pallas kernels for 0% -> 0%
where the time goes in v1:
time: 354 us; the launch traced here: 351 us
  Pallas kernels  310 us (88%)
  local copies, waits for them, and re-layouts  37.3 us (11%)
    pallas_call x3, Pallas kernels, call(): pl.pallas_call(kernel, out_shape=outs, in_specs=[pl.BlockSpec(memory_spac...  128 us
    pallas_call x1, Pallas kernels, reduce_all(): pl.pallas_call(lambda *refs: reduce_kernel(split, *refs), out_shape=[jax....  95.8 us
    pallas_call x1, Pallas kernels, gather_all(): pl.pallas_call(lambda *refs: gather_kernel(split, *refs), out_shape=jax.S...  64.3 us
    pallas_call x2, Pallas kernels, total_of(): pl.pallas_call(total_kernel, out_shape=jax.ShapeDtypeStruct(block, own.dt...  21.8 us

profile of v1, /device:TPU:0, one launch (start us, length us, event | category | flops | bytes accessed | tf_op | source)
XLA Modules:
  0.0 350.8 jit_solution(17898710849000116067)
XLA Ops:
  0.7 0.9 fusion.2
  1.6 0.8 copy.75
  2.5 0.7 reshape.172
  3.2 0.7 reshape.173
  3.9 0.7 reshape.174
  4.7 0.7 reshape.175
  5.4 0.7 reshape.176
  6.2 0.7 reshape.178
  6.9 0.8 reshape_reshape.3
  7.7 2.8 concatenate.9
  10.5 0.8 bitcast_dynamic-update-slice_fusion.1
  11.3 0.8 reshape.181
  12.2 0.7 constant_dynamic-update-slice_fusion.3
  12.9 0.8 copy.101
  13.7 0.7 constant_dynamic-update-slice_fusion.1
  14.5 0.8 bitcast_dynamic-update-slice_fusion.refs_0_
  15.3 0.7 copy-done
  16.1 64.3 %gather_all.1.weights.refs_4_.refs_3_ = bf16[32,384,512]{2,1,0:T(8,128)(2,1)} custom-call(bf16[384,512]{1,0:T(8,128)(2,1)} %copy-done), custom_call_target="tpu_custom_call" | custom-call | tf_op jit(solution)/shard_map/gather_all/pallas_call | solution.py:745
  80.4 1.0 slice.100
  81.8 0.8 copy.83.small.refs_5_.refs_4_
  82.7 0.7 reshape.205.inner_bias.refs_6_
  83.4 0.7 reshape.206.gate_bias
  84.1 0.7 reshape.207.table
  84.9 0.9 broadcast_in_dim.15.bounds.refs_1_
  86.3 42.1 %front.1 = (f32[512,512]{1,0:T(8,128)}, f32[512,512]{1,0:T(8,128)}, bf16[512,512]{1,0:T(8,128)(2,1)}, bf16[512,2048]{1,0:T(8,128)(2,1)}, bf16[512,2048]{1,0:T(8,...) custom-call(bf16[512,512]{1,0:T(8,128)(2,1)} %bitcast.66, ...), custom_call_target="tpu_custom_call" | custom-call | tf_op jit(solution)/shard_map/front/pallas_call | solution.py:549
  128.4 10.7 %total_of.2.refs_3_.refs_20_ = f32[8,512]{1,0:T(8,128)} custom-call(f32[8,512]{1,0:T(8,128)} %get-tuple-element.52.own), custom_call_target="tpu_custom_call" | custom-call | tf_op jit(solution)/shard_map/total_of/pallas_call | solution.py:826
  139.1 31.3 %turn.1 = (bf16[512,512]{1,0:T(8,128)(2,1)}, f32[512,512]{1,0:T(8,128)}, f32[512,512]{1,0:T(8,128)}, f32[512,512]{1,0:T(8,128)}, bf16[32,144,512]{2,1,0:T(8,128)...) custom-call(bf16[512,512]{1,0:T(8,128)(2,1)} %bitcast.76, ...), custom_call_target="tpu_custom_call" | custom-call | tf_op jit(solution)/shard_map/turn/pallas_call | solution.py:549
  170.4 11.2 %total_of.3.refs_21_ = f32[8,512]{1,0:T(8,128)} custom-call(f32[8,512]{1,0:T(8,128)} %get-tuple-element.68.own), custom_call_target="tpu_custom_call" | custom-call | tf_op jit(solution)/shard_map/total_of/pallas_call | solution.py:826
  181.5 54.3 %back.1 = (f32[512,512]{1,0:T(8,128)}, bf16[32,224,512]{2,1,0:T(8,128)(2,1)}, f32[48,512]{1,0:T(8,128)}, f32[2,2048]{1,0:T(2,128)}, f32[1,1024]{1,0:T(1,128)}, /*index=5*/f32[8,32]{1,0:T(8,128)}) custom-call(bf16[512,512]{1,0:T(8,128)(2,1)} %bitcast.67, s32[544,128]{1,0:T(8,128)} %broadcast_in_dim.15.bounds.refs_1_, s32[1,1024]{1,0:T(1,128)} %bitcast.94, ...), custom_call_target="tpu_custom_call" | custom-call | tf_op jit(solution)/shard_map/back/pallas_call | solution.py:549
  235.9 1.0 copy.86
  237.3 0.8 reshape.189
  238.7 1.3 reduce.7
  240.2 0.7 reshape.192
  241.0 0.7 copy.98
  241.7 95.8 %reduce_all.1 = (f32[368,512]{1,0:T(8,128)}, f32[8,128]{1,0:T(8,128)}) custom-call(bf16[32,224,512]{2,1,0:T(8,128)(2,1)} %get-tuple-element.72.refs_0_, bf16[32,144,512]{2,1,0:T(8,128)(2,1)} %get-tuple-element.73.refs_1_, f32[32,8,128]{2,1,0:T(8,128)} %bitcast.72), custom_call_target="tpu_custom_call" | custom-call | tf_op jit(solution)/shard_map/reduce_all/pallas_call | solution.py:991
  337.5 0.8 reshape.194
  338.3 0.7 slice.123
  339.1 0.6 fusion.3
  339.7 1.1 slice_bitcast_fusion.1
  340.8 0.7 pad_maximum_fusion.1
  341.9 0.7 pad_maximum_fusion
  342.7 0.9 slice.114
  343.6 0.7 copy.99
  344.3 0.8 slice.119
  345.1 0.6 copy.96
  345.8 1.4 fusion.1
  347.8 0.7 copy.94
  349.1 0.6 reshape.198
  (50 shorter events, 5.4 us)
Async XLA Ops:
  15.3 0.7 copy-start
  16.1 68.7 %copy-start.2 = (s32[1,512]{1,0:T(1,128)S(1)}, s32[1,512]{1,0:T(1,128)}, u32[]{:S(2)}) copy-start(s32[1,512]{1,0:T(1,128)} %marks.1) | copy-start | bytes 6148
  16.1 69.7 %copy-start.3 = (s32[1023]{0:T(1024)S(1)}, s32[1023]{0:T(1024)}, u32[]{:S(2)}) copy-start(s32[1023]{0:T(1024)} %param.24) | copy-start | bytes 12280
  337.5 10.3 %copy-start.1 = (f32[8,128]{1,0:T(8,128)S(1)}, f32[8,128]{1,0:T(8,128)}, u32[]{:S(2)}) copy-start(f32[8,128]{1,0:T(8,128)} %get-tuple-element.78) | copy-start | bytes 12292

commit v2 on v0

--- a/solution.py
+++ b/solution.py
@@ -1,15 +1,1064 @@
 import jax
 import jax.numpy as jnp
 from jax import lax
+from jax.experimental import pallas as pl
+from jax.experimental.pallas import tpu as pltpu
 from jax.sharding import PartitionSpec as P
 
 D = 512
+FF = 2048
 HEADS = 8
 HEAD_DIM = 64
 BUCKETS = 32
-
-
+L = 512
+TAPS = 32
+PAD = 16
 epsilon = 1e-05
+F32, BF16 = jnp.float32, jnp.bfloat16
+MESH = pl.DeviceIdType.MESH
+
+SMALL, IN0, OUT0, QKV, ATT, GLU, CONV, IN1, OUT1, ROWS = 0, 16, 80, 144, 192, 208, 240, 256, 320, 384
+GRADS = ROWS - IN0
+(S_FFN, S_FOB, S_ATTN, S_AOB, S_CONV, S_BATCH, S_COB, S_FINAL, S_TAPS, S_ROWS) = (0, 4, 6, 8, 9, 11, 13, 14, 16, 48)
+CHUNK = 64
+
+
+def dot(a, b):
+    return jnp.dot(a, b, preferred_element_type=F32)
+
+
+def dot_nt(a, b):
+    return lax.dot_general(a, b, (((1,), (1,)), ((), ())), preferred_element_type=F32)
+
+
+def dot_tn(a, b):
+    return lax.dot_general(a, b, (((0,), (0,)), ((), ())), preferred_element_type=F32)
+
+
+def chunks(body, carry=None, size=CHUNK):
+    def step(i, carry):
+        return body(pl.ds(pl.multiple_of(i * size, size), size), carry)
+
+    return lax.fori_loop(0, L // size, step, carry)
+
+
+def fold(values):
+    return jnp.sum(values.reshape(values.shape[0] // 8, 8, values.shape[1]), axis=0)
+
+
+def zeros8(width=D):
+    return jnp.zeros((8, width), F32)
+
+
+def total_row(values):
+    return jnp.sum(values, axis=0, keepdims=True)
+
+
+class Bag:
+    pass
+
+
+class Place:
+    def __init__(self):
+        self.planes = lax.axis_size("dp")
+        self.chips = lax.axis_size("fsdp") // 2
+        self.plane, inner = lax.axis_index("dp"), lax.axis_index("fsdp")
+        self.z, self.core = inner // 2, inner % 2
+        y, x = self.plane // 2, self.plane % 2
+        self.plane_x, self.plane_y, self.plane_d = y * 2 + 1 - x, (1 - y) * 2 + x, (1 - y) * 2 + 1 - x
+        self.twin = (self.plane, 2 * self.z + 1 - self.core)
+        self.over_x = (self.plane_x, inner)
+        self.over_y = (self.plane_y, inner)
+        self.chip = [lax.rem(self.z + step, self.chips) for step in range(self.chips)]
+        self.along = [(self.plane, 2 * chip + self.core) for chip in self.chip]
+        self.rank = self.plane * 2 + self.core
+        self.members = []
+        for step in range(self.planes):
+            for flip in range(2):
+                if step or flip:
+                    plane, core = lax.rem(self.plane + step, self.planes), lax.rem(self.core + flip, 2)
+                    self.members.append(((plane, 2 * self.z + core), plane * 2 + core))
+
+
+class Copies:
+    def __init__(self, sends, receives, place):
+        self.sends, self.receives, self.place = sends, receives, place
+        self.begun = []
+
+    def start(self, number, make, receive=None):
+        def copy():
+            source, target, device = make()
+            return pltpu.make_async_remote_copy(
+                source, target, self.sends.at[number], self.receives.at[number if receive is None else receive],
+                device_id=device, device_id_type=MESH,
+            )
+
+        copy().start()
+        self.begun.append(copy)
+
+    def arrived(self, number, target):
+        pltpu.make_async_remote_copy(
+            target, target, self.sends.at[number], self.receives.at[number],
+            device_id=self.place.twin, device_id_type=MESH,
+        ).wait_recv()
+
+    def sent(self):
+        for copy in self.begun:
+            copy().wait_send()
+        self.begun = []
+
+
+def gather_steps(place, weights, copies, first, begin, size, split):
+    p, core, chips = place, place.core, place.chips
+    rows = pl.ds(begin, size)
+    parts = (pl.ds(begin, split), pl.ds(begin + split, size - split))
+
+    def column(plane, side, which):
+        return weights.at[plane, :, side, which]
+
+    def move(number, ref, device):
+        copies.start(first + number, lambda: (ref(), ref(), device))
+
+    def along_z():
+        for d in range(1, chips):
+            move(d - 1, lambda: weights.at[p.plane, p.z, core, rows], p.along[d])
+
+    def own_column():
+        for d in range(1, chips):
+            copies.arrived(first + d - 1, weights.at[p.plane, p.chip[chips - d], core, rows])
+        own = lambda: column(p.plane, core, rows)
+        move(chips - 1, own, p.over_x)
+        move(chips, own, p.over_y)
+        move(chips + 3, own, p.twin)
+
+    def beside():
+        copies.arrived(first + chips - 1, column(p.plane_x, core, rows))
+        move(chips + 1, lambda: column(p.plane_x, core, parts[0]), p.over_y)
+        copies.arrived(first + chips, column(p.plane_y, core, rows))
+        move(chips + 2, lambda: column(p.plane_y, core, parts[1]), p.over_x)
+        move(chips + 4, lambda: column(p.plane_x, core, rows), p.twin)
+        move(chips + 5, lambda: column(p.plane_y, core, rows), p.twin)
+
+    def across():
+        copies.arrived(first + chips + 1, column(p.plane_d, core, parts[0]))
+        copies.arrived(first + chips + 2, column(p.plane_d, core, parts[1]))
+        move(chips + 6, lambda: column(p.plane_d, core, rows), p.twin)
+
+    def twins():
+        for number, plane in enumerate((p.plane, p.plane_x, p.plane_y, p.plane_d)):
+            copies.arrived(first + chips + 3 + number, column(plane, 1 - core, rows))
+
+    return [along_z, own_column, beside, across, twins]
+
+
+def reduce_steps(place, data, twin, diagonal, from_x, from_y, from_z, copies, first, begin, size, split, landing, finish):
+    p, core, chips = place, place.core, place.chips
+    rows, lands = pl.ds(begin, size), pl.ds(landing, size)
+    parts = (pl.ds(begin, split), pl.ds(begin + split, size - split))
+    parts_land = (pl.ds(landing, split), pl.ds(landing + split, size - split))
+
+    def column(plane, side, which):
+        return data.at[plane, :, side, which]
+
+    def add(plane, which, *sources):
+        def step(zz, carry):
+            value = data[plane, zz, core, which, :]
+            for ref in sources:
+                value = value + ref(zz)
+            data[plane, zz, core, which, :] = value
+            return carry
+
+        lax.fori_loop(0, chips, step, 0)
+
+    def read(ref, which, *lead):
+        return lambda zz: ref[lead + (zz, which, slice(None))]
+
+    def to_twin():
+        for number, plane in enumerate((p.plane_d, p.plane_y, p.plane_x, p.plane)):
+            copies.start(
+                first + number, lambda plane=plane: (column(plane, 1 - core, rows), twin.at[plane, :, lands], p.twin)
+            )
+
+    def across():
+        copies.arrived(first, twin.at[p.plane_d, :, lands])
+        add(p.plane_d, rows, read(twin, lands, p.plane_d))
+        copies.start(first + 4, lambda: (column(p.plane_d, core, parts[0]), diagonal.at[:, parts_land[0]], p.over_y))
+        if split < size:
+            copies.start(first + 5, lambda: (column(p.plane_d, core, parts[1]), diagonal.at[:, parts_land[1]], p.over_x))
+
+    def beside():
+        copies.arrived(first + 2, twin.at[p.plane_x, :, lands])
+        copies.arrived(first + 4, diagonal.at[:, parts_land[0]])
+        add(p.plane_x, rows, read(twin, lands, p.plane_x))
+        add(p.plane_x, parts[0], read(diagonal, parts_land[0]))
+        copies.start(first + 7, lambda: (column(p.plane_x, core, rows), from_x.at[:, lands], p.over_x))
+        copies.arrived(first + 1, twin.at[p.plane_y, :, lands])
+        add(p.plane_y, rows, read(twin, lands, p.plane_y))
+        if split < size:
+            copies.arrived(first + 5, diagonal.at[:, parts_land[1]])
+            add(p.plane_y, parts[1], read(diagonal, parts_land[1]))
+        copies.start(first + 6, lambda: (column(p.plane_y, core, rows), from_y.at[:, lands], p.over_y))
+
+    def own_column():
+        copies.arrived(first + 3, twin.at[p.plane, :, lands])
+        copies.arrived(first + 6, from_y.at[:, lands])
+        copies.arrived(first + 7, from_x.at[:, lands])
+        add(p.plane, rows, read(twin, lands, p.plane), read(from_x, lands), read(from_y, lands))
+        for d in range(1, chips):
+            copies.start(
+                first + 7 + d,
+                lambda d=d: (data.at[p.plane, p.chip[d], core, rows], from_z.at[d - 1, lands], p.along[d]),
+            )
+
+    def along_z():
+        for d in range(1, chips):
+            copies.arrived(first + 7 + d, from_z.at[d - 1, lands])
+        value = data[p.plane, p.z, core, rows, :].astype(F32)
+        for d in range(1, chips):
+            value = value + from_z[d - 1, lands, :].astype(F32)
+        finish(value)
+
+    return [to_twin, across, beside, own_column, along_z]
+
+
+class Total:
+    def __init__(self, place, own, near, part, far, result, copies, first):
+        self.place, self.own, self.near, self.part, self.far, self.result = place, own, near, part, far, result
+        self.copies, self.first = copies, first
+
+    def start(self):
+        p = self.place
+        me = p.rank
+        for i, (device, rank) in enumerate(p.members):
+            self.copies.start(self.first + i, lambda device=device: (self.own, self.near.at[me], device), self.first + me)
+        self.near[me] = self.own[...]
+
+    def turn(self):
+        p = self.place
+        for device, rank in p.members:
+            self.copies.arrived(self.first + rank, self.near.at[rank])
+        value = self.near[0]
+        for i in range(1, 2 * p.planes):
+            value = value + self.near[i]
+        self.part[...] = value
+        base = self.first + 2 * p.planes
+        for d in range(1, p.chips):
+            self.copies.start(base + d, lambda d=d: (self.part, self.far.at[d], p.along[d]))
+
+    def finish(self):
+        p = self.place
+        base = self.first + 2 * p.planes
+        value = self.part[...]
+        for d in range(1, p.chips):
+            self.copies.arrived(base + d, self.far.at[d])
+            value = value + self.far[d]
+        self.result[...] = value
+
+
+class Queue:
+    def __init__(self):
+        self.steps, self.taken = [], 0
+
+    def add(self, *steps):
+        self.steps += steps
+
+    def take(self, count=1):
+        for step in self.steps[self.taken : self.taken + count]:
+            step()
+        self.taken = min(len(self.steps), self.taken + count)
+
+    def until(self, step):
+        self.take(self.steps.index(step) + 1 - self.taken)
+
+    def drain(self):
+        self.take(len(self.steps) - self.taken)
+
+    def inside(self, index, *at):
+        for i in at:
+            if self.taken < len(self.steps):
+                pl.when(index == i)(self.steps[self.taken])
+                self.taken += 1
+
+
+def standard(values):
+    values = values.astype(F32)
+    center = values - jnp.mean(values, axis=-1, keepdims=True)
+    inverse = lax.rsqrt(jnp.mean(center * center, axis=-1, keepdims=True) + epsilon)
+    return center * inverse, inverse
+
+
+def norm_rows(source, target, small, row):
+    gain, shift = 1.0 + small[row : row + 1, :], small[row + 1 : row + 2, :]
+
+    def body(rows, carry):
+        target[rows, :] = (standard(source[rows, :])[0] * gain + shift).astype(target.dtype)
+        return carry
+
+    chunks(body, 0)
+
+
+def norm_back(source, grad, upstream, result, small, row, grads):
+    gain = 1.0 + small[row : row + 1, :]
+
+    def body(rows, carry):
+        unit, inverse = standard(source[rows, :])
+        given = grad[rows, :].astype(F32)
+        inner = given * gain
+        back = inverse * (
+            inner
+            - jnp.mean(inner, axis=-1, keepdims=True)
+            - unit * jnp.mean(inner * unit, axis=-1, keepdims=True)
+        )
+        result[rows, :] = back if upstream is None else upstream[rows, :] + back
+        return carry[0] + fold(given * unit), carry[1] + fold(given)
+
+    first, second = chunks(body, (zeros8(), zeros8()))
+    grads[row : row + 1, :] = total_row(first)
+    grads[row + 1 : row + 2, :] = total_row(second)
+
+
+def block_cols(c):
+    return pl.ds(pl.multiple_of(c * D, D), D)
+
+
+def columns(weights, start, block):
+    return weights[:, :, :, pl.ds(pl.multiple_of(start + 16 * block, 16), 16), :].reshape(D, D)
+
+
+def put_columns(weights, start, block, value):
+    rows = pl.ds(pl.multiple_of(start + 16 * block, 16), 16)
+    weights[:, :, :, rows, :] = value.astype(BF16).reshape(weights.shape[:3] + (16, D))
+
+
+def lines_of(weights, start, block):
+    return weights[block, :, :, start : start + 64, :].reshape(D, D)
+
+
+def put_lines(weights, start, block, value):
+    weights[block, :, :, start : start + 64, :] = value.astype(BF16).reshape(weights.shape[1:3] + (64, D))
+
+
+def feed_inner(source, normed, active, slope, hold, weights, small, inner_bias, layer, pump):
+    norm_rows(source, normed, small, S_FFN + 2 * layer)
+
+    def block(c, carry):
+        cols = block_cols(c)
+        hold[...] = dot(normed[...], columns(weights, (IN0, IN1)[layer], c))
+        bias = inner_bias[layer : layer + 1, cols]
+
+        def body(rows, carry):
+            inner = hold[rows, :] + bias
+            sigma = jax.nn.sigmoid(inner)
+            value = inner * sigma
+            active[rows, cols] = value.astype(BF16)
+            slope[rows, cols] = (sigma + value * (1.0 - sigma)).astype(BF16)
+            return carry
+
+        chunks(body, 0)
+        pump(c)
+        return carry
+
+    lax.fori_loop(0, FF // D, block, 0)
+
+
+def feed_outer(source, active, result, hold, weights, small, layer):
+    begin = (OUT0, OUT1)[layer]
+
+    def block(c, carry):
+        part = dot(active[:, block_cols(c)], lines_of(weights, begin, c))
+
+        @pl.when(c == 0)
+        def _():
+            hold[...] = part
+
+        @pl.when(c > 0)
+        def _():
+            hold[...] += part
+
+        return carry
+
+    lax.fori_loop(0, FF // D, block, 0)
+    bias = small[S_FOB + layer : S_FOB + layer + 1, :]
+
+    def body(rows, carry):
+        result[rows, :] = source[rows, :].astype(F32) + 0.5 * (hold[rows, :] + bias)
+        return carry
+
+    chunks(body, 0)
+
+
+def feed_back_outer(upstream, active, slope, low, hold, weights, grads, inner_grads, layer, pump):
+    begin = (OUT0, OUT1)[layer]
+
+    def start(rows, carry):
+        half = 0.5 * upstream[rows, :]
+        low[rows, :] = half.astype(BF16)
+        return carry + fold(half)
+
+    grads[S_FOB + layer : S_FOB + layer + 1, :] = total_row(chunks(start, zeros8()))
+
+    def block(c, carry):
+        cols = block_cols(c)
+        hold[...] = dot_nt(low[...], lines_of(weights, begin, c))
+
+        def body(rows, carry):
+            grad = hold[rows, :] * slope[rows, cols].astype(F32)
+            slope[rows, cols] = grad.astype(BF16)
+            return carry + fold(grad)
+
+        inner_grads[layer : layer + 1, cols] = total_row(chunks(body, zeros8()))
+        put_lines(weights, begin, c, dot_tn(active[:, cols], low[...]))
+        pump(c)
+        return carry
+
+    lax.fori_loop(0, FF // D, block, 0)
+
+
+def product_back(grad, normed, total, weights, begin, blocks, pump):
+    def block(c, carry):
+        cols = block_cols(c)
+        part = dot_nt(grad[:, cols], columns(weights, begin, c))
+
+        @pl.when(c == 0)
+        def _():
+            total[...] = part
+
+        @pl.when(c > 0)
+        def _():
+            total[...] += part
+
+        put_columns(weights, begin, c, dot_tn(normed[...], grad[:, cols]))
+        pump(c)
+        return carry
+
+    lax.fori_loop(0, blocks, block, 0)
+
+
+def bucket_choice(buckets):
+    return (lax.broadcasted_iota(jnp.int32, (BUCKETS, 2 * L), 0) == buckets[...]).astype(F32)
+
+
+def attention_mix(source, normed, mixed, weights, small):
+    norm_rows(source, normed, small, S_ATTN)
+
+    def mix(c, carry):
+        mixed[:, block_cols(c)] = dot(normed[...], columns(weights, QKV, c)).astype(BF16)
+        return carry
+
+    lax.fori_loop(0, 3, mix, 0)
+
+
+def attention_forward(source, mixed, probs, joined, result, lines, hold, weights, small, table, buckets, bounds, marks, pump):
+    lines[...] = dot(table[...].astype(BF16), bucket_choice(buckets).astype(BF16))
+    lane = lax.broadcasted_iota(jnp.int32, (1, 128), 1)
+    size = 128
+
+    def pair(index, carry):
+        begin = pl.multiple_of(128 * index, 128)
+        keys = mixed[:, pl.ds(D + begin, 128)]
+        contents = mixed[:, pl.ds(2 * D + begin, 128)]
+        for block in range(L // size):
+            rows = pl.ds(block * size, size)
+            query = mixed[rows, pl.ds(begin, 128)]
+            same = bounds[PAD + block * size : PAD + (block + 1) * size, 0:1] == marks[...]
+            parts = []
+            for half in range(2):
+                head = 2 * index + half
+                here = (lane // HEAD_DIM) == half
+                raw = dot_nt(jnp.where(here, query, jnp.zeros_like(query)), keys)
+                window = lines[pl.ds(head, 1), 384 - block * size : 1024 - block * size]
+                square = pltpu.roll(jnp.broadcast_to(window, (size, 640)), 513, 1, stride=1, stride_axis=0)
+                scores = jnp.where(same, raw * HEAD_DIM ** (-0.5) + square[:, :L], -1e30)
+                raised = jnp.exp(scores - jnp.max(scores, axis=1, keepdims=True))
+                share = (raised * (1.0 / jnp.sum(raised, axis=1, keepdims=True))).astype(BF16)
+                probs[head, rows, :] = share
+                parts.append(dot(share, contents))
+            joined[rows, pl.ds(begin, 128)] = jnp.where(lane < HEAD_DIM, parts[0], parts[1]).astype(BF16)
+        pump(index)
+        return carry
+
+    lax.fori_loop(0, HEADS // 2, pair, 0)
+    hold[...] = dot(joined[...], columns(weights, ATT, 0))
+    bias = small[S_AOB : S_AOB + 1, :]
+
+    def body(rows, carry):
+        result[rows, :] = source[rows, :] + hold[rows, :] + bias
+        return carry
+
+    chunks(body, 0)
+
+
+def attention_backward(
+    upstream, mixed, probs, joined, low, spread, grad_mixed, scaled, hold, lines, weights, buckets, grads, table_grad, pump
+):
+    def start(rows, carry):
+        given = upstream[rows, :]
+        low[rows, :] = given.astype(BF16)
+        return carry + fold(given)
+
+    grads[S_AOB : S_AOB + 1, :] = total_row(chunks(start, zeros8()))
+    spread[...] = dot_nt(low[...], columns(weights, ATT, 0)).astype(BF16)
+    put_columns(weights, ATT, 0, dot_tn(joined[...], low[...]))
+    lane = lax.broadcasted_iota(jnp.int32, (1, 128), 1)
+    row8 = lax.broadcasted_iota(jnp.int32, (8, 2 * L), 0)
+    size = 128
+
+    def pair(index, carry):
+        begin = pl.multiple_of(128 * index, 128)
+        query = mixed[:, pl.ds(begin, 128)]
+        keys = mixed[:, pl.ds(D + begin, 128)]
+        contents = mixed[:, pl.ds(2 * D + begin, 128)]
+        incoming = spread[:, pl.ds(begin, 128)]
+        parts = []
+        for half in range(2):
+            head = 2 * index + half
+            here = (lane // HEAD_DIM) == half
+            hold[...] = dot_nt(jnp.where(here, incoming, jnp.zeros_like(incoming)), contents)
+            sums = zeros8(2 * L)
+            for block in range(L // size):
+                rows = pl.ds(block * size, size)
+                share = probs[head, rows, :].astype(F32)
+                given = hold[rows, :]
+                slant = share * (given - jnp.sum(given * share, axis=1, keepdims=True))
+                scaled[rows, :] = (slant * HEAD_DIM ** (-0.5)).astype(BF16)
+                part = zeros8(640)
+                for t in range(size // 8):
+                    tile = jnp.concatenate([slant[8 * t : 8 * t + 8], zeros8(128)], axis=1)
+                    part += pltpu.roll(tile, 120 - 8 * t, 1)
+                first = 384 - block * size
+                pieces = [part]
+                if first:
+                    pieces = [zeros8(first)] + pieces
+                if block:
+                    pieces = pieces + [zeros8(block * size)]
+                sums += jnp.concatenate(pieces, axis=1)
+            line = zeros8(2 * L)
+            for r in range(8):
+                line += jnp.where(row8 == r, pltpu.roll(sums, 7 - r, 1), 0.0)
+            lines[pl.ds(head, 1), :] = total_row(line)
+            parts.append((dot(scaled[...], keys), dot_tn(scaled[...], query), dot_tn(probs[head], incoming)))
+        for third in range(3):
+            merged = jnp.where(lane < HEAD_DIM, parts[0][third], parts[1][third])
+            grad_mixed[:, pl.ds(third * D + begin, 128)] = merged.astype(BF16)
+        pump(index)
+        return carry
+
+    lax.fori_loop(0, HEADS // 2, pair, 0)
+    table_grad[...] = lax.dot_general(
+        lines[...], bucket_choice(buckets), (((1,), (1,)), ((), ())),
+        precision=lax.Precision.HIGHEST, preferred_element_type=F32,
+    )
+
+
+def clear_pads(padded):
+    edge = jnp.zeros((4, PAD, 128), F32)
+    padded[:, 0:PAD, :] = edge
+    padded[:, PAD + L : 2 * PAD + L, :] = edge
+
+
+def conv_front(source, normed, sigma, gated, middle, sums, hold, weights, small, gate_bias, bounds, pump):
+    norm_rows(source, normed, small, S_CONV)
+    clear_pads(gated)
+    hold[...] = dot(normed[...], columns(weights, GLU, 1))
+    bias = gate_bias[0:1, D:]
+
+    def gate(rows, carry):
+        sigma[rows, :] = jax.nn.sigmoid(hold[rows, :] + bias)
+        return carry
+
+    chunks(gate, 0)
+    hold[...] = dot(normed[...], columns(weights, GLU, 0))
+    bias = gate_bias[0:1, :D]
+
+    def unit(rows, carry):
+        values = (hold[rows, :] + bias) * sigma[rows, :]
+        for j in range(4):
+            gated[j, pl.ds(rows.start + PAD, CHUNK), :] = values[:, 128 * j : 128 * j + 128]
+        return carry
+
+    chunks(unit, 0)
+    size = 16
+
+    def slide(i, carry):
+        begin = pl.multiple_of(i * size, size)
+        marks = bounds[pl.ds(begin + PAD, size), :]
+        accs = [jnp.zeros((size, 128), F32) for _ in range(4)]
+        for k in range(TAPS):
+            same = bounds[pl.ds(begin + k, size), :] == marks
+            for j in range(4):
+                tap = small[S_TAPS + k : S_TAPS + k + 1, 128 * j : 128 * j + 128]
+                accs[j] += jnp.where(same, gated[j, pl.ds(begin + k, size), :], 0.0) * tap
+        result = []
+        for j in range(4):
+            middle[pl.ds(begin, size), 128 * j : 128 * j + 128] = accs[j]
+            result.append(carry[j] + fold(accs[j]))
+            result.append(carry[4 + j] + fold(accs[j] * accs[j]))
+        pump(i)
+        return result[0::2] + result[1::2]
+
+    ends = lax.fori_loop(0, L // size, slide, [zeros8(128)] * 8)
+    sums[...] = zeros8()
+    for j in range(4):
+        sums[0:1, 128 * j : 128 * j + 128] = total_row(ends[j])
+        sums[1:2, 128 * j : 128 * j + 128] = total_row(ends[4 + j])
+
+
+def conv_rest(source, middle, sums, unit, active, slope, result, hold, weights, small, frames):
+    center = sums[0:1, :] * (1.0 / frames)
+    inverse = lax.rsqrt(sums[1:2, :] * (1.0 / frames) - center * center + epsilon)
+    gain, shift = 1.0 + small[S_BATCH : S_BATCH + 1, :], small[S_BATCH + 1 : S_BATCH + 2, :]
+
+    def body(rows, carry):
+        values = (middle[rows, :] - center) * inverse
+        unit[rows, :] = values
+        normal = values * gain + shift
+        sigma = jax.nn.sigmoid(normal)
+        value = normal * sigma
+        active[rows, :] = value.astype(BF16)
+        slope[rows, :] = (sigma + value * (1.0 - sigma)).astype(slope.dtype)
+        return carry
+
+    chunks(body, 0)
+    hold[...] = dot(active[...], columns(weights, CONV, 0))
+    bias = small[S_COB : S_COB + 1, :]
+
+    def add(rows, carry):
+        result[rows, :] = source[rows, :] + hold[rows, :] + bias
+        return carry
+
+    chunks(add, 0)
+
+
+def conv_back_rest(upstream, unit, slope, grad_normal, low, hold, weights, grads, sums):
+    def start(rows, carry):
+        given = upstream[rows, :]
+        low[rows, :] = given.astype(BF16)
+        return carry + fold(given)
+
+    grads[S_COB : S_COB + 1, :] = total_row(chunks(start, zeros8()))
+    hold[...] = dot_nt(low[...], columns(weights, CONV, 0))
+
+    def body(rows, carry):
+        grad = hold[rows, :] * slope[rows, :].astype(F32)
+        grad_normal[rows, :] = grad
+        return carry[0] + fold(grad), carry[1] + fold(grad * unit[rows, :])
+
+    first, second = chunks(body, (zeros8(), zeros8()))
+    sums[...] = zeros8()
+    sums[0:1, :] = total_row(first)
+    sums[1:2, :] = total_row(second)
+    grads[S_BATCH : S_BATCH + 1, :] = total_row(second)
+    grads[S_BATCH + 1 : S_BATCH + 2, :] = total_row(first)
+
+
+def conv_back_front(
+    sigma, gated, unit, grad_normal, front_sums, sums, padded, grad_joined, hold, tap_sums, small, bounds, grads, gate_grads,
+    frames, pump,
+):
+    center = front_sums[0:1, :] * (1.0 / frames)
+    inverse = lax.rsqrt(front_sums[1:2, :] * (1.0 / frames) - center * center + epsilon)
+    gain = 1.0 + small[S_BATCH : S_BATCH + 1, :]
+    mean0, mean1 = gain * sums[0:1, :] * (1.0 / frames), gain * sums[1:2, :] * (1.0 / frames)
+    clear_pads(padded)
+
+    def start(rows, carry):
+        grad = inverse * (gain * grad_normal[rows, :] - mean0 - unit[rows, :] * mean1)
+        for j in range(4):
+            padded[j, pl.ds(rows.start + PAD, CHUNK), :] = grad[:, 128 * j : 128 * j + 128]
+        return carry
+
+    chunks(start, 0)
+    tap_sums[...] = jnp.zeros_like(tap_sums)
+    size = 16
+
+    def slide(i, carry):
+        begin = pl.multiple_of(i * size, size)
+        marks = bounds[pl.ds(begin + PAD, size), :]
+        accs = [jnp.zeros((size, 128), F32) for _ in range(4)]
+        for k in range(TAPS):
+            same = bounds[pl.ds(begin + 2 * PAD - k, size), :] == marks
+            for j in range(4):
+                tap = small[S_TAPS + k : S_TAPS + k + 1, 128 * j : 128 * j + 128]
+                accs[j] += jnp.where(same, padded[j, pl.ds(begin + 2 * PAD - k, size), :], 0.0) * tap
+        for j in range(4):
+            hold[pl.ds(begin, size), 128 * j : 128 * j + 128] = accs[j]
+        grads_here = [padded[j, pl.ds(begin + PAD, size), :] for j in range(4)]
+        for k in range(TAPS):
+            same = bounds[pl.ds(begin + k, size), :] == marks
+            for j in range(4):
+                term = jnp.where(same, gated[j, pl.ds(begin + k, size), :], 0.0) * grads_here[j]
+                tap_sums[k, :, 128 * j : 128 * j + 128] += fold(term)
+        pump(i)
+        return carry
+
+    lax.fori_loop(0, L // size, slide, 0)
+    grads[S_TAPS : S_TAPS + TAPS, :] = jnp.sum(tap_sums[...], axis=1)
+
+    def split(rows, carry):
+        grad = hold[rows, :]
+        gate = sigma[rows, :]
+        values = jnp.concatenate([gated[j, pl.ds(rows.start + PAD, CHUNK), :] for j in range(4)], axis=1)
+        first = grad * gate
+        second = grad * values * (1.0 - gate)
+        grad_joined[rows, :D] = first.astype(BF16)
+        grad_joined[rows, D : 2 * D] = second.astype(BF16)
+        return carry[0] + fold(first), carry[1] + fold(second)
+
+    first, second = chunks(split, (zeros8(), zeros8()))
+    gate_grads[0:1, :D] = total_row(first)
+    gate_grads[0:1, D:] = total_row(second)
+
+
+THIN = (
+    ("ffn_norm", S_FFN), ("ffn_out_bias", S_FOB), ("attn_norm", S_ATTN), ("attn_out_bias", S_AOB), ("conv_norm", S_CONV),
+    ("batch_norm", S_BATCH), ("conv_out_bias", S_COB), ("final_norm", S_FINAL), ("depth_kernel", S_TAPS),
+)
+
+
+def pack_small(b, tile):
+    tile[...] = jnp.zeros_like(tile)
+    for name, row in THIN:
+        value = getattr(b, name)[...].astype(F32)
+        value = value.reshape(-1, value.shape[-1])
+        for r in range(0, value.shape[0], 16):
+            part = value[r : r + 16]
+            begin = (row + r) % 16
+            at = 128 * ((row + r) // 16)
+            tile[begin : begin + part.shape[0], at : at + part.shape[1]] = part
+    tile[0:2, 384 : 384 + b.ffn_in_bias.shape[1]] = b.ffn_in_bias[...].astype(F32)
+    wide, few = b.glu_bias.shape[0], b.rel_table.shape[0]
+    tile[2:3, 384 : 384 + wide] = b.glu_bias[...].astype(F32).reshape(1, wide)
+    tile[3:4, 384 : 384 + few] = b.rel_table[...].astype(F32).reshape(1, few)
+
+
+def pack_weights(b, put):
+    for layer in range(2):
+        for c in range(FF // D):
+            put((IN0, IN1)[layer] + 16 * c, b.ffn_in[layer, :, D * c : D * c + D])
+        put((OUT0, OUT1)[layer], b.ffn_out[layer])
+    for c in range(3):
+        put(QKV + 16 * c, b.qkv_weight[:, D * c : D * c + D])
+    put(ATT, b.attn_out[...])
+    for c in range(2):
+        put(GLU + 16 * c, b.glu_weight[:, D * c : D * c + D])
+    put(CONV, b.conv_out[...])
+
+
+def unpack_small(b, place):
+    per = 2 * place.chips
+    count = place.planes * per
+    width = D // count
+    for device in range(count):
+        tile = b.weights[device // per, (device % per) // 2, device % 2, 0:16, :].astype(F32)
+        for q in range(3):
+            b.small[16 * q : 16 * q + 16, width * device : width * device + width] = tile[:, 128 * q : 128 * q + width]
+        b.inner_bias[:, 4 * width * device : 4 * width * (device + 1)] = tile[0:2, 384 : 384 + 4 * width]
+        b.gate_bias[:, 2 * width * device : 2 * width * (device + 1)] = tile[2:3, 384 : 384 + 2 * width]
+        few = HEADS * BUCKETS // count
+        head, at = few * device // BUCKETS, few * device % BUCKETS
+        b.table[head : head + 1, at : at + few] = tile[3:4, 384 : 384 + few]
+
+
+def pack_small_grads(b, place):
+    per = 2 * place.chips
+    count = place.planes * per
+    width = D // count
+    few = HEADS * BUCKETS // count
+    for device in range(count):
+        tile = b.edges.at[device // per, (device % per) // 2, device % 2]
+        for g in range(8):
+            tile[0:6, 16 * g : 16 * g + width] = b.grads[6 * g : 6 * g + 6, width * device : width * device + width]
+        for m in range(2):
+            tile[6:7, 64 * m : 64 * m + 4 * width] = b.inner_grads[m : m + 1, 4 * width * device : 4 * width * (device + 1)]
+        tile[7:8, 0 : 2 * width] = b.gate_grads[:, 2 * width * device : 2 * width * (device + 1)]
+        head, at = few * device // BUCKETS, few * device % BUCKETS
+        tile[7:8, 64 : 64 + few] = b.table_grad[head : head + 1, at : at + few]
+
+
+INPUTS = (
+    "inputs", "segments", "buckets", "cotangent", "ffn_norm", "ffn_in", "ffn_in_bias", "ffn_out", "ffn_out_bias", "attn_norm",
+    "qkv_weight", "attn_out", "attn_out_bias", "rel_table", "conv_norm", "glu_weight", "glu_bias", "depth_kernel", "batch_norm",
+    "conv_out", "conv_out_bias", "final_norm",
+)
+OUTPUTS = ("output", "grad_x", "shard", "thin")
+GATHERS = ((0, 80, 48), (80, 64, 32), (144, 112, 64), (256, 128, 64))
+REDUCES = ((OUT1, 64, 32), (IN1, 64, 32), (GLU, 48, 32), (QKV, 64, 32), (OUT0, 64, 32), (IN0, 64, 32))
+
+
+def scratch_of(planes, chips):
+    wide, low, big = pltpu.VMEM((L, D), F32), pltpu.VMEM((L, D), BF16), pltpu.VMEM((L, FF), BF16)
+    pads = pltpu.VMEM((4, L + 2 * PAD, 128), F32)
+    stats = pltpu.VMEM((8, D), F32)
+    return dict(
+        weights=pltpu.VMEM((planes, chips, 2, ROWS, D), BF16),
+        twin=pltpu.VMEM((planes, chips, GRADS, D), BF16),
+        diagonal=pltpu.VMEM((chips, GRADS, D), BF16),
+        from_x=pltpu.VMEM((chips, GRADS, D), BF16),
+        from_y=pltpu.VMEM((chips, GRADS, D), BF16),
+        from_z=pltpu.VMEM((chips - 1, GRADS, D), BF16),
+        edges=pltpu.VMEM((planes, chips, 2, 8, 128), F32),
+        edge_twin=pltpu.VMEM((planes, chips, 8, 128), F32),
+        edge_diagonal=pltpu.VMEM((chips, 8, 128), F32),
+        edge_x=pltpu.VMEM((chips, 8, 128), F32),
+        edge_y=pltpu.VMEM((chips, 8, 128), F32),
+        edge_z=pltpu.VMEM((chips - 1, 8, 128), F32),
+        small=pltpu.VMEM((S_ROWS, D), F32),
+        inner_bias=pltpu.VMEM((2, FF), F32),
+        gate_bias=pltpu.VMEM((1, 2 * D), F32),
+        table=pltpu.VMEM((HEADS, BUCKETS), F32),
+        tile=pltpu.VMEM((16, D), F32),
+        grads=pltpu.VMEM((S_ROWS, D), F32),
+        inner_grads=pltpu.VMEM((2, FF), F32),
+        gate_grads=pltpu.VMEM((1, 2 * D), F32),
+        table_grad=pltpu.VMEM((HEADS, BUCKETS), F32),
+        lines=pltpu.VMEM((HEADS, 2 * L), F32),
+        choice=pltpu.VMEM((1, 2 * L), jnp.int32),
+        bounds=pltpu.VMEM((L + 2 * PAD, 128), F32),
+        marks=pltpu.VMEM((1, L), F32),
+        front_own=stats, back_own=stats, front_sums=stats, back_sums=stats, front_part=stats, back_part=stats,
+        front_near=pltpu.VMEM((2 * planes, 8, D), F32), back_near=pltpu.VMEM((2 * planes, 8, D), F32),
+        front_far=pltpu.VMEM((chips, 8, D), F32), back_far=pltpu.VMEM((chips, 8, D), F32),
+        x1=wide, x2=wide, x3=wide, x4=wide, normed0=low, normed_a=low, normed_c=low, normed1=low,
+        active0=big, slope0=big, active1=big, slope1=big, mixed=pltpu.VMEM((L, 3 * D), BF16),
+        probs=pltpu.VMEM((HEADS, L, L), BF16), joined=low, sigma=wide, gated=pads, middle=wide, active_c=low, slope_c=low,
+        padded=pads, low=low, spread=low, hold=wide, total=wide, taps=pltpu.VMEM((TAPS, 8, D), F32),
+        gather_sends=pltpu.SemaphoreType.DMA((len(GATHERS) * (chips + 7),)),
+        gather_receives=pltpu.SemaphoreType.DMA((len(GATHERS) * (chips + 7),)),
+        reduce_sends=pltpu.SemaphoreType.DMA(((len(REDUCES) + 1) * (chips + 7),)),
+        reduce_receives=pltpu.SemaphoreType.DMA(((len(REDUCES) + 1) * (chips + 7),)),
+        total_sends=pltpu.SemaphoreType.DMA((2 * (2 * planes + chips),)),
+        total_receives=pltpu.SemaphoreType.DMA((2 * (2 * planes + chips),)),
+    )
+
+
+def whole_kernel(names, *refs):
+    b = Bag()
+    for name, ref in zip(names, refs):
+        setattr(b, name, ref)
+    place = Place()
+    planes, chips = place.planes, place.chips
+    frames = L * planes * chips * 2
+    barrier = pltpu.get_barrier_semaphore()
+    near = [device for device, rank in place.members] + [place.along[d] for d in range(1, chips)]
+    for device in near:
+        pl.semaphore_signal(barrier, inc=1, device_id=device, device_id_type=MESH)
+    pack_small(b, b.tile)
+
+    def put(row, value):
+        b.weights[place.plane, place.z, place.core, row : row + value.shape[0], :] = value
+
+    put(0, b.tile[...].astype(BF16))
+    pack_weights(b, put)
+    pl.semaphore_wait(barrier, len(near))
+
+    gathers = Copies(b.gather_sends, b.gather_receives, place)
+    rounds = [
+        gather_steps(place, b.weights, gathers, i * (chips + 7), begin, size, split)
+        for i, (begin, size, split) in enumerate(GATHERS)
+    ]
+    queue = Queue()
+    queue.add(
+        rounds[0][0], rounds[1][0], rounds[0][1], rounds[0][2], rounds[1][1], rounds[2][0], rounds[0][3], rounds[1][2],
+        rounds[0][4],
+    )
+    queue.add(
+        rounds[2][1], rounds[1][3], rounds[3][0], rounds[1][4], rounds[2][2], rounds[3][1], rounds[2][3], rounds[2][4],
+        rounds[3][2], rounds[3][3], rounds[3][4],
+    )
+    still = lambda index: None
+    queue.take(2)
+    b.marks[...] = b.segments[...].astype(F32)
+    b.bounds[...] = jnp.full(b.bounds.shape, -1.0, F32)
+    b.bounds[PAD : PAD + L, :] = jnp.broadcast_to(b.marks[...], (128, L)).T
+    b.choice[...] = jnp.full(b.choice.shape, -1, jnp.int32)
+    b.choice[:, 0 : 2 * L - 1] = b.buckets[...].reshape(1, 2 * L - 1)
+    queue.until(rounds[0][4])
+    unpack_small(b, place)
+
+    x0 = b.inputs.at[0]
+    feed_inner(
+        x0, b.normed0, b.active0, b.slope0, b.hold, b.weights, b.small, b.inner_bias, 0, lambda c: queue.inside(c, 0, 1, 2)
+    )
+    queue.until(rounds[1][4])
+    feed_outer(x0, b.active0, b.x1, b.hold, b.weights, b.small, 0)
+    queue.until(rounds[2][4])
+    attention_mix(b.x1, b.normed_a, b.mixed, b.weights, b.small)
+    attention_forward(
+        b.x1, b.mixed, b.probs, b.joined, b.x2, b.lines, b.hold, b.weights, b.small, b.table, b.choice, b.bounds, b.marks,
+        lambda index: queue.inside(index, 0, 1, 2),
+    )
+    conv_front(
+        b.x2, b.normed_c, b.sigma, b.gated, b.middle, b.front_own, b.hold, b.weights, b.small, b.gate_bias, b.bounds, still
+    )
+    totals = Copies(b.total_sends, b.total_receives, place)
+    front = Total(place, b.front_own, b.front_near, b.front_part, b.front_far, b.front_sums, totals, 0)
+    front.start()
+    queue.drain()
+    front.turn()
+    front.finish()
+    conv_rest(b.x2, b.middle, b.front_sums, b.middle, b.active_c, b.slope_c, b.x3, b.hold, b.weights, b.small, frames)
+    feed_inner(b.x3, b.normed1, b.active1, b.slope1, b.hold, b.weights, b.small, b.inner_bias, 1, still)
+    feed_outer(b.x3, b.active1, b.x4, b.hold, b.weights, b.small, 1)
+    norm_rows(b.x4, b.output.at[0], b.small, S_FINAL)
+    flow = b.x4
+    norm_back(b.x4, b.cotangent.at[0], None, flow, b.small, S_FINAL, b.grads)
+    gathers.sent()
+
+    reduces = Copies(b.reduce_sends, b.reduce_receives, place)
+    landings = (b.twin, b.diagonal, b.from_x, b.from_y, b.from_z)
+
+    def finish(begin, size):
+        def act(value):
+            b.shard[begin - IN0 : begin - IN0 + size, :] = value
+
+        return act
+
+    backs = [
+        reduce_steps(
+            place, b.weights, *landings, reduces, i * (chips + 7), begin, size, split, begin - IN0, finish(begin, size)
+        )
+        for i, (begin, size, split) in enumerate(REDUCES)
+    ]
+
+    def finish_thin(value):
+        b.thin[...] = value
+
+    thin = reduce_steps(
+        place, b.edges, b.edge_twin, b.edge_diagonal, b.edge_x, b.edge_y, b.edge_z, reduces, len(REDUCES) * (chips + 7),
+        0, 8, 8, 0, finish_thin,
+    )
+    queue = Queue()
+    feed_back_outer(flow, b.active1, b.slope1, b.low, b.hold, b.weights, b.grads, b.inner_grads, 1, still)
+    queue.add(backs[0][0])
+    queue.take()
+    queue.add(backs[0][1])
+    product_back(b.slope1, b.normed1, b.total, b.weights, IN1, 4, lambda c: queue.inside(c, 2))
+    queue.add(backs[1][0], backs[0][2])
+    queue.take()
+    norm_back(b.x3, b.total, flow, flow, b.small, S_FFN + 2, b.grads)
+    queue.take()
+    grad_normal = b.x3
+    conv_back_rest(flow, b.middle, b.slope_c, grad_normal, b.low, b.hold, b.weights, b.grads, b.back_own)
+    back = Total(place, b.back_own, b.back_near, b.back_part, b.back_far, b.back_sums, totals, 2 * planes + chips)
+    back.start()
+    put_columns(b.weights, CONV, 0, dot_tn(b.active_c[...], b.low[...]))
+    back.turn()
+    queue.add(backs[1][1], backs[0][3], backs[1][2], backs[0][4], backs[1][3], backs[1][4])
+    queue.take()
+    back.finish()
+    queue.take()
+    conv_back_front(
+        b.sigma, b.gated, b.middle, grad_normal, b.front_sums, b.back_sums, b.padded, b.active1, b.hold, b.taps, b.small,
+        b.bounds, b.grads, b.gate_grads, frames, lambda i: queue.inside(i, 4, 12, 20, 28),
+    )
+    product_back(b.active1, b.normed_c, b.total, b.weights, GLU, 2, still)
+    queue.add(backs[2][0])
+    queue.take()
+    norm_back(b.x2, b.total, flow, flow, b.small, S_CONV, b.grads)
+    queue.add(backs[2][1], backs[2][2], backs[2][3], backs[2][4])
+    attention_backward(
+        flow, b.mixed, b.probs, b.joined, b.low, b.spread, b.active1, b.slope1.at[:, pl.ds(0, D)], b.hold, b.lines, b.weights,
+        b.choice, b.grads, b.table_grad, lambda index: queue.inside(index, 0, 1, 2, 3),
+    )
+    product_back(b.active1, b.normed_a, b.total, b.weights, QKV, 3, still)
+    queue.add(backs[3][0])
+    queue.take()
+    norm_back(b.x1, b.total, flow, flow, b.small, S_ATTN, b.grads)
+    queue.add(backs[3][1], backs[3][2], backs[3][3], backs[3][4])
+    feed_back_outer(
+        flow, b.active0, b.slope0, b.low, b.hold, b.weights, b.grads, b.inner_grads, 0, lambda c: queue.inside(c, 0, 2)
+    )
+    queue.add(backs[4][0])
+    product_back(b.slope0, b.normed0, b.total, b.weights, IN0, 4, lambda c: queue.inside(c, 0, 1, 3))
+    queue.add(backs[5][0], backs[4][1], backs[5][1], backs[4][2])
+    queue.take(2)
+    norm_back(x0, b.total, flow, b.grad_x.at[0], b.small, S_FFN, b.grads)
+    queue.take(2)
+    pack_small_grads(b, place)
+    queue.add(
+        thin[0], backs[5][2], thin[1], backs[4][3], thin[2], backs[5][3], backs[4][4], thin[3], backs[5][4], thin[4]
+    )
+    queue.drain()
+    reduces.sent()
+    totals.sent()
+
+
+def finish_kernel(*refs):
+    (
+        shard, thin, grad_ffn_norm, grad_ffn_in, grad_ffn_in_bias, grad_ffn_out, grad_ffn_out_bias, grad_attn_norm,
+        grad_qkv, grad_attn_out, grad_attn_out_bias, grad_rel, grad_conv_norm, grad_glu, grad_glu_bias, grad_depth, grad_batch,
+        grad_conv_out, grad_conv_out_bias, grad_final,
+    ) = refs
+    cut = lambda begin, size: shard[begin - IN0 : begin - IN0 + size, :]
+    width = grad_final.shape[-1]
+
+    def thin_rows(begin, count):
+        rows = []
+        for p in range(begin, begin + count):
+            rows.append(thin[p % 6 : p % 6 + 1, 16 * (p // 6) : 16 * (p // 6) + width])
+        return rows
+
+    for layer in range(2):
+        for c in range(FF // D):
+            grad_ffn_in[layer, :, D * c : D * c + D] = cut((IN0, IN1)[layer] + 16 * c, 16)
+        grad_ffn_out[layer] = cut((OUT0, OUT1)[layer], 64)
+        grad_ffn_in_bias[layer : layer + 1, :] = thin[6:7, 64 * layer : 64 * layer + 4 * width]
+        for r, row in enumerate(thin_rows(S_FFN + 2 * layer, 2)):
+            grad_ffn_norm[layer, r : r + 1, :] = row
+    for c in range(3):
+        grad_qkv[:, D * c : D * c + D] = cut(QKV + 16 * c, 16)
+    grad_attn_out[...] = cut(ATT, 16)
+    for c in range(2):
+        grad_glu[:, D * c : D * c + D] = cut(GLU + 16 * c, 16)
+    grad_conv_out[...] = cut(CONV, 16)
+    for ref, begin in (
+        (grad_ffn_out_bias, S_FOB), (grad_attn_norm, S_ATTN), (grad_conv_norm, S_CONV), (grad_batch, S_BATCH),
+        (grad_final, S_FINAL), (grad_depth, S_TAPS),
+    ):
+        for r, row in enumerate(thin_rows(begin, ref.shape[0])):
+            ref[r : r + 1, :] = row
+    grad_attn_out_bias[...] = thin_rows(S_AOB, 1)[0][0]
+    grad_conv_out_bias[...] = thin_rows(S_COB, 1)[0][0]
+    grad_glu_bias[...] = thin[7:8, 0 : 2 * width][0]
+    grad_rel[...] = thin[7:8, 64 : 64 + grad_rel.shape[0]][0]
+
+
+def shape(dims, kind=F32):
+    return jax.ShapeDtypeStruct(dims, kind)
+
+
+def local(*args):
+    planes, chips = lax.axis_size("dp"), lax.axis_size("fsdp") // 2
+    scratch = scratch_of(planes, chips)
+    names = INPUTS + OUTPUTS + tuple(scratch)
+    vmem = pl.BlockSpec(memory_space=pltpu.VMEM)
+    output, grad_x, shard, thin = pl.pallas_call(
+        lambda *refs: whole_kernel(names, *refs),
+        out_shape=[shape((1, L, D), BF16), shape((1, L, D)), shape((GRADS, D)), shape((8, 128))],
+        in_specs=[vmem] * len(args),
+        out_specs=[vmem] * 4,
+        scratch_shapes=list(scratch.values()),
+        compiler_params=pltpu.CompilerParams(collective_id=0, has_side_effects=True, vmem_limit_bytes=VMEM_BYTES),
+        name="layer",
+    )(*args)
+    given = dict(zip(INPUTS, args))
+    outs = [
+        shape(given[name].shape)
+        for name in (
+            "ffn_norm", "ffn_in", "ffn_in_bias", "ffn_out", "ffn_out_bias", "attn_norm", "qkv_weight", "attn_out",
+            "attn_out_bias", "rel_table", "conv_norm", "glu_weight", "glu_bias", "depth_kernel", "batch_norm", "conv_out",
+            "conv_out_bias", "final_norm",
+        )
+    ]
+    grads = pl.pallas_call(
+        finish_kernel, out_shape=outs, in_specs=[vmem] * 2, out_specs=[vmem] * len(outs), name="unpack",
+    )(shard, thin)
+    return (output, grad_x) + tuple(grads)
+
+
+VMEM_BYTES = 62 * 1024 * 1024
+
+
 highest = lax.Precision.HIGHEST
 
 
@@ -40,7 +1089,7 @@
     )
 
 
-def fetch_feed(norms, inner_weight, inner_bias, outer_weight, outer_bias, layer):
+def plain_fetch_feed(norms, inner_weight, inner_bias, outer_weight, outer_bias, layer):
     return (
         lax.all_gather(norms[layer], ("dp", "fsdp"), axis=1, tiled=True),
         lax.all_gather(inner_weight[layer], ("dp", "fsdp"), axis=0, tiled=True),
@@ -50,7 +1099,7 @@
     )
 
 
-def reduce_feed(grads):
+def plain_reduce_feed(grads):
     return (
         lax.psum_scatter(grads[0], ("dp", "fsdp"), scatter_dimension=1, tiled=True),
         lax.psum_scatter(grads[1], ("dp", "fsdp"), scatter_dimension=0, tiled=True),
@@ -85,7 +1134,7 @@
     )
 
 
-def feed_forward(values, weights):
+def plain_feed_forward(values, weights):
     norm, weight_in, bias_in, weight_out, bias_out = weights
     normed, norm_back = jax.vjp(layer_norm, values, norm.astype(jnp.float32))
     normed_low = normed.astype(jnp.bfloat16)
@@ -95,7 +1144,7 @@
     return (result, (normed_low, inner, active, norm_back))
 
 
-def feed_backward(upstream, weights, saved):
+def plain_feed_backward(upstream, weights, saved):
     norm, weight_in, bias_in, weight_out, bias_out = weights
     normed_low, inner, active, norm_back = saved
     branch = 0.5 * upstream
@@ -140,7 +1189,7 @@
     return jnp.where(same, raw * HEAD_DIM ** (-0.5) + bias_square(line, query.shape[0]), -1e30)
 
 
-def attention_forward(values, weights, marks, buckets):
+def plain_attention_forward(values, weights, marks, buckets):
     norm, mixer, weight_out, bias_out, table = weights
     length = values.shape[0]
     normed, norm_back = jax.vjp(layer_norm, values, norm.astype(jnp.float32))
@@ -169,7 +1218,7 @@
     return (result, (normed_low, mixed, lines, choose, same, joined, logsum, norm_back))
 
 
-def attention_backward(upstream, weights, saved):
+def plain_attention_backward(upstream, weights, saved):
     norm, mixer, weight_out, bias_out, table = weights
     normed_low, mixed, lines, choose, same, joined, logsum, norm_back = saved
     length = upstream.shape[0]
@@ -215,7 +1264,7 @@
     return joined[:, :width] * jax.nn.sigmoid(joined[:, width:])
 
 
-def depthwise(gated, kernel, marks):
+def plain_depthwise(gated, kernel, marks):
     length = gated.shape[0]
     half = kernel.shape[0] // 2
     padded = jnp.pad(gated, ((half, half), (0, 0)))
@@ -227,14 +1276,14 @@
     return total
 
 
-def conv_forward(values, weights, marks, frames):
+def plain_conv_forward(values, weights, marks, frames):
     norm, weight_glu, bias_glu, kernel, batch, weight_out, bias_out, final = weights
     normed, norm_back = jax.vjp(layer_norm, values, norm.astype(jnp.float32))
     normed_low = normed.astype(jnp.bfloat16)
     joined = product(normed_low, weight_glu) + bias_glu.astype(jnp.float32)
     gated, gate_back = jax.vjp(gate_unit, joined)
     middle, depth_back = jax.vjp(
-        lambda inner, taps: depthwise(inner, taps, marks), gated, kernel.astype(jnp.float32)
+        lambda inner, taps: plain_depthwise(inner, taps, marks), gated, kernel.astype(jnp.float32)
     )
     sums = lax.psum((jnp.sum(middle, axis=0), jnp.sum(middle * middle, axis=0)), ("dp", "fsdp"))
     center = sums[0] / frames
@@ -250,7 +1299,7 @@
     )
 
 
-def conv_backward(upstream, weights, saved, frames):
+def plain_conv_backward(upstream, weights, saved, frames):
     norm, weight_glu, bias_glu, kernel, batch, weight_out, bias_out, final = weights
     normed_low, gate_back, depth_back, inverse, gain, unit, normal, active, norm_back = saved
     upstream_low = upstream.astype(jnp.bfloat16)
@@ -282,7 +1331,7 @@
     )
 
 
-def local(
+def plain(
     inputs,
     segments,
     buckets,
@@ -310,10 +1359,10 @@
     marks = segments[0]
     devices = lax.axis_size(("dp", "fsdp"))
     frames = values.shape[0] * devices
-    feed_first = fetch_feed(ffn_norm, ffn_in, ffn_in_bias, ffn_out, ffn_out_bias, 0)
-    first, first_saved = feed_forward(values, feed_first)
+    feed_first = plain_fetch_feed(ffn_norm, ffn_in, ffn_in_bias, ffn_out, ffn_out_bias, 0)
+    first, first_saved = plain_feed_forward(values, feed_first)
     attn_weights = fetch_attention(attn_norm, qkv_weight, attn_out, attn_out_bias, rel_table)
-    second, attn_saved = attention_forward(first, attn_weights, marks, buckets)
+    second, attn_saved = plain_attention_forward(first, attn_weights, marks, buckets)
     conv_weights = fetch_conv(
         conv_norm,
         glu_weight,
@@ -324,13 +1373,13 @@
         conv_out_bias,
         final_norm,
     )
-    third, conv_saved = conv_forward(second, conv_weights, marks, frames)
-    feed_second = fetch_feed(ffn_norm, ffn_in, ffn_in_bias, ffn_out, ffn_out_bias, 1)
-    fourth, second_saved = feed_forward(third, feed_second)
+    third, conv_saved = plain_conv_forward(second, conv_weights, marks, frames)
+    feed_second = plain_fetch_feed(ffn_norm, ffn_in, ffn_in_bias, ffn_out, ffn_out_bias, 1)
+    fourth, second_saved = plain_feed_forward(third, feed_second)
     result, final_back = jax.vjp(layer_norm, fourth, conv_weights[7].astype(jnp.float32))
     grad_fourth, grad_final = final_back(cotangent[0].astype(jnp.float32))
-    second_back = fetch_feed(ffn_norm, ffn_in, ffn_in_bias, ffn_out, ffn_out_bias, 1)
-    grad_third, second_grads = feed_backward(grad_fourth, second_back, second_saved)
+    second_back = plain_fetch_feed(ffn_norm, ffn_in, ffn_in_bias, ffn_out, ffn_out_bias, 1)
+    grad_third, second_grads = plain_feed_backward(grad_fourth, second_back, second_saved)
     conv_back = fetch_conv(
         conv_norm,
         glu_weight,
@@ -341,13 +1390,13 @@
         conv_out_bias,
         final_norm,
     )
-    grad_second, conv_grads, grad_batch = conv_backward(grad_third, conv_back, conv_saved, frames)
+    grad_second, conv_grads, grad_batch = plain_conv_backward(grad_third, conv_back, conv_saved, frames)
     attn_back = fetch_attention(attn_norm, qkv_weight, attn_out, attn_out_bias, rel_table)
-    grad_first, attn_grads = attention_backward(grad_second, attn_back, attn_saved)
-    first_back = fetch_feed(ffn_norm, ffn_in, ffn_in_bias, ffn_out, ffn_out_bias, 0)
-    grad_start, first_grads = feed_backward(grad_first, first_back, first_saved)
-    first_shards = reduce_feed(first_grads)
-    second_shards = reduce_feed(second_grads)
+    grad_first, attn_grads = plain_attention_backward(grad_second, attn_back, attn_saved)
+    first_back = plain_fetch_feed(ffn_norm, ffn_in, ffn_in_bias, ffn_out, ffn_out_bias, 0)
+    grad_start, first_grads = plain_feed_backward(grad_first, first_back, first_saved)
+    first_shards = plain_reduce_feed(first_grads)
+    second_shards = plain_reduce_feed(second_grads)
     attn_shards = (
         lax.psum_scatter(attn_grads[0], ("dp", "fsdp"), scatter_dimension=1, tiled=True),
         lax.psum_scatter(attn_grads[1], ("dp", "fsdp"), scatter_dimension=0, tiled=True),
@@ -439,4 +1488,5 @@
         P(("dp", "fsdp")),
         P(None, ("dp", "fsdp")),
     )
-    return jax.shard_map(local, mesh=mesh, in_specs=in_specs, out_specs=out_specs, check_vma=False)
+    fast = mesh.shape["dp"] == 4 and mesh.shape["fsdp"] == 8
+    return jax.shard_map(local if fast else plain, mesh=mesh, in_specs=in_specs, out_specs=out_specs, check_vma=False)

time: 2700 us -> 239 us (0.09)
  waiting for transfers between devices: 1630 us -> 0 us
  blocking collectives: 515 us -> 0 us
  local copies, waits for them, and re-layouts: 280 us -> 5.59 us
  Pallas kernels: 0 us -> 233 us
  matrix products: 156 us -> 0 us
  other arithmetic: 88.9 us -> 0 us
    reduce_scatter x8 -> x0, waiting for transfers between devices: 1070 us -> none  [the longest x2 282 us: reduce_feed(): lax.psum_scatter(grads[3], ('dp', 'fsdp'), scatter_dimension=0, tiled=True)]
    unnamed x26 -> x0, waiting for transfers between devices: 560 us -> none
    all_gather x9 -> x0, blocking collectives: 356 us -> none  [the longest x2 77.5 us: fetch_feed(): lax.all_gather(norms[layer], ('dp', 'fsdp'), axis=1, tiled=True)]
    pallas_call x0 -> x2, Pallas kernels: none -> 233 us  [the longest x1 230 us: local(): pl.pallas_call(lambda *refs: whole_kernel(names, *refs), out_shape=[shape...]
    dot_general x82 -> x0, matrix products: 156 us -> none  [the longest x24 53.6 us: product(): return jnp.dot(left, right, preferred_element_type=jnp.float32)]
    reshape x43 -> x0, local copies, waits for them, and re-layouts: 95.9 us -> none  [the longest x16 44.7 us: bias_square(): tiled = jnp.broadcast_to(line, (length, 2 * length - 1)).reshape(-1)]
    unnamed x2 -> x0, blocking collectives: 79.4 us -> none
    psum x2 -> x0, blocking collectives: 79.1 us -> none  [the longest x1 41 us: conv_backward(): lax.psum((jnp.sum(grad_normal, axis=0), jnp.sum(grad_normal * unit, axis=...]
  transfers between devices with their start and end apart: 20 -> 0, of which waited for: 13 -> 0; matrix products, arithmetic and copies ran while one was open for 17% -> 0% of each run, Pallas kernels for 0% -> 0%
where the time goes in v2:
time: 239 us
  Pallas kernels  233 us (97%)
  local copies, waits for them, and re-layouts  5.59 us (2%)
    pallas_call x1, Pallas kernels, local(): pl.pallas_call(lambda *refs: whole_kernel(names, *refs), out_shape=[shape...  230 us
    unnamed x6, local copies, waits for them, and re-layouts  5.59 us

profile of v2, /device:TPU:0, one launch (start us, length us, event | category | flops | bytes accessed | tf_op | source)
XLA Modules:
  0.0 238.9 jit_solution(9050454674740595754)
XLA Ops:
  0.7 1.4 copy.42.refs_17_
  2.0 230.4 %layer.1 = (bf16[1,512,512]{2,1,0:T(8,128)(2,1)}, f32[1,512,512]{2,1,0:T(8,128)}, f32[368,512]{1,0:T(8,128)}, f32[8,128]{1,0:T(8,128)}) custom-call(bf16[1,512,512]{2,1,0:T(8,128)(2,1)} %refs_0_.1, s32[1,512]{1,0:T(1,128)} %refs_1_.1, s32[1023]{0:T(1024)} %refs_2_.1, bf16[1,512,512]{2,1,0:T(8,128)(2,1)} %refs_3_.1, bf16[2,2,16]{2,1,0:T(2,128)(2,1)} %refs_4_.1, ...), custom_call_target="tpu_custom_call" | custom-call | tf_op jit(solution)/shard_map/layer/pallas_call | solution.py:1035
  232.5 0.0 copy-start
  232.5 2.2 unpack.1
  234.6 1.4 copy.43
  236.0 1.9 copy.46
  237.9 0.0 copy-done
  237.9 1.0 copy.47
Async XLA Ops:
  232.5 5.4 %copy-start = (f32[1,512,512]{2,1,0:T(8,128)S(1)}, f32[1,512,512]{2,1,0:T(8,128)}, u32[]{:S(2)}) copy-start(f32[1,512,512]{2,1,0:T(8,128)} %get-tuple-element.105) | copy-start | bytes 3145732

commit v3 on v2

--- a/solution.py
+++ b/solution.py
@@ -108,47 +108,72 @@
         self.begun = []
 
 
-def gather_steps(place, weights, copies, first, begin, size, split):
-    p, core, chips = place, place.core, place.chips
-    rows = pl.ds(begin, size)
-    parts = (pl.ds(begin, split), pl.ds(begin + split, size - split))
-
-    def column(plane, side, which):
-        return weights.at[plane, :, side, which]
-
-    def move(number, ref, device):
-        copies.start(first + number, lambda: (ref(), ref(), device))
-
-    def along_z():
-        for d in range(1, chips):
-            move(d - 1, lambda: weights.at[p.plane, p.z, core, rows], p.along[d])
-
-    def own_column():
-        for d in range(1, chips):
-            copies.arrived(first + d - 1, weights.at[p.plane, p.chip[chips - d], core, rows])
-        own = lambda: column(p.plane, core, rows)
-        move(chips - 1, own, p.over_x)
-        move(chips, own, p.over_y)
-        move(chips + 3, own, p.twin)
-
-    def beside():
-        copies.arrived(first + chips - 1, column(p.plane_x, core, rows))
-        move(chips + 1, lambda: column(p.plane_x, core, parts[0]), p.over_y)
-        copies.arrived(first + chips, column(p.plane_y, core, rows))
-        move(chips + 2, lambda: column(p.plane_y, core, parts[1]), p.over_x)
-        move(chips + 4, lambda: column(p.plane_x, core, rows), p.twin)
-        move(chips + 5, lambda: column(p.plane_y, core, rows), p.twin)
-
-    def across():
-        copies.arrived(first + chips + 1, column(p.plane_d, core, parts[0]))
-        copies.arrived(first + chips + 2, column(p.plane_d, core, parts[1]))
-        move(chips + 6, lambda: column(p.plane_d, core, rows), p.twin)
-
-    def twins():
+class Gather:
+    def __init__(self, place, weights, copies, first, begin, size, split):
+        self.place, self.weights, self.copies, self.first = place, weights, copies, first
+        self.rows = pl.ds(begin, size)
+        self.parts = (pl.ds(begin, split), pl.ds(begin + split, size - split))
+        chips = place.chips
+        self.x, self.y, self.d, self.t = chips, 2 * chips, 3 * chips, 3 * chips + 2
+
+    @staticmethod
+    def semaphores(chips):
+        return 3 * chips + 6
+
+    def column(self, plane, side, which):
+        return self.weights.at[plane, :, side, which]
+
+    def slot(self, plane, step):
+        p = self.place
+        return self.weights.at[plane, p.chip[(p.chips - step) % p.chips], p.core, self.rows]
+
+    def move(self, number, ref, device):
+        self.copies.start(self.first + number, lambda: (ref(), ref(), device))
+
+    def arrived(self, number, ref):
+        self.copies.arrived(self.first + number, ref)
+
+    def along_z(self):
+        p = self.place
+        for d in range(1, p.chips):
+            self.move(d, lambda: self.slot(p.plane, 0), p.along[d])
+
+    def beside(self, step):
+        p = self.place
+        self.move(self.x + step, lambda: self.slot(p.plane, step), p.over_x)
+        self.move(self.y + step, lambda: self.slot(p.plane, step), p.over_y)
+
+    def own(self):
+        self.beside(0)
+
+    def forward(self):
+        p = self.place
+        for d in range(1, p.chips):
+            self.arrived(d, self.slot(p.plane, d))
+            self.beside(d)
+        self.move(self.t, lambda: self.column(p.plane, p.core, self.rows), p.twin)
+
+    def turn(self):
+        p = self.place
+        for d in range(p.chips):
+            self.arrived(self.x + d, self.slot(p.plane_x, d))
+        self.move(self.d, lambda: self.column(p.plane_x, p.core, self.parts[0]), p.over_y)
+        for d in range(p.chips):
+            self.arrived(self.y + d, self.slot(p.plane_y, d))
+        self.move(self.d + 1, lambda: self.column(p.plane_y, p.core, self.parts[1]), p.over_x)
+        self.move(self.t + 1, lambda: self.column(p.plane_x, p.core, self.rows), p.twin)
+        self.move(self.t + 2, lambda: self.column(p.plane_y, p.core, self.rows), p.twin)
+
+    def across(self):
+        p = self.place
+        self.arrived(self.d, self.column(p.plane_d, p.core, self.parts[0]))
+        self.arrived(self.d + 1, self.column(p.plane_d, p.core, self.parts[1]))
+        self.move(self.t + 3, lambda: self.column(p.plane_d, p.core, self.rows), p.twin)
+
+    def done(self):
+        p = self.place
         for number, plane in enumerate((p.plane, p.plane_x, p.plane_y, p.plane_d)):
-            copies.arrived(first + chips + 3 + number, column(plane, 1 - core, rows))
-
-    return [along_z, own_column, beside, across, twins]
+            self.arrived(self.t + number, self.column(plane, 1 - p.core, self.rows))
 
 
 def reduce_steps(place, data, twin, diagonal, from_x, from_y, from_z, copies, first, begin, size, split, landing, finish):
@@ -221,6 +246,43 @@
     return [to_twin, across, beside, own_column, along_z]
 
 
+class Thin:
+    def __init__(self, place, tiles, near, part, far, result, copies, first):
+        self.place, self.tiles, self.near, self.part, self.far, self.result = place, tiles, near, part, far, result
+        self.copies, self.first = copies, first
+
+    def start(self):
+        p = self.place
+        for i, (device, rank) in enumerate(p.members):
+            self.copies.start(
+                self.first + i,
+                lambda device=device: (self.tiles.at[device[0], :, lax.rem(device[1], 2)], self.near.at[p.rank], device),
+                self.first + p.rank,
+            )
+        self.near[p.rank] = self.tiles[p.plane, :, p.core]
+
+    def turn(self):
+        p = self.place
+        for device, rank in p.members:
+            self.copies.arrived(self.first + rank, self.near.at[rank])
+        value = self.near[0]
+        for i in range(1, 2 * p.planes):
+            value = value + self.near[i]
+        self.part[...] = value
+        base = self.first + 2 * p.planes
+        for d in range(1, p.chips):
+            self.copies.start(base + d, lambda d=d: (self.part.at[p.chip[d]], self.far.at[d], p.along[d]))
+
+    def finish(self):
+        p = self.place
+        base = self.first + 2 * p.planes
+        value = self.part[p.z]
+        for d in range(1, p.chips):
+            self.copies.arrived(base + d, self.far.at[d])
+            value = value + self.far[d]
+        self.result[...] = value
+
+
 class Total:
     def __init__(self, place, own, near, part, far, result, copies, first):
         self.place, self.own, self.near, self.part, self.far, self.result = place, own, near, part, far, result
@@ -255,29 +317,21 @@
         self.result[...] = value
 
 
-class Queue:
-    def __init__(self):
-        self.steps, self.taken = [], 0
-
-    def add(self, *steps):
-        self.steps += steps
-
-    def take(self, count=1):
-        for step in self.steps[self.taken : self.taken + count]:
-            step()
-        self.taken = min(len(self.steps), self.taken + count)
-
-    def until(self, step):
-        self.take(self.steps.index(step) + 1 - self.taken)
-
-    def drain(self):
-        self.take(len(self.steps) - self.taken)
-
-    def inside(self, index, *at):
-        for i in at:
-            if self.taken < len(self.steps):
-                pl.when(index == i)(self.steps[self.taken])
-                self.taken += 1
+def at_points(table):
+    def pump(index, place=0):
+        for (iteration, where), steps in table.items():
+            if where == place:
+
+                @pl.when(index == iteration)
+                def _(steps=steps):
+                    for step in steps:
+                        step()
+
+    return pump
+
+
+def still(index, place=0):
+    pass
 
 
 def standard(values):
@@ -342,6 +396,7 @@
     norm_rows(source, normed, small, S_FFN + 2 * layer)
 
     def block(c, carry):
+        pump(c)
         cols = block_cols(c)
         hold[...] = dot(normed[...], columns(weights, (IN0, IN1)[layer], c))
         bias = inner_bias[layer : layer + 1, cols]
@@ -355,7 +410,6 @@
             return carry
 
         chunks(body, 0)
-        pump(c)
         return carry
 
     lax.fori_loop(0, FF // D, block, 0)
@@ -387,9 +441,7 @@
     chunks(body, 0)
 
 
-def feed_back_outer(upstream, active, slope, low, hold, weights, grads, inner_grads, layer, pump):
-    begin = (OUT0, OUT1)[layer]
-
+def feed_back_start(upstream, low, grads, layer):
     def start(rows, carry):
         half = 0.5 * upstream[rows, :]
         low[rows, :] = half.astype(BF16)
@@ -397,6 +449,19 @@
 
     grads[S_FOB + layer : S_FOB + layer + 1, :] = total_row(chunks(start, zeros8()))
 
+
+def feed_back_outer(active, low, weights, begin, pump):
+    def block(c, carry):
+        put_lines(weights, begin, c, dot_tn(active[:, block_cols(c)], low[...]))
+        pump(c)
+        return carry
+
+    lax.fori_loop(0, FF // D, block, 0)
+
+
+def feed_back_inner(normed, slope, low, hold, weights, target, inner_grads, layer, pump):
+    begin = (OUT0, OUT1)[layer]
+
     def block(c, carry):
         cols = block_cols(c)
         hold[...] = dot_nt(low[...], lines_of(weights, begin, c))
@@ -407,7 +472,8 @@
             return carry + fold(grad)
 
         inner_grads[layer : layer + 1, cols] = total_row(chunks(body, zeros8()))
-        put_lines(weights, begin, c, dot_tn(active[:, cols], low[...]))
+        if target is not None:
+            put_columns(weights, target, c, dot_tn(normed[...], slope[:, cols]))
         pump(c)
         return carry
 
@@ -427,7 +493,8 @@
         def _():
             total[...] += part
 
-        put_columns(weights, begin, c, dot_tn(normed[...], grad[:, cols]))
+        if normed is not None:
+            put_columns(weights, begin, c, dot_tn(normed[...], grad[:, cols]))
         pump(c)
         return carry
 
@@ -474,7 +541,7 @@
                 probs[head, rows, :] = share
                 parts.append(dot(share, contents))
             joined[rows, pl.ds(begin, 128)] = jnp.where(lane < HEAD_DIM, parts[0], parts[1]).astype(BF16)
-        pump(index)
+            pump(index, block)
         return carry
 
     lax.fori_loop(0, HEADS // 2, pair, 0)
@@ -488,9 +555,7 @@
     chunks(body, 0)
 
 
-def attention_backward(
-    upstream, mixed, probs, joined, low, spread, grad_mixed, scaled, hold, lines, weights, buckets, grads, table_grad, pump
-):
+def attention_back_start(upstream, joined, low, spread, weights, grads):
     def start(rows, carry):
         given = upstream[rows, :]
         low[rows, :] = given.astype(BF16)
@@ -499,6 +564,9 @@
     grads[S_AOB : S_AOB + 1, :] = total_row(chunks(start, zeros8()))
     spread[...] = dot_nt(low[...], columns(weights, ATT, 0)).astype(BF16)
     put_columns(weights, ATT, 0, dot_tn(joined[...], low[...]))
+
+
+def attention_backward(mixed, probs, spread, grad_mixed, scaled, hold, lines, buckets, table_grad, pump):
     lane = lax.broadcasted_iota(jnp.int32, (1, 128), 1)
     row8 = lax.broadcasted_iota(jnp.int32, (8, 2 * L), 0)
     size = 128
@@ -537,10 +605,10 @@
                 line += jnp.where(row8 == r, pltpu.roll(sums, 7 - r, 1), 0.0)
             lines[pl.ds(head, 1), :] = total_row(line)
             parts.append((dot(scaled[...], keys), dot_tn(scaled[...], query), dot_tn(probs[head], incoming)))
+            pump(index, half)
         for third in range(3):
             merged = jnp.where(lane < HEAD_DIM, parts[0][third], parts[1][third])
             grad_mixed[:, pl.ds(third * D + begin, 128)] = merged.astype(BF16)
-        pump(index)
         return carry
 
     lax.fori_loop(0, HEADS // 2, pair, 0)
@@ -715,10 +783,18 @@
 )
 
 
+def turned(value):
+    rows, lanes = value.shape
+    value = jnp.concatenate([value, jnp.zeros((rows, 128 - lanes), F32)], axis=1)
+    return jnp.concatenate([value, jnp.zeros((128 - rows, 128), F32)], axis=0).T[:lanes, :rows]
+
+
 def pack_small(b, tile):
     tile[...] = jnp.zeros_like(tile)
     for name, row in THIN:
         value = getattr(b, name)[...].astype(F32)
+        if name == "depth_kernel":
+            value = turned(value)
         value = value.reshape(-1, value.shape[-1])
         for r in range(0, value.shape[0], 16):
             part = value[r : r + 16]
@@ -781,8 +857,11 @@
     "conv_out", "conv_out_bias", "final_norm",
 )
 OUTPUTS = ("output", "grad_x", "shard", "thin")
-GATHERS = ((0, 80, 48), (80, 64, 32), (144, 112, 64), (256, 128, 64))
-REDUCES = ((OUT1, 64, 32), (IN1, 64, 32), (GLU, 48, 32), (QKV, 64, 32), (OUT0, 64, 32), (IN0, 64, 32))
+GATHERS = ((SMALL, 48, 32), (IN0 + 32, 32, 16), (OUT0, 64, 32), (QKV, 64, 32), (GLU, 48, 32), (IN1, 64, 32), (OUT1, 64, 32))
+REDUCES = (
+    (OUT1, OUT1, 64, 32), (IN1, IN1, 64, 32), (ATT, ATT, 64, 32), (QKV, QKV, 48, 32), (OUT1, OUT0, 64, 32),
+    (IN1, IN0, 32, 16), (IN1 + 32, IN0 + 32, 32, 16),
+)
 
 
 def scratch_of(planes, chips):
@@ -797,11 +876,9 @@
         from_y=pltpu.VMEM((chips, GRADS, D), BF16),
         from_z=pltpu.VMEM((chips - 1, GRADS, D), BF16),
         edges=pltpu.VMEM((planes, chips, 2, 8, 128), F32),
-        edge_twin=pltpu.VMEM((planes, chips, 8, 128), F32),
-        edge_diagonal=pltpu.VMEM((chips, 8, 128), F32),
-        edge_x=pltpu.VMEM((chips, 8, 128), F32),
-        edge_y=pltpu.VMEM((chips, 8, 128), F32),
-        edge_z=pltpu.VMEM((chips - 1, 8, 128), F32),
+        edge_near=pltpu.VMEM((2 * planes, chips, 8, 128), F32),
+        edge_part=pltpu.VMEM((chips, 8, 128), F32),
+        edge_far=pltpu.VMEM((chips, 8, 128), F32),
         small=pltpu.VMEM((S_ROWS, D), F32),
         inner_bias=pltpu.VMEM((2, FF), F32),
         gate_bias=pltpu.VMEM((1, 2 * D), F32),
@@ -822,12 +899,12 @@
         active0=big, slope0=big, active1=big, slope1=big, mixed=pltpu.VMEM((L, 3 * D), BF16),
         probs=pltpu.VMEM((HEADS, L, L), BF16), joined=low, sigma=wide, gated=pads, middle=wide, active_c=low, slope_c=low,
         padded=pads, low=low, spread=low, hold=wide, total=wide, taps=pltpu.VMEM((TAPS, 8, D), F32),
-        gather_sends=pltpu.SemaphoreType.DMA((len(GATHERS) * (chips + 7),)),
-        gather_receives=pltpu.SemaphoreType.DMA((len(GATHERS) * (chips + 7),)),
-        reduce_sends=pltpu.SemaphoreType.DMA(((len(REDUCES) + 1) * (chips + 7),)),
-        reduce_receives=pltpu.SemaphoreType.DMA(((len(REDUCES) + 1) * (chips + 7),)),
-        total_sends=pltpu.SemaphoreType.DMA((2 * (2 * planes + chips),)),
-        total_receives=pltpu.SemaphoreType.DMA((2 * (2 * planes + chips),)),
+        gather_sends=pltpu.SemaphoreType.DMA((len(GATHERS) * Gather.semaphores(chips),)),
+        gather_receives=pltpu.SemaphoreType.DMA((len(GATHERS) * Gather.semaphores(chips),)),
+        reduce_sends=pltpu.SemaphoreType.DMA((len(REDUCES) * (chips + 7),)),
+        reduce_receives=pltpu.SemaphoreType.DMA((len(REDUCES) * (chips + 7),)),
+        total_sends=pltpu.SemaphoreType.DMA((3 * (2 * planes + chips),)),
+        total_receives=pltpu.SemaphoreType.DMA((3 * (2 * planes + chips),)),
     )
 
 
@@ -853,48 +930,52 @@
 
     gathers = Copies(b.gather_sends, b.gather_receives, place)
     rounds = [
-        gather_steps(place, b.weights, gathers, i * (chips + 7), begin, size, split)
+        Gather(place, b.weights, gathers, i * Gather.semaphores(chips), begin, size, split)
         for i, (begin, size, split) in enumerate(GATHERS)
     ]
-    queue = Queue()
-    queue.add(
-        rounds[0][0], rounds[1][0], rounds[0][1], rounds[0][2], rounds[1][1], rounds[2][0], rounds[0][3], rounds[1][2],
-        rounds[0][4],
-    )
-    queue.add(
-        rounds[2][1], rounds[1][3], rounds[3][0], rounds[1][4], rounds[2][2], rounds[3][1], rounds[2][3], rounds[2][4],
-        rounds[3][2], rounds[3][3], rounds[3][4],
-    )
-    still = lambda index: None
-    queue.take(2)
+    r0, r1, r2, r3, r4, r5, r6 = rounds
+    r0.along_z()
+    r0.own()
+    r1.along_z()
+    r1.own()
+    for r in rounds[2:]:
+        r.along_z()
     b.marks[...] = b.segments[...].astype(F32)
     b.bounds[...] = jnp.full(b.bounds.shape, -1.0, F32)
     b.bounds[PAD : PAD + L, :] = jnp.broadcast_to(b.marks[...], (128, L)).T
     b.choice[...] = jnp.full(b.choice.shape, -1, jnp.int32)
     b.choice[:, 0 : 2 * L - 1] = b.buckets[...].reshape(1, 2 * L - 1)
-    queue.until(rounds[0][4])
+    for step in (r0.forward, r1.forward, r2.own, r0.turn, r1.turn, r2.forward, r3.own, r0.across, r0.done):
+        step()
     unpack_small(b, place)
 
     x0 = b.inputs.at[0]
     feed_inner(
-        x0, b.normed0, b.active0, b.slope0, b.hold, b.weights, b.small, b.inner_bias, 0, lambda c: queue.inside(c, 0, 1, 2)
-    )
-    queue.until(rounds[1][4])
+        x0, b.normed0, b.active0, b.slope0, b.hold, b.weights, b.small, b.inner_bias, 0,
+        at_points({(1, 0): (r1.across, r2.turn), (2, 0): (r1.done, r3.forward), (3, 0): (r4.own,)}),
+    )
+    r2.across()
+    r2.done()
     feed_outer(x0, b.active0, b.x1, b.hold, b.weights, b.small, 0)
-    queue.until(rounds[2][4])
+    for step in (r4.forward, r3.turn, r5.own, r5.forward, r3.across, r3.done):
+        step()
     attention_mix(b.x1, b.normed_a, b.mixed, b.weights, b.small)
+    for step in (r4.turn, r6.own, r6.forward):
+        step()
     attention_forward(
         b.x1, b.mixed, b.probs, b.joined, b.x2, b.lines, b.hold, b.weights, b.small, b.table, b.choice, b.bounds, b.marks,
-        lambda index: queue.inside(index, 0, 1, 2),
+        at_points({(2, 1): (r5.turn,), (2, 3): (r4.across,), (3, 3): (r4.done,)}),
     )
     conv_front(
-        b.x2, b.normed_c, b.sigma, b.gated, b.middle, b.front_own, b.hold, b.weights, b.small, b.gate_bias, b.bounds, still
+        b.x2, b.normed_c, b.sigma, b.gated, b.middle, b.front_own, b.hold, b.weights, b.small, b.gate_bias, b.bounds,
+        at_points({(4, 0): (r6.turn,), (16, 0): (r5.across,), (28, 0): (r6.across,)}),
     )
     totals = Copies(b.total_sends, b.total_receives, place)
     front = Total(place, b.front_own, b.front_near, b.front_part, b.front_far, b.front_sums, totals, 0)
     front.start()
-    queue.drain()
+    r5.done()
     front.turn()
+    r6.done()
     front.finish()
     conv_rest(b.x2, b.middle, b.front_sums, b.middle, b.active_c, b.slope_c, b.x3, b.hold, b.weights, b.small, frames)
     feed_inner(b.x3, b.normed1, b.active1, b.slope1, b.hold, b.weights, b.small, b.inner_bias, 1, still)
@@ -915,80 +996,79 @@
 
     backs = [
         reduce_steps(
-            place, b.weights, *landings, reduces, i * (chips + 7), begin, size, split, begin - IN0, finish(begin, size)
+            place, b.weights, *landings, reduces, i * (chips + 7), begin, size, split, owner - IN0, finish(owner, size)
         )
-        for i, (begin, size, split) in enumerate(REDUCES)
+        for i, (begin, owner, size, split) in enumerate(REDUCES)
     ]
-
-    def finish_thin(value):
-        b.thin[...] = value
-
-    thin = reduce_steps(
-        place, b.edges, b.edge_twin, b.edge_diagonal, b.edge_x, b.edge_y, b.edge_z, reduces, len(REDUCES) * (chips + 7),
-        0, 8, 8, 0, finish_thin,
-    )
-    queue = Queue()
-    feed_back_outer(flow, b.active1, b.slope1, b.low, b.hold, b.weights, b.grads, b.inner_grads, 1, still)
-    queue.add(backs[0][0])
-    queue.take()
-    queue.add(backs[0][1])
-    product_back(b.slope1, b.normed1, b.total, b.weights, IN1, 4, lambda c: queue.inside(c, 2))
-    queue.add(backs[1][0], backs[0][2])
-    queue.take()
+    out1, in1, conv, mix, out0, in0, in0_end = backs
+    feed_back_start(flow, b.low, b.grads, 1)
+    feed_back_inner(b.normed1, b.slope1, b.low, b.hold, b.weights, None, b.inner_grads, 1, still)
+    feed_back_outer(b.active1, b.low, b.weights, OUT1, still)
+    out1[0]()
+    product_back(b.slope1, b.normed1, b.total, b.weights, IN1, 4, at_points({(1, 0): (out1[1],)}))
+    in1[0]()
     norm_back(b.x3, b.total, flow, flow, b.small, S_FFN + 2, b.grads)
-    queue.take()
+    in1[1]()
     grad_normal = b.x3
     conv_back_rest(flow, b.middle, b.slope_c, grad_normal, b.low, b.hold, b.weights, b.grads, b.back_own)
     back = Total(place, b.back_own, b.back_near, b.back_part, b.back_far, b.back_sums, totals, 2 * planes + chips)
     back.start()
     put_columns(b.weights, CONV, 0, dot_tn(b.active_c[...], b.low[...]))
+    out1[2]()
     back.turn()
-    queue.add(backs[1][1], backs[0][3], backs[1][2], backs[0][4], backs[1][3], backs[1][4])
-    queue.take()
+    in1[2]()
     back.finish()
-    queue.take()
     conv_back_front(
         b.sigma, b.gated, b.middle, grad_normal, b.front_sums, b.back_sums, b.padded, b.active1, b.hold, b.taps, b.small,
-        b.bounds, b.grads, b.gate_grads, frames, lambda i: queue.inside(i, 4, 12, 20, 28),
-    )
+        b.bounds, b.grads, b.gate_grads, frames, at_points({(10, 0): (out1[3],), (26, 0): (in1[3],)}),
+    )
+    out1[4]()
     product_back(b.active1, b.normed_c, b.total, b.weights, GLU, 2, still)
-    queue.add(backs[2][0])
-    queue.take()
     norm_back(b.x2, b.total, flow, flow, b.small, S_CONV, b.grads)
-    queue.add(backs[2][1], backs[2][2], backs[2][3], backs[2][4])
+    attention_back_start(flow, b.joined, b.low, b.spread, b.weights, b.grads)
+    conv[0]()
     attention_backward(
-        flow, b.mixed, b.probs, b.joined, b.low, b.spread, b.active1, b.slope1.at[:, pl.ds(0, D)], b.hold, b.lines, b.weights,
-        b.choice, b.grads, b.table_grad, lambda index: queue.inside(index, 0, 1, 2, 3),
+        b.mixed, b.probs, b.spread, b.active1, b.slope1.at[:, pl.ds(0, D)], b.hold, b.lines, b.choice, b.table_grad,
+        at_points({(0, 1): (conv[1], in1[4]), (2, 0): (conv[2],), (3, 1): (conv[3],)}),
     )
     product_back(b.active1, b.normed_a, b.total, b.weights, QKV, 3, still)
-    queue.add(backs[3][0])
-    queue.take()
+    mix[0]()
     norm_back(b.x1, b.total, flow, flow, b.small, S_ATTN, b.grads)
-    queue.add(backs[3][1], backs[3][2], backs[3][3], backs[3][4])
-    feed_back_outer(
-        flow, b.active0, b.slope0, b.low, b.hold, b.weights, b.grads, b.inner_grads, 0, lambda c: queue.inside(c, 0, 2)
-    )
-    queue.add(backs[4][0])
-    product_back(b.slope0, b.normed0, b.total, b.weights, IN0, 4, lambda c: queue.inside(c, 0, 1, 3))
-    queue.add(backs[5][0], backs[4][1], backs[5][1], backs[4][2])
-    queue.take(2)
+    mix[1]()
+    conv[4]()
+    reduces.sent()
+    feed_back_start(flow, b.low, b.grads, 0)
+    feed_back_outer(b.active0, b.low, b.weights, OUT1, still)
+    out0[0]()
+    feed_back_inner(
+        b.normed0, b.slope0, b.low, b.hold, b.weights, IN1, b.inner_grads, 0,
+        at_points({(0, 0): (mix[2],), (1, 0): (in0[0], out0[1]), (2, 0): (in0[1],)}),
+    )
+    in0_end[0]()
+    out0[2]()
+    product_back(b.slope0, None, b.total, b.weights, IN0, 4, at_points({(1, 0): (in0_end[1], mix[3])}))
+    in0[2]()
     norm_back(x0, b.total, flow, b.grad_x.at[0], b.small, S_FFN, b.grads)
-    queue.take(2)
     pack_small_grads(b, place)
-    queue.add(
-        thin[0], backs[5][2], thin[1], backs[4][3], thin[2], backs[5][3], backs[4][4], thin[3], backs[5][4], thin[4]
-    )
-    queue.drain()
+    thin = Thin(place, b.edges, b.edge_near, b.edge_part, b.edge_far, b.thin, totals, 2 * (2 * planes + chips))
+    thin.start()
+    for step in (in0_end[2], out0[3], mix[4], thin.turn, in0[3], in0_end[3], out0[4], thin.finish, in0[4], in0_end[4]):
+        step()
     reduces.sent()
     totals.sent()
 
 
 def finish_kernel(*refs):
     (
-        shard, thin, grad_ffn_norm, grad_ffn_in, grad_ffn_in_bias, grad_ffn_out, grad_ffn_out_bias, grad_attn_norm,
-        grad_qkv, grad_attn_out, grad_attn_out_bias, grad_rel, grad_conv_norm, grad_glu, grad_glu_bias, grad_depth, grad_batch,
-        grad_conv_out, grad_conv_out_bias, grad_final,
+        output_in, grad_x_in, shard, thin, output, grad_x, grad_ffn_norm, grad_ffn_in, grad_ffn_in_bias, grad_ffn_out,
+        grad_ffn_out_bias, grad_attn_norm, grad_qkv, grad_attn_out, grad_attn_out_bias, grad_rel, grad_conv_norm, grad_glu,
+        grad_glu_bias, grad_depth, grad_batch, grad_conv_out, grad_conv_out_bias, grad_final, taps, semaphores,
     ) = refs
+    copies = [
+        pltpu.make_async_copy(output_in, output, semaphores.at[0]), pltpu.make_async_copy(grad_x_in, grad_x, semaphores.at[1])
+    ]
+    for copy in copies:
+        copy.start()
     cut = lambda begin, size: shard[begin - IN0 : begin - IN0 + size, :]
     width = grad_final.shape[-1]
 
@@ -1013,14 +1093,19 @@
     grad_conv_out[...] = cut(CONV, 16)
     for ref, begin in (
         (grad_ffn_out_bias, S_FOB), (grad_attn_norm, S_ATTN), (grad_conv_norm, S_CONV), (grad_batch, S_BATCH),
-        (grad_final, S_FINAL), (grad_depth, S_TAPS),
+        (grad_final, S_FINAL),
     ):
         for r, row in enumerate(thin_rows(begin, ref.shape[0])):
             ref[r : r + 1, :] = row
+    for r, row in enumerate(thin_rows(S_TAPS, TAPS)):
+        taps[r : r + 1, 0:width] = row
+    grad_depth[...] = taps[...].T[0:width, 0:TAPS]
     grad_attn_out_bias[...] = thin_rows(S_AOB, 1)[0][0]
     grad_conv_out_bias[...] = thin_rows(S_COB, 1)[0][0]
     grad_glu_bias[...] = thin[7:8, 0 : 2 * width][0]
     grad_rel[...] = thin[7:8, 64 : 64 + grad_rel.shape[0]][0]
+    for copy in copies:
+        copy.wait()
 
 
 def shape(dims, kind=F32):
@@ -1031,17 +1116,19 @@
     planes, chips = lax.axis_size("dp"), lax.axis_size("fsdp") // 2
     scratch = scratch_of(planes, chips)
     names = INPUTS + OUTPUTS + tuple(scratch)
-    vmem = pl.BlockSpec(memory_space=pltpu.VMEM)
-    output, grad_x, shard, thin = pl.pallas_call(
+    vmem, anywhere = pl.BlockSpec(memory_space=pltpu.VMEM), pl.BlockSpec(memory_space=pl.ANY)
+    given = dict(zip(INPUTS, args))
+    given["depth_kernel"] = given["depth_kernel"].T
+    firsts = [shape((1, L, D), BF16), shape((1, L, D))]
+    passed = pl.pallas_call(
         lambda *refs: whole_kernel(names, *refs),
-        out_shape=[shape((1, L, D), BF16), shape((1, L, D)), shape((GRADS, D)), shape((8, 128))],
+        out_shape=firsts + [shape((GRADS, D)), shape((8, 128))],
         in_specs=[vmem] * len(args),
         out_specs=[vmem] * 4,
         scratch_shapes=list(scratch.values()),
         compiler_params=pltpu.CompilerParams(collective_id=0, has_side_effects=True, vmem_limit_bytes=VMEM_BYTES),
         name="layer",
-    )(*args)
-    given = dict(zip(INPUTS, args))
+    )(*given.values())
     outs = [
         shape(given[name].shape)
         for name in (
@@ -1051,9 +1138,16 @@
         )
     ]
     grads = pl.pallas_call(
-        finish_kernel, out_shape=outs, in_specs=[vmem] * 2, out_specs=[vmem] * len(outs), name="unpack",
-    )(shard, thin)
-    return (output, grad_x) + tuple(grads)
+        finish_kernel,
+        out_shape=firsts + outs,
+        in_specs=[anywhere, anywhere, vmem, vmem],
+        out_specs=[vmem] * (2 + len(outs)),
+        scratch_shapes=[pltpu.VMEM((128, 128), F32), pltpu.SemaphoreType.DMA((2,))],
+        name="unpack",
+    )(*passed)
+    grads = list(grads)
+    grads[15] = grads[15].T
+    return tuple(grads)
 
 
 VMEM_BYTES = 62 * 1024 * 1024

time: 239 us -> 204 us (0.85)
  Pallas kernels: 233 us -> 203 us
  local copies, waits for them, and re-layouts: 5.59 us -> 0 us
    pallas_call x2, Pallas kernels: 233 us -> 203 us  [the longest x1 199 us: local(): pl.pallas_call(lambda *refs: whole_kernel(names, *refs), out_shape=firsts...]
    unnamed x6 -> x0, local copies, waits for them, and re-layouts: 5.59 us -> none
where the time goes in v3:
time: 204 us
  Pallas kernels  203 us (100%)
    pallas_call x1, Pallas kernels, local(): pl.pallas_call(lambda *refs: whole_kernel(names, *refs), out_shape=firsts...  199 us

profile of v3, /device:TPU:0, one launch (start us, length us, event | category | flops | bytes accessed | tf_op | source)
XLA Modules:
  0.0 204.0 jit_solution(4398995189615320577)
XLA Ops:
  0.7 199.2 %layer.1 = (bf16[1,512,512]{2,1,0:T(8,128)(2,1)}, f32[1,512,512]{2,1,0:T(8,128)}, f32[368,512]{1,0:T(8,128)}, f32[8,128]{1,0:T(8,128)}) custom-call(bf16[1,512,512]{2,1,0:T(8,128)(2,1)} %refs_0_.1, s32[1,512]{1,0:T(1,128)} %refs_1_.1, s32[1023]{0:T(1024)} %refs_2_.1, bf16[1,512,512]{2,1,0:T(8,128)(2,1)} %refs_3_.1, bf16[2,2,16]{2,1,0:T(2,128)(2,1)} %refs_4_.1, ...), custom_call_target="tpu_custom_call" | custom-call | tf_op jit(solution)/shard_map/layer/pallas_call | solution.py:1123
  199.9 4.0 %unpack.1 = (bf16[1,512,512]{2,1,0:T(8,128)(2,1)}, f32[1,512,512]{2,1,0:T(8,128)}, f32[2,2,16]{2,1,0:T(2,128)}, f32[2,16,2048]{2,1,0:T(8,128)}, f32[2,64]{1,0:T(...) custom-call(bf16[1,512,512]{2,1,0:T(8,128)(2,1)} %get-tuple-element., ...), custom_call_target="tpu_custom_call" | custom-call | tf_op jit(solution)/shard_map/unpack/pallas_call | solution.py:1140

commit v4 on v3

--- a/solution.py
+++ b/solution.py
@@ -21,6 +21,9 @@
 GRADS = ROWS - IN0
 (S_FFN, S_FOB, S_ATTN, S_AOB, S_CONV, S_BATCH, S_COB, S_FINAL, S_TAPS, S_ROWS) = (0, 4, 6, 8, 9, 11, 13, 14, 16, 48)
 CHUNK = 64
+BLOCK = 128
+SOFT = 32
+UNROLL = True
 
 
 def dot(a, b):
@@ -39,7 +42,7 @@
     def step(i, carry):
         return body(pl.ds(pl.multiple_of(i * size, size), size), carry)
 
-    return lax.fori_loop(0, L // size, step, carry)
+    return lax.fori_loop(0, L // size, step, carry, unroll=True)
 
 
 def fold(values):
@@ -320,12 +323,17 @@
 def at_points(table):
     def pump(index, place=0):
         for (iteration, where), steps in table.items():
-            if where == place:
-
-                @pl.when(index == iteration)
-                def _(steps=steps):
-                    for step in steps:
-                        step()
+            if where != place or (isinstance(index, int) and index != iteration):
+                continue
+
+            def act(steps=steps):
+                for step in steps:
+                    step()
+
+            if isinstance(index, int):
+                act()
+            else:
+                pl.when(index == iteration)(act)
 
     return pump
 
@@ -372,15 +380,15 @@
 
 
 def block_cols(c):
-    return pl.ds(pl.multiple_of(c * D, D), D)
+    return pl.ds(c * D if isinstance(c, int) else pl.multiple_of(c * D, D), D)
 
 
 def columns(weights, start, block):
-    return weights[:, :, :, pl.ds(pl.multiple_of(start + 16 * block, 16), 16), :].reshape(D, D)
+    return weights[:, :, :, start + 16 * block : start + 16 * block + 16, :].reshape(D, D)
 
 
 def put_columns(weights, start, block, value):
-    rows = pl.ds(pl.multiple_of(start + 16 * block, 16), 16)
+    rows = pl.ds(start + 16 * block, 16)
     weights[:, :, :, rows, :] = value.astype(BF16).reshape(weights.shape[:3] + (16, D))
 
 
@@ -392,17 +400,16 @@
     weights[block, :, :, start : start + 64, :] = value.astype(BF16).reshape(weights.shape[1:3] + (64, D))
 
 
-def feed_inner(source, normed, active, slope, hold, weights, small, inner_bias, layer, pump):
+def feed_inner(source, normed, active, slope, raws, weights, small, inner_bias, layer, pump):
     norm_rows(source, normed, small, S_FFN + 2 * layer)
-
-    def block(c, carry):
+    for c in range(FF // D):
         pump(c)
-        cols = block_cols(c)
-        hold[...] = dot(normed[...], columns(weights, (IN0, IN1)[layer], c))
+        cols, raw = block_cols(c), raws[c % 2]
+        raw[...] = dot(normed[...], columns(weights, (IN0, IN1)[layer], c))
         bias = inner_bias[layer : layer + 1, cols]
 
-        def body(rows, carry):
-            inner = hold[rows, :] + bias
+        def body(rows, carry, cols=cols, raw=raw, bias=bias):
+            inner = raw[rows, :] + bias
             sigma = jax.nn.sigmoid(inner)
             value = inner * sigma
             active[rows, cols] = value.astype(BF16)
@@ -410,28 +417,11 @@
             return carry
 
         chunks(body, 0)
-        return carry
-
-    lax.fori_loop(0, FF // D, block, 0)
 
 
 def feed_outer(source, active, result, hold, weights, small, layer):
     begin = (OUT0, OUT1)[layer]
-
-    def block(c, carry):
-        part = dot(active[:, block_cols(c)], lines_of(weights, begin, c))
-
-        @pl.when(c == 0)
-        def _():
-            hold[...] = part
-
-        @pl.when(c > 0)
-        def _():
-            hold[...] += part
-
-        return carry
-
-    lax.fori_loop(0, FF // D, block, 0)
+    hold[...] = dot(active[...], weights[:, :, :, begin : begin + 64, :].reshape(FF, D))
     bias = small[S_FOB + layer : S_FOB + layer + 1, :]
 
     def body(rows, carry):
@@ -451,23 +441,19 @@
 
 
 def feed_back_outer(active, low, weights, begin, pump):
-    def block(c, carry):
+    for c in range(FF // D):
         put_lines(weights, begin, c, dot_tn(active[:, block_cols(c)], low[...]))
         pump(c)
-        return carry
-
-    lax.fori_loop(0, FF // D, block, 0)
-
-
-def feed_back_inner(normed, slope, low, hold, weights, target, inner_grads, layer, pump):
+
+
+def feed_back_inner(normed, slope, low, raws, weights, target, inner_grads, layer, pump):
     begin = (OUT0, OUT1)[layer]
-
-    def block(c, carry):
-        cols = block_cols(c)
-        hold[...] = dot_nt(low[...], lines_of(weights, begin, c))
-
-        def body(rows, carry):
-            grad = hold[rows, :] * slope[rows, cols].astype(F32)
+    for c in range(FF // D):
+        cols, raw = block_cols(c), raws[c % 2]
+        raw[...] = dot_nt(low[...], lines_of(weights, begin, c))
+
+        def body(rows, carry, cols=cols, raw=raw):
+            grad = raw[rows, :] * slope[rows, cols].astype(F32)
             slope[rows, cols] = grad.astype(BF16)
             return carry + fold(grad)
 
@@ -475,30 +461,18 @@
         if target is not None:
             put_columns(weights, target, c, dot_tn(normed[...], slope[:, cols]))
         pump(c)
-        return carry
-
-    lax.fori_loop(0, FF // D, block, 0)
 
 
 def product_back(grad, normed, total, weights, begin, blocks, pump):
-    def block(c, carry):
-        cols = block_cols(c)
-        part = dot_nt(grad[:, cols], columns(weights, begin, c))
-
-        @pl.when(c == 0)
-        def _():
-            total[...] = part
-
-        @pl.when(c > 0)
-        def _():
-            total[...] += part
-
+    value = None
+    for c in range(blocks):
+        part = dot_nt(grad[:, block_cols(c)], columns(weights, begin, c))
+        value = part if value is None else value + part
+    total[...] = value
+    for c in range(blocks):
         if normed is not None:
-            put_columns(weights, begin, c, dot_tn(normed[...], grad[:, cols]))
+            put_columns(weights, begin, c, dot_tn(normed[...], grad[:, block_cols(c)]))
         pump(c)
-        return carry
-
-    lax.fori_loop(0, blocks, block, 0)
 
 
 def bucket_choice(buckets):
@@ -508,44 +482,71 @@
 def attention_mix(source, normed, mixed, weights, small):
     norm_rows(source, normed, small, S_ATTN)
 
-    def mix(c, carry):
+    for c in range(3):
         mixed[:, block_cols(c)] = dot(normed[...], columns(weights, QKV, c)).astype(BF16)
+
+
+def attention_squares(lines, squares, mask, table, buckets, bounds, marks):
+    lines[...] = dot(table[...].astype(BF16), bucket_choice(buckets).astype(BF16))
+
+    def head(h, carry):
+        line = jnp.broadcast_to(lines[pl.ds(h, 1), :], (BLOCK, 2 * L))
+        square = pltpu.roll(line, 2 * L - BLOCK + 1, 1, stride=1, stride_axis=0).astype(BF16)
+        for part in range(2):
+            squares[lax.rem(h, 4), lax.div(h, 4), part * BLOCK : (part + 1) * BLOCK, :] = square[:, part * L : (part + 1) * L]
         return carry
 
-    lax.fori_loop(0, 3, mix, 0)
-
-
-def attention_forward(source, mixed, probs, joined, result, lines, hold, weights, small, table, buckets, bounds, marks, pump):
-    lines[...] = dot(table[...].astype(BF16), bucket_choice(buckets).astype(BF16))
+    lax.fori_loop(0, HEADS, head, 0)
+
+    def body(rows, carry):
+        same = bounds[pl.ds(rows.start + PAD, CHUNK), 0:1] == marks[...]
+        mask[rows, :] = jnp.where(same, 3e38, -1e30)
+        return carry
+
+    chunks(body, 0)
+
+
+def attention_forward(source, mixed, probs, joined, recips, result, squares, mask, hold, hold2, weights, small, pump):
     lane = lax.broadcasted_iota(jnp.int32, (1, 128), 1)
-    size = 128
 
     def pair(index, carry):
         begin = pl.multiple_of(128 * index, 128)
+        query = mixed[:, pl.ds(begin, 128)] * HEAD_DIM ** (-0.5)
         keys = mixed[:, pl.ds(D + begin, 128)]
         contents = mixed[:, pl.ds(2 * D + begin, 128)]
-        for block in range(L // size):
-            rows = pl.ds(block * size, size)
-            query = mixed[rows, pl.ds(begin, 128)]
-            same = bounds[PAD + block * size : PAD + (block + 1) * size, 0:1] == marks[...]
-            parts = []
-            for half in range(2):
-                head = 2 * index + half
-                here = (lane // HEAD_DIM) == half
-                raw = dot_nt(jnp.where(here, query, jnp.zeros_like(query)), keys)
-                window = lines[pl.ds(head, 1), 384 - block * size : 1024 - block * size]
-                square = pltpu.roll(jnp.broadcast_to(window, (size, 640)), 513, 1, stride=1, stride_axis=0)
-                scores = jnp.where(same, raw * HEAD_DIM ** (-0.5) + square[:, :L], -1e30)
-                raised = jnp.exp(scores - jnp.max(scores, axis=1, keepdims=True))
-                share = (raised * (1.0 / jnp.sum(raised, axis=1, keepdims=True))).astype(BF16)
-                probs[head, rows, :] = share
-                parts.append(dot(share, contents))
-            joined[rows, pl.ds(begin, 128)] = jnp.where(lane < HEAD_DIM, parts[0], parts[1]).astype(BF16)
-            pump(index, block)
+        parts = []
+        for half, raw in enumerate((hold, hold2)):
+            here = (lane // HEAD_DIM) == half
+            raw[...] = dot_nt(jnp.where(here, query, jnp.zeros_like(query)), keys)
+        for half, raw in enumerate((hold, hold2)):
+            head = 2 * index + half
+            here = (lane // HEAD_DIM) == half
+            for block in range(L // BLOCK):
+
+                def body(i, carry, block=block, raw=raw, head=head):
+                    at = pl.multiple_of(i * SOFT, SOFT)
+                    rows = pl.ds(block * BLOCK + at, SOFT)
+                    square = squares[lax.rem(head, 4), lax.div(head, 4), pl.ds(at, SOFT), 384 - block * BLOCK : L]
+                    if block < L // BLOCK - 1:
+                        more = squares[lax.rem(head, 4), lax.div(head, 4), pl.ds(BLOCK + at, SOFT), 0 : 384 - block * BLOCK]
+                        square = jnp.concatenate([square, more], axis=1)
+                    scores = jnp.minimum(raw[rows, :] + square.astype(F32), mask[rows, :])
+                    probs[head, rows, :] = jnp.exp(scores - jnp.max(scores, axis=1, keepdims=True)).astype(BF16)
+                    return carry
+
+                lax.fori_loop(0, BLOCK // SOFT, body, 0, unroll=UNROLL)
+                if half:
+                    pump(index, block)
+            parts.append(dot(probs[head], jnp.where(here, contents, jnp.ones_like(contents))))
+        value = jnp.where(lane < HEAD_DIM, parts[0], parts[1])
+        sums = jnp.where(lane < HEAD_DIM, pltpu.roll(parts[0], HEAD_DIM, 1), pltpu.roll(parts[1], HEAD_DIM, 1))
+        recip = 1.0 / sums
+        recips[:, pl.ds(begin, 128)] = recip
+        joined[:, pl.ds(begin, 128)] = value * recip
         return carry
 
     lax.fori_loop(0, HEADS // 2, pair, 0)
-    hold[...] = dot(joined[...], columns(weights, ATT, 0))
+    hold[...] = dot(joined[...].astype(BF16), columns(weights, ATT, 0))
     bias = small[S_AOB : S_AOB + 1, :]
 
     def body(rows, carry):
@@ -555,21 +556,27 @@
     chunks(body, 0)
 
 
-def attention_back_start(upstream, joined, low, spread, weights, grads):
+def attention_back_start(upstream, joined, recips, low, spread, hold, weights, grads):
     def start(rows, carry):
         given = upstream[rows, :]
         low[rows, :] = given.astype(BF16)
         return carry + fold(given)
 
     grads[S_AOB : S_AOB + 1, :] = total_row(chunks(start, zeros8()))
-    spread[...] = dot_nt(low[...], columns(weights, ATT, 0)).astype(BF16)
-    put_columns(weights, ATT, 0, dot_tn(joined[...], low[...]))
-
-
-def attention_backward(mixed, probs, spread, grad_mixed, scaled, hold, lines, buckets, table_grad, pump):
+    hold[...] = dot_nt(low[...], columns(weights, ATT, 0))
+
+    def body(rows, carry):
+        spread[rows, :] = (hold[rows, :] * recips[rows, :]).astype(BF16)
+        return carry
+
+    chunks(body, 0)
+    put_columns(weights, ATT, 0, dot_tn(joined[...].astype(BF16), low[...]))
+
+
+def attention_backward(mixed, probs, spread, joined, grad_mixed, scaled, hold, hold2, means, diagonals, lines, buckets, table_grad, pump):
     lane = lax.broadcasted_iota(jnp.int32, (1, 128), 1)
-    row8 = lax.broadcasted_iota(jnp.int32, (8, 2 * L), 0)
-    size = 128
+    sides = lax.broadcasted_iota(jnp.int32, (256, 256), 0) // HEAD_DIM % 2 == lax.broadcasted_iota(jnp.int32, (256, 256), 1) // 128
+    sides = jnp.where(sides, 1.0, 0.0).astype(BF16)
 
     def pair(index, carry):
         begin = pl.multiple_of(128 * index, 128)
@@ -577,43 +584,50 @@
         keys = mixed[:, pl.ds(D + begin, 128)]
         contents = mixed[:, pl.ds(2 * D + begin, 128)]
         incoming = spread[:, pl.ds(begin, 128)]
-        parts = []
-        for half in range(2):
+        for half, raw in enumerate((hold, hold2)):
+            here = (lane // HEAD_DIM) == half
+            raw[...] = dot_nt(jnp.where(here, incoming, jnp.zeros_like(incoming)), contents)
+        both = incoming.astype(F32) * joined[:, pl.ds(begin, 128)]
+        upper = both.astype(BF16)
+        lower = (both - upper.astype(F32)).astype(BF16)
+        means[:, 0:256] = dot(jnp.concatenate([upper, lower], axis=1), sides)
+        turned_query, turned_incoming = query.T, incoming.T
+        grads_query, grads_keys, grads_contents = [], [], []
+        for half, raw in enumerate((hold, hold2)):
             head = 2 * index + half
-            here = (lane // HEAD_DIM) == half
-            hold[...] = dot_nt(jnp.where(here, incoming, jnp.zeros_like(incoming)), contents)
-            sums = zeros8(2 * L)
-            for block in range(L // size):
-                rows = pl.ds(block * size, size)
-                share = probs[head, rows, :].astype(F32)
-                given = hold[rows, :]
-                slant = share * (given - jnp.sum(given * share, axis=1, keepdims=True))
-                scaled[rows, :] = (slant * HEAD_DIM ** (-0.5)).astype(BF16)
-                part = zeros8(640)
-                for t in range(size // 8):
-                    tile = jnp.concatenate([slant[8 * t : 8 * t + 8], zeros8(128)], axis=1)
-                    part += pltpu.roll(tile, 120 - 8 * t, 1)
-                first = 384 - block * size
-                pieces = [part]
-                if first:
-                    pieces = [zeros8(first)] + pieces
-                if block:
-                    pieces = pieces + [zeros8(block * size)]
-                sums += jnp.concatenate(pieces, axis=1)
-            line = zeros8(2 * L)
-            for r in range(8):
-                line += jnp.where(row8 == r, pltpu.roll(sums, 7 - r, 1), 0.0)
-            lines[pl.ds(head, 1), :] = total_row(line)
-            parts.append((dot(scaled[...], keys), dot_tn(scaled[...], query), dot_tn(probs[head], incoming)))
+            side = slice(half * HEAD_DIM, (half + 1) * HEAD_DIM)
+            cols = pl.ds(half * L, L)
+            part = zeros8(2 * L)
+            for u in range(BLOCK // 16):
+                tiles = [None] * 7 + [jnp.zeros((16, 128), F32)]
+                for block in range(L // BLOCK):
+                    rows = pl.ds(block * BLOCK + 16 * u, 16)
+                    mean = means[rows, 128 * half : 128 * half + 128]
+                    slant = probs[head, rows, :].astype(F32) * (raw[rows, :] - jnp.concatenate([mean] * 4, axis=1))
+                    scaled[rows, cols] = slant.astype(BF16)
+                    for j in range(4):
+                        piece = slant[:, 128 * j : 128 * j + 128]
+                        at = 3 - block + j
+                        tiles[at] = piece if tiles[at] is None else tiles[at] + piece
+                full = jnp.concatenate(tiles, axis=1)
+                part = part + pltpu.roll(full[0:8], BLOCK - 8 - 16 * u, 1) + pltpu.roll(full[8:16], BLOCK - 16 - 16 * u, 1)
+            diagonals[:, pl.ds(head, 1), :] = part.reshape(8, 1, 2 * L)
+            grads_query.append(dot(scaled[:, cols], keys))
+            grads_keys.append(dot(turned_query[side], scaled[:, cols]))
+            grads_contents.append(dot(turned_incoming[side], probs[head]))
             pump(index, half)
-        for third in range(3):
-            merged = jnp.where(lane < HEAD_DIM, parts[0][third], parts[1][third])
-            grad_mixed[:, pl.ds(third * D + begin, 128)] = merged.astype(BF16)
+        scale = HEAD_DIM ** (-0.5)
+        grad_mixed[:, pl.ds(begin, 128)] = (jnp.where(lane < HEAD_DIM, *grads_query) * scale).astype(BF16)
+        grad_mixed[:, pl.ds(D + begin, 128)] = (jnp.concatenate(grads_keys, axis=0).T * scale).astype(BF16)
+        grad_mixed[:, pl.ds(2 * D + begin, 128)] = jnp.concatenate(grads_contents, axis=0).T.astype(BF16)
         return carry
 
     lax.fori_loop(0, HEADS // 2, pair, 0)
+    line = diagonals[7]
+    for r in range(7):
+        line = line + pltpu.roll(diagonals[r], 7 - r, 1)
     table_grad[...] = lax.dot_general(
-        lines[...], bucket_choice(buckets), (((1,), (1,)), ((), ())),
+        line, bucket_choice(buckets), (((1,), (1,)), ((), ())),
         precision=lax.Precision.HIGHEST, preferred_element_type=F32,
     )
 
@@ -624,14 +638,16 @@
     padded[:, PAD + L : 2 * PAD + L, :] = edge
 
 
-def conv_front(source, normed, sigma, gated, middle, sums, hold, weights, small, gate_bias, bounds, pump):
+def conv_front(source, normed, sigma, tilt, gated, middle, sums, hold, spare, weights, small, gate_bias, bounds, pump):
     norm_rows(source, normed, small, S_CONV)
     clear_pads(gated)
     hold[...] = dot(normed[...], columns(weights, GLU, 1))
     bias = gate_bias[0:1, D:]
 
     def gate(rows, carry):
-        sigma[rows, :] = jax.nn.sigmoid(hold[rows, :] + bias)
+        gate = jax.nn.sigmoid(hold[rows, :] + bias)
+        spare[rows, :] = gate
+        sigma[rows, :] = gate.astype(BF16)
         return carry
 
     chunks(gate, 0)
@@ -639,13 +655,15 @@
     bias = gate_bias[0:1, :D]
 
     def unit(rows, carry):
-        values = (hold[rows, :] + bias) * sigma[rows, :]
+        gate = spare[rows, :]
+        values = (hold[rows, :] + bias) * gate
+        tilt[rows, :] = (values * (1.0 - gate)).astype(BF16)
         for j in range(4):
             gated[j, pl.ds(rows.start + PAD, CHUNK), :] = values[:, 128 * j : 128 * j + 128]
         return carry
 
     chunks(unit, 0)
-    size = 16
+    size = 32
 
     def slide(i, carry):
         begin = pl.multiple_of(i * size, size)
@@ -664,7 +682,7 @@
         pump(i)
         return result[0::2] + result[1::2]
 
-    ends = lax.fori_loop(0, L // size, slide, [zeros8(128)] * 8)
+    ends = lax.fori_loop(0, L // size, slide, [zeros8(128)] * 8, unroll=2)
     sums[...] = zeros8()
     for j in range(4):
         sums[0:1, 128 * j : 128 * j + 128] = total_row(ends[j])
@@ -720,7 +738,7 @@
 
 
 def conv_back_front(
-    sigma, gated, unit, grad_normal, front_sums, sums, padded, grad_joined, hold, tap_sums, small, bounds, grads, gate_grads,
+    sigma, tilt, gated, unit, grad_normal, front_sums, sums, padded, grad_joined, hold, tap_sums, small, bounds, grads, gate_grads,
     frames, pump,
 ):
     center = front_sums[0:1, :] * (1.0 / frames)
@@ -737,7 +755,7 @@
 
     chunks(start, 0)
     tap_sums[...] = jnp.zeros_like(tap_sums)
-    size = 16
+    size = 32
 
     def slide(i, carry):
         begin = pl.multiple_of(i * size, size)
@@ -759,15 +777,13 @@
         pump(i)
         return carry
 
-    lax.fori_loop(0, L // size, slide, 0)
+    lax.fori_loop(0, L // size, slide, 0, unroll=2)
     grads[S_TAPS : S_TAPS + TAPS, :] = jnp.sum(tap_sums[...], axis=1)
 
     def split(rows, carry):
         grad = hold[rows, :]
-        gate = sigma[rows, :]
-        values = jnp.concatenate([gated[j, pl.ds(rows.start + PAD, CHUNK), :] for j in range(4)], axis=1)
-        first = grad * gate
-        second = grad * values * (1.0 - gate)
+        first = grad * sigma[rows, :].astype(F32)
+        second = grad * tilt[rows, :].astype(F32)
         grad_joined[rows, :D] = first.astype(BF16)
         grad_joined[rows, D : 2 * D] = second.astype(BF16)
         return carry[0] + fold(first), carry[1] + fold(second)
@@ -895,10 +911,10 @@
         front_own=stats, back_own=stats, front_sums=stats, back_sums=stats, front_part=stats, back_part=stats,
         front_near=pltpu.VMEM((2 * planes, 8, D), F32), back_near=pltpu.VMEM((2 * planes, 8, D), F32),
         front_far=pltpu.VMEM((chips, 8, D), F32), back_far=pltpu.VMEM((chips, 8, D), F32),
-        x1=wide, x2=wide, x3=wide, x4=wide, normed0=low, normed_a=low, normed_c=low, normed1=low,
+        x1=wide, x2=wide, x3=wide, x4=wide, normed_a=low, normed_c=low, normed1=low,
         active0=big, slope0=big, active1=big, slope1=big, mixed=pltpu.VMEM((L, 3 * D), BF16),
-        probs=pltpu.VMEM((HEADS, L, L), BF16), joined=low, sigma=wide, gated=pads, middle=wide, active_c=low, slope_c=low,
-        padded=pads, low=low, spread=low, hold=wide, total=wide, taps=pltpu.VMEM((TAPS, 8, D), F32),
+        probs=pltpu.VMEM((HEADS, L, L), BF16), joined=wide, recips=wide, diagonals=pltpu.VMEM((8, HEADS, 2 * L), F32), sigma=low, tilt=low, gated=pads, middle=wide, active_c=low, slope_c=low,
+        padded=pads, low=low, hold=wide, total=wide, taps=pltpu.VMEM((TAPS, 8, D), F32),
         gather_sends=pltpu.SemaphoreType.DMA((len(GATHERS) * Gather.semaphores(chips),)),
         gather_receives=pltpu.SemaphoreType.DMA((len(GATHERS) * Gather.semaphores(chips),)),
         reduce_sends=pltpu.SemaphoreType.DMA((len(REDUCES) * (chips + 7),)),
@@ -950,35 +966,43 @@
     unpack_small(b, place)
 
     x0 = b.inputs.at[0]
+    raws = (b.hold, b.total)
     feed_inner(
-        x0, b.normed0, b.active0, b.slope0, b.hold, b.weights, b.small, b.inner_bias, 0,
-        at_points({(1, 0): (r1.across, r2.turn), (2, 0): (r1.done, r3.forward), (3, 0): (r4.own,)}),
-    )
+        x0, b.normed_c, b.active0, b.slope0, raws, b.weights, b.small, b.inner_bias, 0,
+        at_points({(2, 0): (r1.across, r1.done, r3.forward)}),
+    )
+    r4.own()
+    attention_squares(b.lines, b.twin, b.x4, b.table, b.choice, b.bounds, b.marks)
+    r2.turn()
+    r4.forward()
     r2.across()
     r2.done()
     feed_outer(x0, b.active0, b.x1, b.hold, b.weights, b.small, 0)
-    for step in (r4.forward, r3.turn, r5.own, r5.forward, r3.across, r3.done):
+    for step in (r3.turn, r5.own, r5.forward, r3.across, r3.done):
         step()
     attention_mix(b.x1, b.normed_a, b.mixed, b.weights, b.small)
     for step in (r4.turn, r6.own, r6.forward):
         step()
     attention_forward(
-        b.x1, b.mixed, b.probs, b.joined, b.x2, b.lines, b.hold, b.weights, b.small, b.table, b.choice, b.bounds, b.marks,
-        at_points({(2, 1): (r5.turn,), (2, 3): (r4.across,), (3, 3): (r4.done,)}),
-    )
+        b.x1, b.mixed, b.probs, b.joined, b.recips, b.x2, b.twin, b.x4, b.hold, b.x3, b.weights, b.small, still
+    )
+    r4.across()
+    r5.turn()
+    r4.done()
     conv_front(
-        b.x2, b.normed_c, b.sigma, b.gated, b.middle, b.front_own, b.hold, b.weights, b.small, b.gate_bias, b.bounds,
-        at_points({(4, 0): (r6.turn,), (16, 0): (r5.across,), (28, 0): (r6.across,)}),
+        b.x2, b.normed_c, b.sigma, b.tilt, b.gated, b.middle, b.front_own, b.hold, b.total, b.weights, b.small, b.gate_bias, b.bounds,
+        at_points({(4, 0): (r5.across,), (10, 0): (r6.turn,)}),
     )
     totals = Copies(b.total_sends, b.total_receives, place)
     front = Total(place, b.front_own, b.front_near, b.front_part, b.front_far, b.front_sums, totals, 0)
     front.start()
     r5.done()
     front.turn()
-    r6.done()
+    r6.across()
     front.finish()
     conv_rest(b.x2, b.middle, b.front_sums, b.middle, b.active_c, b.slope_c, b.x3, b.hold, b.weights, b.small, frames)
-    feed_inner(b.x3, b.normed1, b.active1, b.slope1, b.hold, b.weights, b.small, b.inner_bias, 1, still)
+    feed_inner(b.x3, b.normed1, b.active1, b.slope1, raws, b.weights, b.small, b.inner_bias, 1, still)
+    r6.done()
     feed_outer(b.x3, b.active1, b.x4, b.hold, b.weights, b.small, 1)
     norm_rows(b.x4, b.output.at[0], b.small, S_FINAL)
     flow = b.x4
@@ -1002,11 +1026,12 @@
     ]
     out1, in1, conv, mix, out0, in0, in0_end = backs
     feed_back_start(flow, b.low, b.grads, 1)
-    feed_back_inner(b.normed1, b.slope1, b.low, b.hold, b.weights, None, b.inner_grads, 1, still)
+    feed_back_inner(b.normed1, b.slope1, b.low, raws, b.weights, None, b.inner_grads, 1, still)
     feed_back_outer(b.active1, b.low, b.weights, OUT1, still)
     out1[0]()
-    product_back(b.slope1, b.normed1, b.total, b.weights, IN1, 4, at_points({(1, 0): (out1[1],)}))
+    product_back(b.slope1, b.normed1, b.total, b.weights, IN1, 4, still)
     in1[0]()
+    out1[1]()
     norm_back(b.x3, b.total, flow, flow, b.small, S_FFN + 2, b.grads)
     in1[1]()
     grad_normal = b.x3
@@ -1014,45 +1039,47 @@
     back = Total(place, b.back_own, b.back_near, b.back_part, b.back_far, b.back_sums, totals, 2 * planes + chips)
     back.start()
     put_columns(b.weights, CONV, 0, dot_tn(b.active_c[...], b.low[...]))
+    back.turn()
     out1[2]()
-    back.turn()
-    in1[2]()
     back.finish()
     conv_back_front(
-        b.sigma, b.gated, b.middle, grad_normal, b.front_sums, b.back_sums, b.padded, b.active1, b.hold, b.taps, b.small,
-        b.bounds, b.grads, b.gate_grads, frames, at_points({(10, 0): (out1[3],), (26, 0): (in1[3],)}),
-    )
-    out1[4]()
+        b.sigma, b.tilt, b.gated, b.middle, grad_normal, b.front_sums, b.back_sums, b.padded, b.active1, b.hold, b.taps, b.small,
+        b.bounds, b.grads, b.gate_grads, frames, at_points({(4, 0): (in1[2],), (14, 0): (out1[3],)}),
+    )
     product_back(b.active1, b.normed_c, b.total, b.weights, GLU, 2, still)
     norm_back(b.x2, b.total, flow, flow, b.small, S_CONV, b.grads)
-    attention_back_start(flow, b.joined, b.low, b.spread, b.weights, b.grads)
+    attention_back_start(flow, b.joined, b.recips, b.low, b.normed1, b.hold, b.weights, b.grads)
     conv[0]()
     attention_backward(
-        b.mixed, b.probs, b.spread, b.active1, b.slope1.at[:, pl.ds(0, D)], b.hold, b.lines, b.choice, b.table_grad,
-        at_points({(0, 1): (conv[1], in1[4]), (2, 0): (conv[2],), (3, 1): (conv[3],)}),
+        b.mixed, b.probs, b.normed1, b.joined, b.active1, b.slope1, b.hold, b.x3, b.total, b.diagonals, b.lines, b.choice,
+        b.table_grad, at_points({(0, 1): (in1[3],), (1, 0): (conv[1],), (3, 0): (out1[4],)}),
     )
     product_back(b.active1, b.normed_a, b.total, b.weights, QKV, 3, still)
     mix[0]()
+    conv[2]()
     norm_back(b.x1, b.total, flow, flow, b.small, S_ATTN, b.grads)
     mix[1]()
-    conv[4]()
+    in1[4]()
     reduces.sent()
+    norm_rows(x0, b.normed_c, b.small, S_FFN)
     feed_back_start(flow, b.low, b.grads, 0)
     feed_back_outer(b.active0, b.low, b.weights, OUT1, still)
     out0[0]()
     feed_back_inner(
-        b.normed0, b.slope0, b.low, b.hold, b.weights, IN1, b.inner_grads, 0,
-        at_points({(0, 0): (mix[2],), (1, 0): (in0[0], out0[1]), (2, 0): (in0[1],)}),
+        b.normed_c, b.slope0, b.low, raws, b.weights, IN1, b.inner_grads, 0,
+        at_points({(1, 0): (in0[0], out0[1])}),
     )
     in0_end[0]()
-    out0[2]()
-    product_back(b.slope0, None, b.total, b.weights, IN0, 4, at_points({(1, 0): (in0_end[1], mix[3])}))
-    in0[2]()
+    in0[1]()
+    product_back(b.slope0, None, b.total, b.weights, IN0, 4, still)
     norm_back(x0, b.total, flow, b.grad_x.at[0], b.small, S_FFN, b.grads)
     pack_small_grads(b, place)
     thin = Thin(place, b.edges, b.edge_near, b.edge_part, b.edge_far, b.thin, totals, 2 * (2 * planes + chips))
     thin.start()
-    for step in (in0_end[2], out0[3], mix[4], thin.turn, in0[3], in0_end[3], out0[4], thin.finish, in0[4], in0_end[4]):
+    for step in (
+        conv[3], mix[2], in0_end[1], thin.turn, out0[2], conv[4], mix[3], in0[2], in0_end[2], thin.finish, out0[3], mix[4], in0[3],
+        in0_end[3], out0[4], in0[4], in0_end[4],
+    ):
         step()
     reduces.sent()
     totals.sent()
@@ -1150,7 +1177,7 @@
     return tuple(grads)
 
 
-VMEM_BYTES = 62 * 1024 * 1024
+VMEM_BYTES = 127 * 512 * 1024
 
 
 highest = lax.Precision.HIGHEST

time: 204 us -> 177 us (0.87)
  Pallas kernels: 203 us -> 175 us
    pallas_call x1, Pallas kernels: 199 us -> 171 us  [local(): pl.pallas_call(lambda *refs: whole_kernel(names, *refs), out_shape=firsts...]
where the time goes in v4:
time: 177 us; the launch traced here: 176 us
  Pallas kernels  175 us (99%)
    pallas_call x1, Pallas kernels, local(): pl.pallas_call(lambda *refs: whole_kernel(names, *refs), out_shape=firsts...  171 us
    pallas_call x1, Pallas kernels, local(): pl.pallas_call(finish_kernel, out_shape=firsts + outs, in_specs=[anywhere...  3.98 us

profile of v4, /device:TPU:0, one launch (start us, length us, event | category | flops | bytes accessed | tf_op | source)
XLA Modules:
  0.0 176.3 jit_solution(4787469148949376373)
XLA Ops:
  0.7 171.5 %layer.1 = (bf16[1,512,512]{2,1,0:T(8,128)(2,1)}, f32[1,512,512]{2,1,0:T(8,128)}, f32[368,512]{1,0:T(8,128)}, f32[8,128]{1,0:T(8,128)}) custom-call(bf16[1,512,512]{2,1,0:T(8,128)(2,1)} %refs_0_.1, s32[1,512]{1,0:T(1,128)} %refs_1_.1, s32[1023]{0:T(1024)} %refs_2_.1, bf16[1,512,512]{2,1,0:T(8,128)(2,1)} %refs_3_.1, bf16[2,2,16]{2,1,0:T(2,128)(2,1)} %refs_4_.1, ...), custom_call_target="tpu_custom_call" | custom-call | tf_op jit(solution)/shard_map/layer/pallas_call | solution.py:1150
  172.2 4.0 %unpack.1 = (bf16[1,512,512]{2,1,0:T(8,128)(2,1)}, f32[1,512,512]{2,1,0:T(8,128)}, f32[2,2,16]{2,1,0:T(2,128)}, f32[2,16,2048]{2,1,0:T(8,128)}, f32[2,64]{1,0:T(...) custom-call(bf16[1,512,512]{2,1,0:T(8,128)(2,1)} %get-tuple-element., ...), custom_call_target="tpu_custom_call" | custom-call | tf_op jit(solution)/shard_map/unpack/pallas_call | solution.py:1167

commit v5 on v4

--- a/solution.py
+++ b/solution.py
@@ -486,7 +486,16 @@
         mixed[:, block_cols(c)] = dot(normed[...], columns(weights, QKV, c)).astype(BF16)
 
 
-def attention_squares(lines, squares, mask, table, buckets, bounds, marks):
+def attention_mask(mask, bounds, marks):
+    def body(rows, carry):
+        same = bounds[pl.ds(rows.start + PAD, CHUNK), 0:1] == marks[...]
+        mask[rows, :] = jnp.where(same, 3e38, -1e30)
+        return carry
+
+    chunks(body, 0)
+
+
+def attention_squares(lines, squares, table, buckets):
     lines[...] = dot(table[...].astype(BF16), bucket_choice(buckets).astype(BF16))
 
     def head(h, carry):
@@ -497,13 +506,6 @@
         return carry
 
     lax.fori_loop(0, HEADS, head, 0)
-
-    def body(rows, carry):
-        same = bounds[pl.ds(rows.start + PAD, CHUNK), 0:1] == marks[...]
-        mask[rows, :] = jnp.where(same, 3e38, -1e30)
-        return carry
-
-    chunks(body, 0)
 
 
 def attention_forward(source, mixed, probs, joined, recips, result, squares, mask, hold, hold2, weights, small, pump):
@@ -683,7 +685,6 @@
         return result[0::2] + result[1::2]
 
     ends = lax.fori_loop(0, L // size, slide, [zeros8(128)] * 8, unroll=2)
-    sums[...] = zeros8()
     for j in range(4):
         sums[0:1, 128 * j : 128 * j + 128] = total_row(ends[j])
         sums[1:2, 128 * j : 128 * j + 128] = total_row(ends[4 + j])
@@ -730,7 +731,6 @@
         return carry[0] + fold(grad), carry[1] + fold(grad * unit[rows, :])
 
     first, second = chunks(body, (zeros8(), zeros8()))
-    sums[...] = zeros8()
     sums[0:1, :] = total_row(first)
     sums[1:2, :] = total_row(second)
     grads[S_BATCH : S_BATCH + 1, :] = total_row(second)
@@ -823,17 +823,26 @@
     tile[3:4, 384 : 384 + few] = b.rel_table[...].astype(F32).reshape(1, few)
 
 
-def pack_weights(b, put):
+def load_weights(b, place):
+    copies = {}
+
+    def load(row, source):
+        target = b.weights.at[place.plane, place.z, place.core, pl.ds(row, source.shape[0])]
+        copies[row] = pltpu.make_async_copy(source, target, b.load_sems.at[len(copies)])
+        copies[row].start()
+
     for layer in range(2):
         for c in range(FF // D):
-            put((IN0, IN1)[layer] + 16 * c, b.ffn_in[layer, :, D * c : D * c + D])
-        put((OUT0, OUT1)[layer], b.ffn_out[layer])
-    for c in range(3):
-        put(QKV + 16 * c, b.qkv_weight[:, D * c : D * c + D])
-    put(ATT, b.attn_out[...])
-    for c in range(2):
-        put(GLU + 16 * c, b.glu_weight[:, D * c : D * c + D])
-    put(CONV, b.conv_out[...])
+            load((IN0, IN1)[layer] + 16 * c, b.ffn_in.at[layer, :, pl.ds(D * c, D)])
+        load((OUT0, OUT1)[layer], b.ffn_out.at[layer])
+        if layer == 0:
+            for c in range(3):
+                load(QKV + 16 * c, b.qkv_weight.at[:, pl.ds(D * c, D)])
+            load(ATT, b.attn_out.at[:, :])
+            for c in range(2):
+                load(GLU + 16 * c, b.glu_weight.at[:, pl.ds(D * c, D)])
+            load(CONV, b.conv_out.at[:, :])
+    return copies
 
 
 def unpack_small(b, place):
@@ -872,18 +881,20 @@
     "qkv_weight", "attn_out", "attn_out_bias", "rel_table", "conv_norm", "glu_weight", "glu_bias", "depth_kernel", "batch_norm",
     "conv_out", "conv_out_bias", "final_norm",
 )
+LOADED = ("inputs", "cotangent", "ffn_in", "ffn_out", "qkv_weight", "attn_out", "glu_weight", "conv_out")
 OUTPUTS = ("output", "grad_x", "shard", "thin")
 GATHERS = ((SMALL, 48, 32), (IN0 + 32, 32, 16), (OUT0, 64, 32), (QKV, 64, 32), (GLU, 48, 32), (IN1, 64, 32), (OUT1, 64, 32))
 REDUCES = (
-    (OUT1, OUT1, 64, 32), (IN1, IN1, 64, 32), (ATT, ATT, 64, 32), (QKV, QKV, 48, 32), (OUT1, OUT0, 64, 32),
-    (IN1, IN0, 32, 16), (IN1 + 32, IN0 + 32, 32, 16),
+    (OUT1, OUT1, 64, 32), (IN1, IN1, 64, 32), (CONV, CONV, 16, 16), (GLU, GLU, 32, 16),
+    (ATT, ATT, 16, 16), (QKV, QKV, 48, 32), (OUT1, OUT0, 32, 16),
+    (OUT1 + 32, OUT0 + 32, 32, 16), (IN1, IN0, 32, 16), (IN1 + 32, IN0 + 32, 32, 16),
 )
 
 
 def scratch_of(planes, chips):
     wide, low, big = pltpu.VMEM((L, D), F32), pltpu.VMEM((L, D), BF16), pltpu.VMEM((L, FF), BF16)
     pads = pltpu.VMEM((4, L + 2 * PAD, 128), F32)
-    stats = pltpu.VMEM((8, D), F32)
+    stats = pltpu.VMEM((2, D), F32)
     return dict(
         weights=pltpu.VMEM((planes, chips, 2, ROWS, D), BF16),
         twin=pltpu.VMEM((planes, chips, GRADS, D), BF16),
@@ -909,12 +920,15 @@
         bounds=pltpu.VMEM((L + 2 * PAD, 128), F32),
         marks=pltpu.VMEM((1, L), F32),
         front_own=stats, back_own=stats, front_sums=stats, back_sums=stats, front_part=stats, back_part=stats,
-        front_near=pltpu.VMEM((2 * planes, 8, D), F32), back_near=pltpu.VMEM((2 * planes, 8, D), F32),
-        front_far=pltpu.VMEM((chips, 8, D), F32), back_far=pltpu.VMEM((chips, 8, D), F32),
+        front_near=pltpu.VMEM((2 * planes, 2, D), F32), back_near=pltpu.VMEM((2 * planes, 2, D), F32),
+        front_far=pltpu.VMEM((chips, 2, D), F32), back_far=pltpu.VMEM((chips, 2, D), F32),
         x1=wide, x2=wide, x3=wide, x4=wide, normed_a=low, normed_c=low, normed1=low,
         active0=big, slope0=big, active1=big, slope1=big, mixed=pltpu.VMEM((L, 3 * D), BF16),
         probs=pltpu.VMEM((HEADS, L, L), BF16), joined=wide, recips=wide, diagonals=pltpu.VMEM((8, HEADS, 2 * L), F32), sigma=low, tilt=low, gated=pads, middle=wide, active_c=low, slope_c=low,
         padded=pads, low=low, hold=wide, total=wide, taps=pltpu.VMEM((TAPS, 8, D), F32),
+        x0=low, given=low, result=low,
+        load_sems=pltpu.SemaphoreType.DMA((17,)),
+        edge_sems=pltpu.SemaphoreType.DMA((4,)),
         gather_sends=pltpu.SemaphoreType.DMA((len(GATHERS) * Gather.semaphores(chips),)),
         gather_receives=pltpu.SemaphoreType.DMA((len(GATHERS) * Gather.semaphores(chips),)),
         reduce_sends=pltpu.SemaphoreType.DMA((len(REDUCES) * (chips + 7),)),
@@ -935,13 +949,13 @@
     near = [device for device, rank in place.members] + [place.along[d] for d in range(1, chips)]
     for device in near:
         pl.semaphore_signal(barrier, inc=1, device_id=device, device_id_type=MESH)
+    loads = load_weights(b, place)
+    load_x = pltpu.make_async_copy(b.inputs.at[0], b.x0, b.edge_sems.at[0])
+    load_cotangent = pltpu.make_async_copy(b.cotangent.at[0], b.given, b.edge_sems.at[1])
+    load_x.start()
+    load_cotangent.start()
     pack_small(b, b.tile)
-
-    def put(row, value):
-        b.weights[place.plane, place.z, place.core, row : row + value.shape[0], :] = value
-
-    put(0, b.tile[...].astype(BF16))
-    pack_weights(b, put)
+    b.weights[place.plane, place.z, place.core, 0:16, :] = b.tile[...].astype(BF16)
     pl.semaphore_wait(barrier, len(near))
 
     gathers = Copies(b.gather_sends, b.gather_receives, place)
@@ -950,65 +964,70 @@
         for i, (begin, size, split) in enumerate(GATHERS)
     ]
     r0, r1, r2, r3, r4, r5, r6 = rounds
-    r0.along_z()
-    r0.own()
-    r1.along_z()
-    r1.own()
-    for r in rounds[2:]:
+    for r, (begin, size, _) in zip(rounds, GATHERS):
+        for row, copy in loads.items():
+            if begin <= row < begin + size:
+                copy.wait()
         r.along_z()
+        if r in rounds[:5]:
+            r.own()
     b.marks[...] = b.segments[...].astype(F32)
     b.bounds[...] = jnp.full(b.bounds.shape, -1.0, F32)
     b.bounds[PAD : PAD + L, :] = jnp.broadcast_to(b.marks[...], (128, L)).T
     b.choice[...] = jnp.full(b.choice.shape, -1, jnp.int32)
     b.choice[:, 0 : 2 * L - 1] = b.buckets[...].reshape(1, 2 * L - 1)
-    for step in (r0.forward, r1.forward, r2.own, r0.turn, r1.turn, r2.forward, r3.own, r0.across, r0.done):
+    attention_mask(b.x4, b.bounds, b.marks)
+    for step in (r0.forward, r1.forward, r0.turn, r1.turn, r2.forward, r0.across, r0.done):
         step()
     unpack_small(b, place)
 
-    x0 = b.inputs.at[0]
+    x0 = b.x0
+    load_x.wait()
     raws = (b.hold, b.total)
     feed_inner(
         x0, b.normed_c, b.active0, b.slope0, raws, b.weights, b.small, b.inner_bias, 0,
         at_points({(2, 0): (r1.across, r1.done, r3.forward)}),
     )
-    r4.own()
-    attention_squares(b.lines, b.twin, b.x4, b.table, b.choice, b.bounds, b.marks)
-    r2.turn()
-    r4.forward()
-    r2.across()
-    r2.done()
+    attention_squares(b.lines, b.twin, b.table, b.choice)
+    for step in (r2.turn, r3.turn, r4.forward, r5.own, r2.across, r2.done):
+        step()
     feed_outer(x0, b.active0, b.x1, b.hold, b.weights, b.small, 0)
-    for step in (r3.turn, r5.own, r5.forward, r3.across, r3.done):
-        step()
+    r3.across()
+    r3.done()
     attention_mix(b.x1, b.normed_a, b.mixed, b.weights, b.small)
-    for step in (r4.turn, r6.own, r6.forward):
+    for step in (r4.turn, r5.forward, r6.own, r6.forward):
         step()
     attention_forward(
         b.x1, b.mixed, b.probs, b.joined, b.recips, b.x2, b.twin, b.x4, b.hold, b.x3, b.weights, b.small, still
     )
     r4.across()
-    r5.turn()
     r4.done()
     conv_front(
         b.x2, b.normed_c, b.sigma, b.tilt, b.gated, b.middle, b.front_own, b.hold, b.total, b.weights, b.small, b.gate_bias, b.bounds,
-        at_points({(4, 0): (r5.across,), (10, 0): (r6.turn,)}),
+        at_points({(5, 0): (r5.turn,)}),
     )
     totals = Copies(b.total_sends, b.total_receives, place)
     front = Total(place, b.front_own, b.front_near, b.front_part, b.front_far, b.front_sums, totals, 0)
     front.start()
-    r5.done()
+    r6.turn()
     front.turn()
-    r6.across()
     front.finish()
     conv_rest(b.x2, b.middle, b.front_sums, b.middle, b.active_c, b.slope_c, b.x3, b.hold, b.weights, b.small, frames)
+    r5.across()
+    r5.done()
     feed_inner(b.x3, b.normed1, b.active1, b.slope1, raws, b.weights, b.small, b.inner_bias, 1, still)
+    r6.across()
     r6.done()
     feed_outer(b.x3, b.active1, b.x4, b.hold, b.weights, b.small, 1)
-    norm_rows(b.x4, b.output.at[0], b.small, S_FINAL)
+    norm_rows(b.x4, b.result, b.small, S_FINAL)
+    save_output = pltpu.make_async_copy(b.result, b.output.at[0], b.edge_sems.at[2])
+    save_output.start()
+    load_cotangent.wait()
     flow = b.x4
-    norm_back(b.x4, b.cotangent.at[0], None, flow, b.small, S_FINAL, b.grads)
+    norm_back(b.x4, b.given, None, flow, b.small, S_FINAL, b.grads)
     gathers.sent()
 
+    early = Copies(b.reduce_sends, b.reduce_receives, place)
     reduces = Copies(b.reduce_sends, b.reduce_receives, place)
     landings = (b.twin, b.diagonal, b.from_x, b.from_y, b.from_z)
 
@@ -1020,11 +1039,12 @@
 
     backs = [
         reduce_steps(
-            place, b.weights, *landings, reduces, i * (chips + 7), begin, size, split, owner - IN0, finish(owner, size)
+            place, b.weights, *landings, early if i < 2 else reduces, i * (chips + 7), begin, size, split, owner - IN0,
+            finish(owner, size),
         )
         for i, (begin, owner, size, split) in enumerate(REDUCES)
     ]
-    out1, in1, conv, mix, out0, in0, in0_end = backs
+    out1, in1, tip, glu, att, mix, out0, out0_end, in0, in0_end = backs
     feed_back_start(flow, b.low, b.grads, 1)
     feed_back_inner(b.normed1, b.slope1, b.low, raws, b.weights, None, b.inner_grads, 1, still)
     feed_back_outer(b.active1, b.low, b.weights, OUT1, still)
@@ -1039,50 +1059,63 @@
     back = Total(place, b.back_own, b.back_near, b.back_part, b.back_far, b.back_sums, totals, 2 * planes + chips)
     back.start()
     put_columns(b.weights, CONV, 0, dot_tn(b.active_c[...], b.low[...]))
+    tip[0]()
     back.turn()
     out1[2]()
+    tip[1]()
     back.finish()
     conv_back_front(
         b.sigma, b.tilt, b.gated, b.middle, grad_normal, b.front_sums, b.back_sums, b.padded, b.active1, b.hold, b.taps, b.small,
-        b.bounds, b.grads, b.gate_grads, frames, at_points({(4, 0): (in1[2],), (14, 0): (out1[3],)}),
+        b.bounds, b.grads, b.gate_grads, frames, at_points({(4, 0): (in1[2],), (8, 0): (tip[2],), (14, 0): (out1[3],)}),
     )
     product_back(b.active1, b.normed_c, b.total, b.weights, GLU, 2, still)
+    glu[0]()
     norm_back(b.x2, b.total, flow, flow, b.small, S_CONV, b.grads)
     attention_back_start(flow, b.joined, b.recips, b.low, b.normed1, b.hold, b.weights, b.grads)
-    conv[0]()
+    att[0]()
+    glu[1]()
     attention_backward(
         b.mixed, b.probs, b.normed1, b.joined, b.active1, b.slope1, b.hold, b.x3, b.total, b.diagonals, b.lines, b.choice,
-        b.table_grad, at_points({(0, 1): (in1[3],), (1, 0): (conv[1],), (3, 0): (out1[4],)}),
+        b.table_grad, at_points({(0, 1): (in1[3], att[1]), (2, 0): (tip[3],), (2, 1): (glu[2],), (3, 0): (out1[4],), (3, 1): (att[2],)}),
     )
     product_back(b.active1, b.normed_a, b.total, b.weights, QKV, 3, still)
     mix[0]()
-    conv[2]()
     norm_back(b.x1, b.total, flow, flow, b.small, S_ATTN, b.grads)
-    mix[1]()
     in1[4]()
-    reduces.sent()
+    tip[4]()
+    early.sent()
     norm_rows(x0, b.normed_c, b.small, S_FFN)
     feed_back_start(flow, b.low, b.grads, 0)
     feed_back_outer(b.active0, b.low, b.weights, OUT1, still)
     out0[0]()
+    out0_end[0]()
+    mix[1]()
+    glu[3]()
+    att[3]()
     feed_back_inner(
         b.normed_c, b.slope0, b.low, raws, b.weights, IN1, b.inner_grads, 0,
-        at_points({(1, 0): (in0[0], out0[1])}),
+        at_points({(1, 0): (in0[0], out0[1]), (2, 0): (out0_end[1],)}),
     )
     in0_end[0]()
     in0[1]()
     product_back(b.slope0, None, b.total, b.weights, IN0, 4, still)
-    norm_back(x0, b.total, flow, b.grad_x.at[0], b.small, S_FFN, b.grads)
+    in0_end[1]()
+    norm_back(x0, b.total, flow, b.x3, b.small, S_FFN, b.grads)
+    save_grad_x = pltpu.make_async_copy(b.x3, b.grad_x.at[0], b.edge_sems.at[3])
+    save_grad_x.start()
     pack_small_grads(b, place)
     thin = Thin(place, b.edges, b.edge_near, b.edge_part, b.edge_far, b.thin, totals, 2 * (2 * planes + chips))
     thin.start()
     for step in (
-        conv[3], mix[2], in0_end[1], thin.turn, out0[2], conv[4], mix[3], in0[2], in0_end[2], thin.finish, out0[3], mix[4], in0[3],
-        in0_end[3], out0[4], in0[4], in0_end[4],
+        mix[2], thin.turn, out0[2], out0_end[2], in0[2], in0_end[2], glu[4], att[4], thin.finish, mix[3], out0[3], out0_end[3],
+        mix[4], in0[3], out0[4], in0_end[3], out0_end[4], in0[4], in0_end[4],
     ):
         step()
+    early.sent()
     reduces.sent()
     totals.sent()
+    save_output.wait()
+    save_grad_x.wait()
 
 
 def finish_kernel(*refs):
@@ -1150,8 +1183,8 @@
     passed = pl.pallas_call(
         lambda *refs: whole_kernel(names, *refs),
         out_shape=firsts + [shape((GRADS, D)), shape((8, 128))],
-        in_specs=[vmem] * len(args),
-        out_specs=[vmem] * 4,
+        in_specs=[anywhere if name in LOADED else vmem for name in INPUTS],
+        out_specs=[anywhere, anywhere, vmem, vmem],
         scratch_shapes=list(scratch.values()),
         compiler_params=pltpu.CompilerParams(collective_id=0, has_side_effects=True, vmem_limit_bytes=VMEM_BYTES),
         name="layer",

time: 177 us -> 162 us (0.915)
  Pallas kernels: 175 us -> 161 us
    pallas_call x1, Pallas kernels: 171 us -> 157 us  [local(): pl.pallas_call(lambda *refs: whole_kernel(names, *refs), out_shape=firsts...]
where the time goes in v5:
time: 162 us
  Pallas kernels  161 us (99%)
    pallas_call x1, Pallas kernels, local(): pl.pallas_call(lambda *refs: whole_kernel(names, *refs), out_shape=firsts...  157 us
    pallas_call x1, Pallas kernels, local(): pl.pallas_call(finish_kernel, out_shape=firsts + outs, in_specs=[anywhere...  3.98 us

profile of v5, /device:TPU:0, one launch (start us, length us, event | category | flops | bytes accessed | tf_op | source)
XLA Modules:
  0.0 162.2 jit_solution(14382536606420169947)
XLA Ops:
  0.7 157.3 %layer.1 = (bf16[1,512,512]{2,1,0:T(8,128)(2,1)}, f32[1,512,512]{2,1,0:T(8,128)}, f32[368,512]{1,0:T(8,128)}, f32[8,128]{1,0:T(8,128)}) custom-call(bf16[1,512,512]{2,1,0:T(8,128)(2,1)} %refs_0_.1, s32[1,512]{1,0:T(1,128)} %refs_1_.1, s32[1023]{0:T(1024)} %refs_2_.1, bf16[1,512,512]{2,1,0:T(8,128)(2,1)} %refs_3_.1, bf16[2,2,16]{2,1,0:T(2,128)(2,1)} %refs_4_.1, ...), custom_call_target="tpu_custom_call" | custom-call | tf_op jit(solution)/shard_map/layer/pallas_call | solution.py:1183
  158.0 4.0 %unpack.1 = (bf16[1,512,512]{2,1,0:T(8,128)(2,1)}, f32[1,512,512]{2,1,0:T(8,128)}, f32[2,2,16]{2,1,0:T(2,128)}, f32[2,16,2048]{2,1,0:T(8,128)}, f32[2,64]{1,0:T(...) custom-call(bf16[1,512,512]{2,1,0:T(8,128)(2,1)} %get-tuple-element., ...), custom_call_target="tpu_custom_call" | custom-call | tf_op jit(solution)/shard_map/unpack/pallas_call | solution.py:1200

commit v6 on v5

--- a/solution.py
+++ b/solution.py
@@ -1,3 +1,5 @@
+import math
+
 import jax
 import jax.numpy as jnp
 from jax import lax
@@ -196,7 +198,7 @@
             data[plane, zz, core, which, :] = value
             return carry
 
-        lax.fori_loop(0, chips, step, 0)
+        lax.fori_loop(0, chips, step, 0, unroll=True)
 
     def read(ref, which, *lead):
         return lambda zz: ref[lead + (zz, which, slice(None))]
@@ -761,19 +763,16 @@
         begin = pl.multiple_of(i * size, size)
         marks = bounds[pl.ds(begin + PAD, size), :]
         accs = [jnp.zeros((size, 128), F32) for _ in range(4)]
+        here = [gated[j, pl.ds(begin + PAD, size), :] for j in range(4)]
         for k in range(TAPS):
             same = bounds[pl.ds(begin + 2 * PAD - k, size), :] == marks
             for j in range(4):
                 tap = small[S_TAPS + k : S_TAPS + k + 1, 128 * j : 128 * j + 128]
-                accs[j] += jnp.where(same, padded[j, pl.ds(begin + 2 * PAD - k, size), :], 0.0) * tap
+                grad = jnp.where(same, padded[j, pl.ds(begin + 2 * PAD - k, size), :], 0.0)
+                accs[j] += grad * tap
+                tap_sums[k, :, 128 * j : 128 * j + 128] += fold(grad * here[j])
         for j in range(4):
             hold[pl.ds(begin, size), 128 * j : 128 * j + 128] = accs[j]
-        grads_here = [padded[j, pl.ds(begin + PAD, size), :] for j in range(4)]
-        for k in range(TAPS):
-            same = bounds[pl.ds(begin + k, size), :] == marks
-            for j in range(4):
-                term = jnp.where(same, gated[j, pl.ds(begin + k, size), :], 0.0) * grads_here[j]
-                tap_sums[k, :, 128 * j : 128 * j + 128] += fold(term)
         pump(i)
         return carry
 

time: 162 us -> 160 us (0.988)
  Pallas kernels: 161 us -> 159 us
    pallas_call x1, Pallas kernels: 157 us -> 155 us  [local(): pl.pallas_call(lambda *refs: whole_kernel(names, *refs), out_shape=firsts...]
where the time goes in v6:
time: 160 us
  Pallas kernels  159 us (99%)
    pallas_call x1, Pallas kernels, local(): pl.pallas_call(lambda *refs: whole_kernel(names, *refs), out_shape=firsts...  155 us
    pallas_call x1, Pallas kernels, local(): pl.pallas_call(finish_kernel, out_shape=firsts + outs, in_specs=[anywhere...  3.98 us

profile of v6, /device:TPU:0, one launch (start us, length us, event | category | flops | bytes accessed | tf_op | source)
XLA Modules:
  0.0 160.1 jit_solution(17722679033816819546)
XLA Ops:
  0.7 155.3 %layer.1 = (bf16[1,512,512]{2,1,0:T(8,128)(2,1)}, f32[1,512,512]{2,1,0:T(8,128)}, f32[368,512]{1,0:T(8,128)}, f32[8,128]{1,0:T(8,128)}) custom-call(bf16[1,512,512]{2,1,0:T(8,128)(2,1)} %refs_0_.1, s32[1,512]{1,0:T(1,128)} %refs_1_.1, s32[1023]{0:T(1024)} %refs_2_.1, bf16[1,512,512]{2,1,0:T(8,128)(2,1)} %refs_3_.1, bf16[2,2,16]{2,1,0:T(2,128)(2,1)} %refs_4_.1, ...), custom_call_target="tpu_custom_call" | custom-call | tf_op jit(solution)/shard_map/layer/pallas_call | solution.py:1182
  155.9 4.0 %unpack.1 = (bf16[1,512,512]{2,1,0:T(8,128)(2,1)}, f32[1,512,512]{2,1,0:T(8,128)}, f32[2,2,16]{2,1,0:T(2,128)}, f32[2,16,2048]{2,1,0:T(8,128)}, f32[2,64]{1,0:T(...) custom-call(bf16[1,512,512]{2,1,0:T(8,128)(2,1)} %get-tuple-element., ...), custom_call_target="tpu_custom_call" | custom-call | tf_op jit(solution)/shard_map/unpack/pallas_call | solution.py:1199

commit v7 on v6

--- a/solution.py
+++ b/solution.py
@@ -1083,20 +1083,20 @@
     in1[4]()
     tip[4]()
     early.sent()
-    norm_rows(x0, b.normed_c, b.small, S_FFN)
     feed_back_start(flow, b.low, b.grads, 0)
     feed_back_outer(b.active0, b.low, b.weights, OUT1, still)
     out0[0]()
     out0_end[0]()
     mix[1]()
+    norm_rows(x0, b.normed_c, b.small, S_FFN)
     glu[3]()
-    att[3]()
     feed_back_inner(
         b.normed_c, b.slope0, b.low, raws, b.weights, IN1, b.inner_grads, 0,
         at_points({(1, 0): (in0[0], out0[1]), (2, 0): (out0_end[1],)}),
     )
     in0_end[0]()
     in0[1]()
+    att[3]()
     product_back(b.slope0, None, b.total, b.weights, IN0, 4, still)
     in0_end[1]()
     norm_back(x0, b.total, flow, b.x3, b.small, S_FFN, b.grads)

time: 160 us -> 160 us (level)
  no operation moved by 1% of the time
where the time goes in v7:
time: 160 us
  Pallas kernels  159 us (99%)
    pallas_call x1, Pallas kernels, local(): pl.pallas_call(lambda *refs: whole_kernel(names, *refs), out_shape=firsts...  155 us
    pallas_call x1, Pallas kernels, local(): pl.pallas_call(finish_kernel, out_shape=firsts + outs, in_specs=[anywhere...  3.98 us

profile of v7, /device:TPU:0, one launch (start us, length us, event | category | flops | bytes accessed | tf_op | source)
XLA Modules:
  0.0 159.9 jit_solution(10057887576365257576)
XLA Ops:
  0.7 155.0 %layer.1 = (bf16[1,512,512]{2,1,0:T(8,128)(2,1)}, f32[1,512,512]{2,1,0:T(8,128)}, f32[368,512]{1,0:T(8,128)}, f32[8,128]{1,0:T(8,128)}) custom-call(bf16[1,512,512]{2,1,0:T(8,128)(2,1)} %refs_0_.1, s32[1,512]{1,0:T(1,128)} %refs_1_.1, s32[1023]{0:T(1024)} %refs_2_.1, bf16[1,512,512]{2,1,0:T(8,128)(2,1)} %refs_3_.1, bf16[2,2,16]{2,1,0:T(2,128)(2,1)} %refs_4_.1, ...), custom_call_target="tpu_custom_call" | custom-call | tf_op jit(solution)/shard_map/layer/pallas_call | solution.py:1182
  155.7 4.0 %unpack.1 = (bf16[1,512,512]{2,1,0:T(8,128)(2,1)}, f32[1,512,512]{2,1,0:T(8,128)}, f32[2,2,16]{2,1,0:T(2,128)}, f32[2,16,2048]{2,1,0:T(8,128)}, f32[2,64]{1,0:T(...) custom-call(bf16[1,512,512]{2,1,0:T(8,128)(2,1)} %get-tuple-element., ...), custom_call_target="tpu_custom_call" | custom-call | tf_op jit(solution)/shard_map/unpack/pallas_call | solution.py:1199
